TPU v7x, 128 devices: a whole 4x4x4 slice. The times are simulated.
128 devices in a mesh: dp: 32 (over z, y, core), mp: 4 (over x).
Axes of the slice: x: 4, y: 4, z: 4, core: 2. Of those that a mesh axis runs over, the one named last changes fastest.
Arguments:
- gradients: bfloat16 [32, 4, 28, 512, 512], P('dp', 'mp'), may hold values from -24 to 24
- left_stats: float32 [4, 64, 512, 512], P('mp', 'dp'), may hold values from -1 to 4, as said below
- right_stats: float32 [4, 64, 512, 512], P('mp', 'dp'), may hold values from -1 to 4, as said below
- owner_list: int32 [4, 28], replicated, may hold values from 0 to 31, as said below
- owner_counts: int32 [4, 32], replicated, may hold values from 0 to 2, as said below
- block_offsets: int32 [4, 32], replicated, may hold values from 0 to 28, as said below
Outputs:
- new_left: float32 [4, 64, 512, 512], P('mp', 'dp')
- new_right: float32 [4, 64, 512, 512], P('mp', 'dp')
- update: bfloat16 [4, 28, 512, 512], P(None, None, 'dp')
Inputs may be any that keep to these rules, and one draw needn't show every extreme that they name: Each owner's blocks are consecutive: block_offsets[g, o] is the sum of owner_counts[g, p] over p < o, and owner_list[g, k] = o exactly for the blocks block_offsets[g, o] .. block_offsets[g, o] + owner_counts[g, o] - 1. The counts of a group sum to 28; some owner of every group holds 2. `block_offsets`: consistent with owner_counts as stated there. `owner_list`: consistent with owner_counts as stated there. `left_stats`: symmetric positive definite. `right_stats`: symmetric positive definite.
All inputs are finite; a program needn't handle non-finite values. Where the computation divides by a largest or mean magnitude, that divisor is 1e-20 or more.
Results may differ from a plain program's by a relative error of at most 0.015.
Values may be sent and summed in bfloat16 or wider, within the bound.
No kernel may reach another device: no remote copies, remote signals or barrier semaphores. Data moves between devices by JAX's collectives and lax.ppermute only.
A program may use at most 192 MiB of HBM per device.

v0:
```python
import jax
import jax.numpy as jnp
from jax import lax
from jax.sharding import PartitionSpec as P

ITERS = 3


def batched(first_mat, second_mat):
    return jnp.einsum(
        "sij,sjk->sik",
        first_mat,
        second_mat,
        precision=lax.Precision.HIGHEST,
        preferred_element_type=jnp.float32,
    )


def inverse_root(statistic):
    extent = statistic.shape[-1]
    identity = jnp.eye(extent, dtype=jnp.float32)
    scale = jnp.max(jnp.sum(jnp.abs(statistic), axis=2), axis=1)[:, None, None] + 1e-06
    target = statistic / scale
    iterate = identity
    for sweep in range(ITERS):
        factor = (5.0 * identity - target) * 0.25
        iterate = factor if sweep == 0 else batched(iterate, factor)
        if sweep < ITERS - 1:
            square = batched(factor, factor)
            target = batched(square, batched(square, target))
    return iterate * (1.0 / jnp.sqrt(jnp.sqrt(scale)))


def precondition(root_left, block, root_right):
    return batched(root_left, batched(block, root_right)).astype(jnp.bfloat16)


def per_device(gradients, left_stats, right_stats, owner_list, owner_counts, block_offsets):
    group_index = lax.axis_index("mp")
    owner_index = lax.axis_index("dp")
    owners = lax.axis_size("dp")
    partial_value = gradients[0, 0]
    blocks = partial_value.shape[0]
    extent = partial_value.shape[1]
    slot_count = left_stats.shape[1]
    row_share = extent // owners
    counts_row = lax.dynamic_index_in_dim(owner_counts, group_index, 0, keepdims=False)
    offsets_row = lax.dynamic_index_in_dim(block_offsets, group_index, 0, keepdims=False)
    owners_row = lax.dynamic_index_in_dim(owner_list, group_index, 0, keepdims=False)
    slot_ids = jnp.arange(slot_count, dtype=jnp.int32)
    wanted = jnp.minimum(offsets_row[:, None] + slot_ids[None, :], blocks - 1)
    alive_all = slot_ids[None, :] < counts_row[:, None]
    outgoing = partial_value[wanted] * alive_all[:, :, None, None].astype(jnp.bfloat16)
    received = lax.all_to_all(outgoing, "dp", split_axis=0, concat_axis=0, tiled=True)
    summed = jnp.sum(received, axis=0, dtype=jnp.float32)
    own_count = lax.dynamic_index_in_dim(counts_row, owner_index, 0, keepdims=False)
    alive = (slot_ids < own_count)[:, None, None]
    left = left_stats[0]
    right = right_stats[0]
    gram_left = jnp.einsum(
        "sij,skj->sik",
        summed,
        summed,
        precision=lax.Precision.HIGHEST,
        preferred_element_type=jnp.float32,
    )
    gram_right = jnp.einsum(
        "sji,sjk->sik",
        summed,
        summed,
        precision=lax.Precision.HIGHEST,
        preferred_element_type=jnp.float32,
    )
    fresh_left = jnp.where(alive, 0.9 * left + 0.1 / extent * gram_left, left)
    fresh_right = jnp.where(alive, 0.9 * right + 0.1 / extent * gram_right, right)
    roots = inverse_root(jnp.concatenate([fresh_left, fresh_right], 0))
    updates = precondition(roots[:slot_count], summed, roots[slot_count:])
    pieces = updates.reshape(slot_count, owners, row_share, extent)
    returned = lax.all_to_all(pieces, "dp", split_axis=1, concat_axis=0, tiled=True).reshape(
        owners * slot_count, row_share, extent
    )
    slot_of_block = jnp.arange(blocks, dtype=jnp.int32) - offsets_row[owners_row]
    placed = returned[owners_row * slot_count + slot_of_block]
    update = lax.all_gather(placed[None], "mp", axis=0, tiled=True)
    return (fresh_left[None], fresh_right[None], update)


def solution(mesh):
    placed = (
        P("dp", "mp", None, None, None),
        P("mp", "dp", None, None),
        P("mp", "dp", None, None),
        P(),
        P(),
        P(),
    )
    return jax.shard_map(
        per_device,
        mesh=mesh,
        in_specs=placed,
        out_specs=(P("mp", "dp", None, None), P("mp", "dp", None, None), P(None, None, "dp", None)),
        check_vma=False,
    )
```

profile of v0, /device:TPU:0, one launch (start us, length us, event | category | flops | bytes accessed | tf_op | source)
XLA Modules:
  0.0 682.6 jit_solution(4975015068713911632)
XLA Ops:
  7.2 0.7 fusion.24
  7.9 0.1 compare_select_fusion
  8.0 0.1 reshape.177
  8.1 0.1 fusion.23
  8.1 17.8 %gather_fusion = bf16[64,512,512]{2,1,0:T(8,128)(2,1)} fusion(bf16[28,512,512]{2,1,0:T(8,128)(2,1)} %bitcast.64, s32[1024]{0:T(1024)S(1)} %pad_clamp_fusion.2), kind=kCustom, calls=%fused_computation | custom fusion | bytes 67109120 | tf_op jit(solution)/shard_map/gather | solution.py:53
  25.9 22.9 %broadcast_multiply_fusion = bf16[32,2,512,512]{3,2,1,0:T(8,128)(2,1)} fusion(bf16[32,2,512,512]{3,2,1,0:T(8,128)(2,1)} %bitcast.63, bf16[32,2]{1,0:T(8,128)(2,1)S(1)} %fusion.23), kind=kLoop, calls=%fused_computation.4 | loop fusion | flops 16777216 | bytes 67108992 | tf_op jit(solution)/shard_map/mul | solution.py:53
  48.8 0.0 copy-start.10
  48.8 8.7 %all-to-all-start = ((bf16[32,2,512,512]{3,2,1,0:T(8,128)(2,1)}), bf16[32,2,512,512]{3,2,1,0:T(8,128)(2,1)}, u32[]{:S(2)}, u32[]{:S(2)}) async-start(bf16[32,2,512,512]{3,2,1,0:T(8,128)(2,1)} %broadcast_multiply_fusion), calls=%async_computation | async-start | bytes 67108864 | tf_op jit(solution)/shard_map/all_to_all | solution.py:54
  57.5 0.0 copy-done.10
  57.6 1.8 copy.49
  59.4 2.9 copy.48
  62.2 1.3 dynamic_slice.15
  63.5 0.6 iota_compare_fusion.2
  64.2 0.1 fusion.22
  64.3 432.9 %all-to-all-done = bf16[32,2,512,512]{3,2,1,0:T(8,128)(2,1)} async-done(((bf16[32,2,512,512]{3,2,1,0:T(8,128)(2,1)}), bf16[32,2,512,512]{3,2,1,0:T(8,128)(2,1)}, u32[]{:S(2)}, u32[]{:S(2)}) %all-to-all-start) | async-done | bytes 33554464 | tf_op jit(solution)/shard_map/all_to_all | solution.py:54
  497.2 11.3 %convert_reduce_fusion = f32[2,512,512]{2,1,0:T(8,128)S(1)} fusion(bf16[32,2,512,512]{3,2,1,0:T(8,128)(2,1)} %all-to-all-done), kind=kLoop, calls=%fused_computation.3 | loop fusion | flops 33030144 | bytes 35651584 | tf_op jit(solution)/shard_map/reduce_sum | solution.py:55
  508.5 0.0 copy-start.9
  508.5 5.8 bitcast_select_fusion
  514.3 0.0 copy-done.9
  514.3 0.0 copy-start.1
  514.3 3.8 bitcast_select_fusion.1
  518.1 0.0 copy-done.1
  518.1 0.0 copy-start.5
  518.1 1.4 copy-done.5
  519.5 0.5 abs_reduce_fusion
  520.0 0.1 reduce_max.9
  520.1 0.0 copy-start.2
  520.1 0.0 copy-start.6
  520.1 18.8 %fusion.4 = f32[4,512,512]{2,1,0:T(8,128)S(1)} fusion(f32[512,512]{0,1:T(8,128)S(1)} %fusion.22, f32[2,512,512]{1,2,0:T(8,128)} %copy-done.1, f32[2,512,512]{1,2,0:T(8,128)} %copy-done.5, f32[4]{0:T(128)S(1)} %get-tuple-element.16), kind=kOutput, calls=%fused_computation.13 | convolution fusion | flops 6446645248 | bytes 9437200 | tf_op jit(solution)/shard_map/sij,sjk->sik/dot_general | solution.py:10
  539.0 0.0 copy-done.2
  539.0 0.0 copy-done.6
  539.0 7.4 %fusion.35 = f32[4,512,512]{2,1,0:T(8,128)S(1)} fusion(f32[4,512,512]{2,1,0:T(8,128)S(1)} %fusion.4, f32[2,512,512]{1,2,0:T(8,128)S(1)} %copy-done.2, f32[2,512,512]{1,2,0:T(8,128)S(1)} %copy-done.6, f32[4]{0:T(128)S(1)} %get-tuple-element.16), kind=kOutput, calls=%fused_computation.61 | convolution fusion | flops 6444548096 | bytes 12582928 | tf_op jit(solution)/shard_map/sij,sjk->sik/dot_general | solution.py:10
  546.4 8.4 %fusion.38 = f32[4,512,512]{2,1,0:T(8,128)} fusion(f32[4,512,512]{2,1,0:T(8,128)S(1)} %fusion.4, f32[4,512,512]{2,1,0:T(8,128)S(1)} %fusion.35), kind=kOutput, calls=%fused_computation.62 | convolution fusion | flops 6442450944 | bytes 12582912 | tf_op jit(solution)/shard_map/sij,sjk->sik/dot_general | solution.py:10
  554.8 5.3 copy.54
  560.0 0.0 copy-start.3
  560.0 0.0 copy-start.7
  560.0 0.0 copy-start.8
  560.0 17.9 %fusion.5 = f32[4,512,512]{2,1,0:T(8,128)S(1)} fusion(f32[4,512,512]{1,2,0:T(8,128)} %copy.54, f32[512,512]{0,1:T(8,128)S(1)} %fusion.22), kind=kOutput, calls=%fused_computation.14 | convolution fusion | flops 6444548096 | bytes 9437184 | tf_op jit(solution)/shard_map/sij,sjk->sik/dot_general | solution.py:10
  577.9 0.0 copy-done.3
  578.0 0.0 copy-done.7
  578.0 0.0 copy-done.8
  578.0 0.0 copy-start
  578.0 14.2 %fusion.3 = f32[4,512,512]{2,1,0:T(8,128)S(1)} fusion(f32[4,512,512]{1,2,0:T(8,128)S(1)} %copy-done.8, f32[512,512]{0,1:T(8,128)S(1)} %fusion.22, f32[2,512,512]{1,2,0:T(8,128)S(1)} %copy-done.3, f32[2,512,512]{1,2,0:T(8,128)S(1)} %copy-done.7, f32[4]{0:T(128)S(1)} %get-tuple-element.16), kind=kOutput, calls=%fused_computation.12 | convolution fusion | flops 6448742400 | bytes 13631504 | tf_op jit(solution)/shard_map/sij,sjk->sik/dot_general | solution.py:10
  592.2 0.0 copy-done
  592.2 7.3 %fusion.39 = f32[4,512,512]{2,1,0:T(8,128)S(1)} fusion(f32[4,512,512]{2,1,0:T(8,128)S(1)} %fusion.5, f32[4,512,512]{2,1,0:T(8,128)S(1)} %copy-done), kind=kOutput, calls=%fused_computation.63 | convolution fusion | flops 6442450944 | bytes 12582912 | tf_op jit(solution)/shard_map/sij,sjk->sik/dot_general | solution.py:10
  599.6 7.7 %fusion.40 = f32[4,512,512]{1,2,0:T(8,128)S(1)} fusion(f32[4,512,512]{2,1,0:T(8,128)S(1)} %fusion.5, f32[4,512,512]{2,1,0:T(8,128)S(1)} %fusion.39), kind=kOutput, calls=%fused_computation.64 | convolution fusion | flops 6442450944 | bytes 12582912 | tf_op jit(solution)/shard_map/sij,sjk->sik/dot_general | solution.py:10
  607.3 7.4 %fusion.7 = f32[4,512,512]{2,1,0:T(8,128)S(1)} fusion(f32[4,512,512]{2,1,0:T(8,128)S(1)} %fusion.3, f32[4,512,512]{1,2,0:T(8,128)S(1)} %fusion.40, f32[4]{0:T(128)S(1)} %get-tuple-element.15, f32[512,512]{0,1:T(8,128)S(1)} %fusion.22), kind=kOutput, calls=%fused_computation.16 | convolution fusion | flops 6445596672 | bytes 13631504 | tf_op jit(solution)/shard_map/sij,sjk->sik/dot_general | solution.py:10
  614.7 3.8 fusion.10
  618.6 3.8 convolution_convert_fusion
  622.4 0.0 copy-start.11
  622.4 0.0 copy-start.4
  622.4 1.1 copy.61
  623.5 3.9 all-to-all-start.1
  627.4 0.0 all-gather.3.cloned.1.call-start
  627.4 0.0 copy-done.11
  627.5 0.7 gather_fusion.1
  628.2 16.5 %all-to-all-done.1 = bf16[2,32,16,512]{3,2,0,1:T(8,128)(2,1)S(1)} async-done(((bf16[2,32,16,512]{3,2,0,1:T(8,128)(2,1)}), bf16[2,32,16,512]{3,2,0,1:T(8,128)(2,1)S(1)}, u32[]{:S(2)}, u32[]{:S(2)}) %all-to-all-start.1) | async-done | bytes 1048608 | tf_op jit(solution)/shard_map/all_to_all | solution.py:79
  644.7 1.4 gather_fusion.2
  646.1 0.0 all-gather.3.cloned.1.call-update
  646.1 0.0 copy-done.4
  646.1 1.8 copy.63
  647.9 2.9 copy.62
  650.8 21.7 %all-gather.3.cloned.1.call-done = bf16[112,16,512]{2,1,0:T(8,128)(2,1)} async-done(((bf16[28,16,512]{2,1,0:T(8,128)(2,1)}), bf16[112,16,512]{2,1,0:T(8,128)(2,1)}) %all-gather.3.cloned.1.call-update) | async-done | bytes 1835024 | tf_op jit(solution)/shard_map/all_gather | solution.py:84
  672.5 2.9 copy.75
  (6 shorter events, 0.1 us)
Async XLA Ops:
  48.8 8.7 %copy-start.10 = (f32[1,2,512,512]{3,2,1,0:T(8,128)S(1)}, f32[1,2,512,512]{3,2,1,0:T(8,128)}, u32[]{:S(2)}) copy-start(f32[1,2,512,512]{3,2,1,0:T(8,128)} %param.8) | copy-start | bytes 6291460
  48.8 448.3 %all-to-all-start = ((bf16[32,2,512,512]{3,2,1,0:T(8,128)(2,1)}), bf16[32,2,512,512]{3,2,1,0:T(8,128)(2,1)}, u32[]{:S(2)}, u32[]{:S(2)}) async-start(bf16[32,2,512,512]{3,2,1,0:T(8,128)(2,1)} %broadcast_multiply_fusion), calls=%async_computation | async-start | bytes 67108864 | tf_op jit(solution)/shard_map/all_to_all | solution.py:54
  508.5 5.8 copy-start.9
  514.3 3.8 copy-start.1
  518.1 1.4 copy-start.5
  520.1 18.9 %copy-start.2 = (f32[2,512,512]{1,2,0:T(8,128)S(1)}, f32[2,512,512]{1,2,0:T(8,128)}, u32[]{:S(2)}) copy-start(f32[2,512,512]{1,2,0:T(8,128)} %copy-done.1) | copy-start | bytes 6291460
  520.1 18.9 %copy-start.6 = (f32[2,512,512]{1,2,0:T(8,128)S(1)}, f32[2,512,512]{1,2,0:T(8,128)}, u32[]{:S(2)}) copy-start(f32[2,512,512]{1,2,0:T(8,128)} %copy-done.5) | copy-start | bytes 6291460
  560.0 17.9 %copy-start.3 = (f32[2,512,512]{1,2,0:T(8,128)S(1)}, f32[2,512,512]{1,2,0:T(8,128)}, u32[]{:S(2)}) copy-start(f32[2,512,512]{1,2,0:T(8,128)} %copy-done.1) | copy-start | bytes 6291460
  560.0 17.9 %copy-start.7 = (f32[2,512,512]{1,2,0:T(8,128)S(1)}, f32[2,512,512]{1,2,0:T(8,128)}, u32[]{:S(2)}) copy-start(f32[2,512,512]{1,2,0:T(8,128)} %copy-done.5) | copy-start | bytes 6291460
  560.0 17.9 %copy-start.8 = (f32[4,512,512]{1,2,0:T(8,128)S(1)}, f32[4,512,512]{1,2,0:T(8,128)}, u32[]{:S(2)}) copy-start(f32[4,512,512]{1,2,0:T(8,128)} %copy.54) | copy-start | bytes 12582916
  578.0 14.3 %copy-start = (f32[4,512,512]{2,1,0:T(8,128)S(1)}, f32[4,512,512]{2,1,0:T(8,128)}, u32[]{:S(2)}) copy-start(f32[4,512,512]{2,1,0:T(8,128)} %fusion.38) | copy-start | bytes 12582916
  622.4 5.1 copy-start.11
  622.4 23.7 %copy-start.4 = (f32[2,512,512]{1,2,0:T(8,128)S(1)}, f32[2,512,512]{1,2,0:T(8,128)}, u32[]{:S(2)}) copy-start(f32[2,512,512]{1,2,0:T(8,128)} %copy-done.1) | copy-start | bytes 6291460
  623.5 21.3 %all-to-all-start.1 = ((bf16[2,32,16,512]{3,2,0,1:T(8,128)(2,1)}), bf16[2,32,16,512]{3,2,0,1:T(8,128)(2,1)S(1)}, u32[]{:S(2)}, u32[]{:S(2)}) async-start(bf16[2,32,16,512]{3,2,0,1:T(8,128)(2,1)} %copy.61), calls=%async_computation.1 | async-start | bytes 2097152 | tf_op jit(solution)/shard_map/all_to_all | solution.py:79
  627.4 45.1 %all-gather.3.cloned.1.call-start = ((), (), s32[]{:S(2)}) async-start(), calls=%async_computation.2 | async-start | bytes 2293760 | tf_op jit(solution)/shard_map/all_gather | solution.py:84
Sparse Core Ops, SparseCore 0:
  646.2 26.2 all-gather.2
where the time goes:
time: 692 us; the launch traced here: 683 us
  waiting for transfers between devices  471 us (68%)
  matrix products  106 us (15%)
  local copies, waits for them, and re-layouts  41.9 us (6%)
  other arithmetic  35.8 us (5%)
  between operations  14.8 us (2%)
  starting transfers between devices  12.7 us (2%)
    all_to_all x1, waiting for transfers between devices, per_device(): lax.all_to_all(outgoing, 'dp', split_axis=0, concat_axis=0, tiled=True)  433 us
    dot_general x10, matrix products, batched(): jnp.einsum('sij,sjk->sik', first_mat, second_mat, precision=lax.Precision...  96.8 us
    mul x1, other arithmetic, per_device(): partial_value[wanted] * alive_all[:, :, None, None].astype(jnp.bfloat16)  22.9 us
    all_gather x1, waiting for transfers between devices, per_device(): update = lax.all_gather(placed[None], 'mp', axis=0, tiled=True)  21.7 us
    gather x1, local copies, waits for them, and re-layouts, per_device(): partial_value[wanted] * alive_all[:, :, None, None].astype(jnp.bfloat16)  17.8 us
    all_to_all x1, waiting for transfers between devices, per_device(): lax.all_to_all(pieces, 'dp', split_axis=1, concat_axis=0, tiled=True)  16.5 us
  transfers between devices with their start and end apart: 3, of which 3 were waited for; matrix products, arithmetic and copies ran while one was open for 2% of the time, Pallas kernels for 0%

commit v1 on v0

v1 whole, which is shorter than its diff:
```python
import jax
import jax.numpy as jnp
import numpy as np
from jax import lax
from jax.experimental import pallas as pl
from jax.experimental.pallas import tpu as pltpu
from jax.sharding import PartitionSpec as P

RING = 4
CORES = 2
START = 25.0 / 16.0


def tail_coefficients():
    m1 = np.polynomial.Polynomial([1.25, -0.25])
    m2 = 1.25 - 0.25 * np.polynomial.Polynomial([0.0, 1.0]) * m1**4
    return [float(v) for v in (m1 * m2).coef]


TAIL = tail_coefficients()
EYE_PART = 1.25 * TAIL[0]


def dot(first, second, dims=((1,), (0,))):
    return lax.dot_general(
        first.astype(jnp.bfloat16),
        second.astype(jnp.bfloat16),
        (dims, ((), ())),
        preferred_element_type=jnp.float32,
    )


def roots(statistics):
    both = range(len(statistics))
    scales = [jnp.max(jnp.sum(jnp.abs(a), axis=0, keepdims=True), axis=1, keepdims=True) + 1e-06 for a in statistics]
    z = [statistics[i] * (1.0 / scales[i]) for i in both]
    zb = [z[i].astype(jnp.bfloat16) for i in both]
    square = [dot(zb[i], zb[i]) for i in both]
    e = [(0.0625 * square[i] - 0.625 * z[i]).astype(jnp.bfloat16) for i in both]
    t = [START * z[i] + dot(e[i], zb[i]) for i in both]
    y = [START * t[i] + dot(e[i], t[i]) for i in both]
    yb = [y[i].astype(jnp.bfloat16) for i in both]
    y2 = [dot(yb[i], yb[i]) for i in both]
    y3 = [dot(y2[i], yb[i]) for i in both]
    y3b = [y3[i].astype(jnp.bfloat16) for i in both]
    high = [(TAIL[6] * y3[i] + TAIL[5] * y2[i] + TAIL[4] * y[i]).astype(jnp.bfloat16) for i in both]
    q = [TAIL[1] * y[i] + TAIL[2] * y2[i] + TAIL[3] * y3[i] + dot(high[i], y3b[i]) for i in both]
    f = [1.25 * q[i] - (0.25 * TAIL[0]) * z[i] - 0.25 * dot(zb[i], q[i]) for i in both]
    return f, [1.0 / jnp.sqrt(jnp.sqrt(s)) for s in scales]


def slot_kernel(count_ref, block_ref, left_ref, right_ref, new_left_ref, new_right_ref, update_ref):
    alive = pl.program_id(0) < count_ref[0]
    extent = left_ref.shape[-1]

    @pl.when(jnp.logical_not(alive))
    def _():
        new_left_ref[...] = left_ref[...]
        new_right_ref[...] = right_ref[...]
        update_ref[...] = jnp.zeros_like(update_ref)

    @pl.when(alive)
    def _():
        block = block_ref[:, 0].reshape(extent, extent)
        fresh_left = 0.9 * left_ref[0] + (0.1 / extent) * dot(block, block, ((1,), (1,)))
        fresh_right = 0.9 * right_ref[0] + (0.1 / extent) * dot(block, block, ((0,), (0,)))
        new_left_ref[0] = fresh_left
        new_right_ref[0] = fresh_right
        (f_left, f_right), (c_left, c_right) = roots([fresh_left, fresh_right])
        half = EYE_PART * block.astype(jnp.float32) + dot(block, f_right)
        result = (EYE_PART * half + dot(f_left, half)) * (c_left * c_right)
        update_ref[:, 0] = result.astype(jnp.bfloat16).reshape(update_ref.shape[0], update_ref.shape[2], extent)


def slot_step(count, received, left, right):
    owners, slots, rows, extent = received.shape
    spread = pl.BlockSpec((owners, 1, rows, extent), lambda s, count: (0, s, 0, 0))
    whole = pl.BlockSpec((1, extent, extent), lambda s, count: (s, 0, 0))
    return pl.pallas_call(
        slot_kernel,
        grid_spec=pltpu.PrefetchScalarGridSpec(
            num_scalar_prefetch=1,
            grid=(slots,),
            in_specs=[spread, whole, whole],
            out_specs=[whole, whole, spread],
        ),
        out_shape=[
            jax.ShapeDtypeStruct(left.shape, jnp.float32),
            jax.ShapeDtypeStruct(right.shape, jnp.float32),
            jax.ShapeDtypeStruct(received.shape, jnp.bfloat16),
        ],
        compiler_params=pltpu.CompilerParams(vmem_limit_bytes=56 * 1024 * 1024),
        cost_estimate=pl.CostEstimate(
            flops=slots * 18 * 2 * extent**3,
            bytes_accessed=4 * left.size * 4 + 2 * received.size * 2,
            transcendentals=0,
        ),
    )(count, received, left, right)


def shifted(axis, steps):
    pairs = []
    for z in range(RING):
        for y in range(RING):
            for core in range(CORES):
                to = [z, y, core]
                to[axis] = (to[axis] + steps) % (CORES if axis == 2 else RING)
                pairs.append(((z * RING + y) * CORES + core, (to[0] * RING + to[1]) * CORES + to[2]))
    return pairs


def send(value, axis, steps):
    return lax.ppermute(value.astype(jnp.bfloat16), "dp", shifted(axis, steps))


def reduce_scatter(gradient, z, y, core):
    blocks, extent = gradient.shape[0], gradient.shape[1]
    rows = extent // (RING * RING * CORES)
    view = gradient.reshape(blocks, RING, RING, CORES, rows, extent)
    part_blocks = blocks // 2
    mid = part_blocks // 2
    f32 = jnp.float32
    where = (z, y)

    def rows_for(part, away, which_core):
        first = 1 - part
        starts = [part * part_blocks, 0, 0, which_core, 0, 0]
        starts[1 + first] = (where[first] + away) % RING
        sizes = [part_blocks, RING, RING, 1, rows, extent]
        sizes[1 + first] = 1
        return lax.dynamic_slice(view, starts, sizes).reshape(part_blocks, RING, rows, extent)

    chip = {}
    for away in (2, 1, 3, 0):
        for part in (0, 1):
            other = send(rows_for(part, away, 1 - core), 2, 1)
            chip[part, away] = rows_for(part, away, core).astype(f32) + other.astype(f32)
    ahead, back = {}, {}
    for part in (0, 1):
        ahead[part] = send(chip[part, 2][:mid], 1 - part, 1)
        back[part] = send(chip[part, 2][mid:], 1 - part, -1)
    ahead_raw, back_raw = {}, {}
    for part in (0, 1):
        ahead_raw[part] = send(chip[part, 1][mid:], 1 - part, 1)
        back_raw[part] = send(chip[part, 3][:mid], 1 - part, -1)
    ahead_sum, back_sum = {}, {}
    for part in (0, 1):
        ahead_sum[part] = send(chip[part, 1][:mid] + ahead[part].astype(f32), 1 - part, 1)
        back_sum[part] = send(chip[part, 3][mid:] + back[part].astype(f32), 1 - part, -1)
    results = []
    for part in (0, 1):
        own = chip[part, 0]
        low = own[:mid] + ahead_sum[part].astype(f32) + back_raw[part].astype(f32)
        top = own[mid:] + ahead_raw[part].astype(f32) + back_sum[part].astype(f32)
        line = jnp.concatenate([low, top], 0)
        second = part

        def piece(away):
            return lax.dynamic_index_in_dim(line, (where[second] + away) % RING, 1, keepdims=False)

        arrived = [send(piece(away), second, away) for away in (1, 3, 2)]
        total = piece(0)
        for value in arrived:
            total = total + value.astype(f32)
        results.append(total.astype(jnp.bfloat16))
    return jnp.concatenate(results, 0)


def gather_groups(mine, group):
    count = lax.axis_size("mp")
    up = [(i, (i + 1) % count) for i in range(count)]
    down = [(i, (i - 1) % count) for i in range(count)]
    mid = mine.shape[0] // 2
    low, top = mine[:mid], mine[mid:]
    below_low = lax.ppermute(low, "mp", up)
    above_top = lax.ppermute(top, "mp", down)
    below_top = lax.ppermute(top, "mp", up)
    above_low = lax.ppermute(low, "mp", down)
    far_low = lax.ppermute(below_low, "mp", up)
    far_top = lax.ppermute(above_top, "mp", down)
    out = jnp.zeros((count,) + mine.shape, mine.dtype)
    for away, part, value in (
        (0, 0, low),
        (0, mid, top),
        (-1, 0, below_low),
        (-1, mid, below_top),
        (1, 0, above_low),
        (1, mid, above_top),
        (2, 0, far_low),
        (2, mid, far_top),
    ):
        out = lax.dynamic_update_slice(out, value[None], ((group + away) % count, part, 0, 0))
    return out


def per_device(gradients, left_stats, right_stats, owner_list, owner_counts, block_offsets):
    group = lax.axis_index("mp")
    owner = lax.axis_index("dp")
    blocks = gradients.shape[2]
    slots = left_stats.shape[1]
    core = owner % CORES
    y = (owner // CORES) % RING
    z = owner // (CORES * RING)
    counts_row = lax.dynamic_index_in_dim(owner_counts, group, 0, keepdims=False)
    offsets_row = lax.dynamic_index_in_dim(block_offsets, group, 0, keepdims=False)
    owners_row = lax.dynamic_index_in_dim(owner_list, group, 0, keepdims=False)
    slot_ids = jnp.arange(slots, dtype=jnp.int32)
    wanted = jnp.minimum(offsets_row[:, None] + slot_ids[None, :], blocks - 1)

    summed = reduce_scatter(gradients[0, 0], z, y, core)
    received = lax.all_to_all(summed[wanted], "dp", split_axis=0, concat_axis=0, tiled=True)
    own_count = lax.dynamic_slice(counts_row, (owner,), (1,))
    new_left, new_right, updates = slot_step(own_count, received, left_stats[0], right_stats[0])
    returned = lax.all_to_all(updates, "dp", split_axis=0, concat_axis=0, tiled=True)
    returned = returned.reshape(-1, *returned.shape[2:])
    slot_of_block = jnp.arange(blocks, dtype=jnp.int32) - offsets_row[owners_row]
    placed = returned[owners_row * slots + slot_of_block]
    return new_left[None], new_right[None], gather_groups(placed, group)


def solution(mesh):
    placed = (
        P("dp", "mp", None, None, None),
        P("mp", "dp", None, None),
        P("mp", "dp", None, None),
        P(),
        P(),
        P(),
    )
    return jax.shard_map(
        per_device,
        mesh=mesh,
        in_specs=placed,
        out_specs=(P("mp", "dp", None, None), P("mp", "dp", None, None), P(None, None, "dp", None)),
        check_vma=False,
    )
```

time: 692 us -> 181 us (0.26); the launches traced: 683 us -> 180 us
  waiting for transfers between devices: 471 us -> 76.8 us
  matrix products: 106 us -> 0 us
  starting transfers between devices: 12.7 us -> 58.2 us
  other arithmetic: 35.8 us -> 9.73 us
  local copies, waits for them, and re-layouts: 41.9 us -> 23.2 us
  between operations: 14.8 us -> 1.28 us
  Pallas kernels: 0 us -> 11 us
    all_to_all x2, waiting for transfers between devices: 449 us -> 32.5 us  [the longest x1 16.5 us: per_device(): lax.all_to_all(updates, 'dp', split_axis=0, concat_axis=0, tiled=True)]
    dot_general x12 -> x0, matrix products: 106 us -> none  [the longest x10 96.8 us: batched(): jnp.einsum('sij,sjk->sik', first_mat, second_mat, precision=lax.Precision...]
    ppermute x0 -> x32, waiting for transfers between devices: none -> 44.4 us  [the longest x26 33.7 us: send(): return lax.ppermute(value.astype(jnp.bfloat16), 'dp', shifted(axis, steps))]
    ppermute x0 -> x32, starting transfers between devices: none -> 43.1 us  [the longest x26 32.6 us: send(): return lax.ppermute(value.astype(jnp.bfloat16), 'dp', shifted(axis, steps))]
    mul x2 -> x0, other arithmetic: 23 us -> none  [the longest x1 22.9 us: per_device(): partial_value[wanted] * alive_all[:, :, None, None].astype(jnp.bfloat16)]
    all_gather x1 -> x0, waiting for transfers between devices: 21.7 us -> none  [per_device(): update = lax.all_gather(placed[None], 'mp', axis=0, tiled=True)]
    gather x2, local copies, waits for them, and re-layouts: 19.1 us -> 2.16 us  [the longest x1 1.58 us: per_device(): summed[wanted]]
    reduce_sum x2 -> x0, other arithmetic: 11.8 us -> none  [the longest x1 11.3 us: per_device(): summed = jnp.sum(received, axis=0, dtype=jnp.float32)]
  transfers between devices with their start and end apart: 3 -> 34, of which waited for: 3 -> 14; matrix products, arithmetic and copies ran while one was open for 2% -> 13% of each run, Pallas kernels for 0% -> 0%
where the time goes in v1:
time: 181 us; the launch traced here: 180 us
  waiting for transfers between devices  76.8 us (42%)
  starting transfers between devices  58.2 us (32%)
  local copies, waits for them, and re-layouts  23.2 us (13%)
  Pallas kernels  11 us (6%)
  other arithmetic  9.73 us (5%)
    ppermute x26, waiting for transfers between devices, send(): return lax.ppermute(value.astype(jnp.bfloat16), 'dp', shifted(axis, steps))  33.7 us
    ppermute x26, starting transfers between devices, send(): return lax.ppermute(value.astype(jnp.bfloat16), 'dp', shifted(axis, steps))  32.6 us
    all_to_all x1, waiting for transfers between devices, per_device(): lax.all_to_all(updates, 'dp', split_axis=0, concat_axis=0, tiled=True)  16.5 us
    all_to_all x1, waiting for transfers between devices, per_device(): lax.all_to_all(summed[wanted], 'dp', split_axis=0, concat_axis=0, tiled=T...  16 us
    dynamic_slice x5, local copies, waits for them, and re-layouts, rows_for(): lax.dynamic_slice(view, starts, sizes)  11.1 us
    pallas_call x1, Pallas kernels, slot_step(): pl.pallas_call(slot_kernel, grid_spec=pltpu.PrefetchScalarGridSpec(num_sc...  11 us
    all_to_all x1, starting transfers between devices, per_device(): lax.all_to_all(updates, 'dp', split_axis=0, concat_axis=0, tiled=True)  8.84 us
    all_to_all x1, starting transfers between devices, per_device(): lax.all_to_all(summed[wanted], 'dp', split_axis=0, concat_axis=0, tiled=T...  6.28 us
  transfers between devices with their start and end apart: 34, of which 14 were waited for; matrix products, arithmetic and copies ran while one was open for 13% of the time, Pallas kernels for 0%

profile of v1, /device:TPU:0, one launch (start us, length us, event | category | flops | bytes accessed | tf_op | source)
XLA Modules:
  0.0 180.2 jit_solution(5438675601739132897)
XLA Ops:
  0.8 4.1 %dynamic-slice_bitcast_fusion.1 = (bf16[14,4,16,512]{3,2,1,0:T(8,128)(2,1)}, bf16[14,4,16,512]{3,2,1,0:T(8,128)(2,1)}, bf16[14,4,16,512]{3,2,1,0:T(8,128)(2,1)}, bf16[14,4,16,512]{3,2,1,0:T(8,128)(2,1)}) fusion(bf16[28,4,4,2,16,512]{5,4,3,2,1,0:T(8,128)(2,1)} %bitcast.146, s32[]{:T(128)S(6)} %select_n.252, s32[]{:T(128)S(6)} %select_n.237, ...), kind=kLoop, calls=%fused_computation.58 | loop fusion | bytes 7340052 | tf_op jit(solution)/shard_map/reshape | solution.py:131
  4.9 0.5 collective-permute-start.13
  5.4 0.5 collective-permute-start.14
  5.9 5.7 %constant_dynamic-slice_fusion.5 = (bf16[14,4,1,1,16,512]{5,4,3,2,1,0:T(8,128)(2,1)}, bf16[14,4,1,1,16,512]{5,4,3,2,1,0:T(8,128)(2,1)S(1)}, bf16[14,4,1,1,16,512...) fusion(bf16[28,4,4,2,16,512]{5,4,3,2,1,0:T(8,128)(2,1)} %bitcas, ...), kind=kLoop, calls=%fused_computation.108 | loop fusion | bytes 14680088 | tf_op jit(solution)/shard_map/dynamic_slice | solution.py:131
  11.6 1.0 copy.62
  12.7 2.3 %copy.63 = bf16[14,4,1,1,16,512]{5,4,0,1,3,2:T(8,128)(2,1)} copy(bf16[14,4,1,1,16,512]{5,4,3,2,1,0:T(8,128)(2,1)} %get-tuple-element.16) | data formatting | bytes 1835008 | tf_op jit(solution)/shard_map/dynamic_slice | solution.py:131
  15.0 1.0 copy.60
  16.0 1.0 copy.61
  17.2 0.6 collective-permute-start
  17.9 0.4 collective-permute-start.2
  18.3 4.9 %fusion = (bf16[14,4,16,512]{3,2,1,0:T(8,128)(2,1)S(1)}, f32[14,4,16,512]{3,2,1,0:T(8,128)S(1)}, f32[14,4,16,512]{3,2,1,0:T(8,128)S(1)}, f32[14,4,16,512]{3,2,1,0:T(8,128)S(1)}) fusion(bf16[14,4,16,512]{3,2,1,0:T(8,128)(2,1)} %collective-permute-done.15, bf16[28,4,4,2,16,512]{5,4,3,2,1,0:T(8,128)(2,1)} %bitcast.148, s32[]{:T(128)S(6)} %select_n.252, ...), kind=kLoop, calls=%fused_computation.21 | loop fusion | flops 5963776 | bytes 13762580 | tf_op jit(solution)/shard_map/convert.11
  23.3 4.2 %collective-permute-start.21 = (bf16[7,4,16,512]{3,2,1,0:T(8,128)(2,1)S(1)}, bf16[7,4,16,512]{3,2,1,0:T(8,128)(2,1)S(1)}, u32[]{:S(2)}, u32[]{:S(2)}) collective-permute-start(bf16[7,4,16,512]{3,2,1,0:T(8,128)(2,1)S(1)} %get-tuple-element.37), channel_id=1, source_target_pairs={{0,96},{4,100},{8,104},{12,108},{16,112},{20,116},{24,120},{28,124... | collective-permute-start | bytes 1376264 | tf_op jit(solution)/shard_map/ppermute | solution.py:113
  27.6 1.5 convert_add_fusion.6
  29.3 3.3 %collective-permute-start.19 = (bf16[7,4,16,512]{3,2,1,0:T(8,128)(2,1)S(1)}, bf16[7,4,16,512]{3,2,1,0:T(8,128)(2,1)S(1)}, u32[]{:S(2)}, u32[]{:S(2)}) collective-permute-start(bf16[7,4,16,512]{3,2,1,0:T(8,128)(2,1)S(1)} %slice.135), channel_id=1, source_target_pairs={{0,96},{4,100},{8,104},{12,108},{16,112},{20,116},{24,120},{28,124... | collective-permute-start | bytes 1376264 | tf_op jit(solution)/shard_map/ppermute | solution.py:113
  32.6 0.3 convert_add_fusion.4
  33.1 0.7 copy-done.4
  33.7 0.3 fusion.1
  34.2 3.1 %collective-permute-start.8 = (bf16[7,4,16,512]{3,2,0,1:T(8,128)(2,1)S(1)}, bf16[7,4,16,512]{3,2,0,1:T(8,128)(2,1)S(1)}, u32[]{:S(2)}, u32[]{:S(2)}) collective-permute-start(bf16[7,4,16,512]{3,2,0,1:T(8,128)(2,1)S(1)} %get-tuple-element.35), channel_id=1, source_target_pairs={{0,24},{4,28},{8,0},{12,4},{16,8},{20,12},{24,16},{28,20},{32,56},... | collective-permute-start | bytes 1376264 | tf_op jit(solution)/shard_map/ppermute | solution.py:113
  37.2 0.3 convert_add_fusion.7
  37.6 0.8 collective-permute-done.21
  38.3 1.6 collective-permute-start.3
  39.9 0.2 fusion.2
  40.1 10.8 %collective-permute-done.16 = bf16[7,4,16,512]{3,2,1,0:T(8,128)(2,1)S(1)} collective-permute-done((bf16[7,4,16,512]{3,2,1,0:T(8,128)(2,1)S(1)}, bf16[7,4,16,512]{3,2,1,0:T(8,128)(2,1)S(1)}, u32[]{:S(2)}, u32[]{:S(2)}) %collective-permute-start.16) | collective-permute-done | bytes 458784 | tf_op jit(solution)/shard_map/ppermute | solution.py:113
  50.9 0.2 fusion.4
  51.1 2.1 %collective-permute-start.17 = (bf16[7,4,16,512]{3,2,1,0:T(8,128)(2,1)S(1)}, bf16[7,4,16,512]{3,2,1,0:T(8,128)(2,1)S(1)}, u32[]{:S(2)}, u32[]{:S(2)}) collective-permute-start(bf16[7,4,16,512]{3,2,1,0:T(8,128)(2,1)S(1)} %fusion.4), channel_id=1, source_target_pairs={{0,32},{4,36},{8,40},{12,44},{16,48},{20,52},{24,56},{28,60},{32,6... | collective-permute-start | bytes 1376264 | tf_op jit(solution)/shard_map/ppermute | solution.py:113
  53.2 0.2 fusion.6
  53.4 1.6 collective-permute-start.7
  55.0 0.2 fusion.8
  55.2 1.9 %collective-permute-start.6 = (bf16[7,4,16,512]{3,2,0,1:T(8,128)(2,1)S(1)}, bf16[7,4,16,512]{3,2,0,1:T(8,128)(2,1)S(1)}, u32[]{:S(2)}, u32[]{:S(2)}) collective-permute-start(bf16[7,4,16,512]{3,2,0,1:T(8,128)(2,1)S(1)} %slice.137), channel_id=1, source_target_pairs={{0,24},{4,28},{8,0},{12,4},{16,8},{20,12},{24,16},{28,20},{32,56},... | collective-permute-start | bytes 1376264 | tf_op jit(solution)/shard_map/ppermute | solution.py:113
  57.1 1.8 collective-permute-start.9
  58.9 3.3 %collective-permute-done.22 = bf16[7,4,16,512]{3,2,1,0:T(8,128)(2,1)S(1)} collective-permute-done((bf16[7,4,16,512]{3,2,1,0:T(8,128)(2,1)S(1)}, bf16[7,4,16,512]{3,2,1,0:T(8,128)(2,1)S(1)}, u32[]{:S(2)}, u32[]{:S(2)}) %collective-permute-start.22) | collective-permute-done | bytes 458784 | tf_op jit(solution)/shard_map/ppermute | solution.py:113
  62.3 1.6 collective-permute-start.4
  63.8 0.5 fusion.3
  64.4 3.2 %collective-permute-start.25 = (bf16[14,16,512]{2,1,0:T(8,128)(2,1)S(1)}, bf16[14,16,512]{2,1,0:T(8,128)(2,1)S(1)}, u32[]{:S(2)}, u32[]{:S(2)}) collective-permute-start(bf16[14,16,512]{2,1,0:T(8,128)(2,1)S(1)} %get-tuple-element.32), channel_id=1, source_target_pairs={{0,16},{4,20},{8,24},{12,28},{16,0},{20,4},{24,8},{28,12},{32,48},... | collective-permute-start | bytes 688136 | tf_op jit(solution)/shard_map/ppermute | solution.py:113
  67.6 1.2 collective-permute-start.24
  68.8 0.2 collective-permute-done.6
  68.9 1.6 collective-permute-start.23
  70.5 11.5 %collective-permute-done.9 = bf16[7,4,16,512]{3,2,0,1:T(8,128)(2,1)S(1)} collective-permute-done((bf16[7,4,16,512]{3,2,0,1:T(8,128)(2,1)S(1)}, bf16[7,4,16,512]{3,2,0,1:T(8,128)(2,1)S(1)}, u32[]{:S(2)}, u32[]{:S(2)}) %collective-permute-start.9) | collective-permute-done | bytes 458784 | tf_op jit(solution)/shard_map/ppermute | solution.py:113
  82.0 0.5 fusion.7
  82.8 3.2 %collective-permute-start.11 = (bf16[14,16,512]{2,1,0:T(8,128)(2,1)S(1)}, bf16[14,16,512]{2,1,0:T(8,128)(2,1)S(1)}, u32[]{:S(2)}, u32[]{:S(2)}) collective-permute-start(bf16[14,16,512]{2,1,0:T(8,128)(2,1)S(1)} %get-tuple-element.26), channel_id=1, source_target_pairs={{0,96},{4,100},{8,104},{12,108},{16,112},{20,116},{24,120},{28,124... | collective-permute-start | bytes 688136 | tf_op jit(solution)/shard_map/ppermute | solution.py:113
  86.0 0.1 fusion.17
  86.1 4.2 %collective-permute-done.12 = bf16[14,16,512]{2,1,0:T(8,128)(2,1)S(1)} collective-permute-done((bf16[14,16,512]{2,1,0:T(8,128)(2,1)S(1)}, bf16[14,16,512]{2,1,0:T(8,128)(2,1)S(1)}, u32[]{:S(2)}, u32[]{:S(2)}) %collective-permute-start.12) | collective-permute-done | bytes 229408 | tf_op jit(solution)/shard_map/ppermute | solution.py:113
  90.3 1.5 collective-permute-done.11
  91.8 1.4 collective-permute-done.10
  93.4 1.6 gather_fusion
  94.9 6.3 %all-to-all-start = ((bf16[32,2,16,512]{3,2,1,0:T(8,128)(2,1)}), bf16[32,2,16,512]{3,2,1,0:T(8,128)(2,1)S(1)}, u32[]{:S(2)}, u32[]{:S(2)}) async-start(bf16[32,2,16,512]{3,2,1,0:T(8,128)(2,1)} %bitcast.27), calls=%async_computation | async-start | bytes 2097152 | tf_op jit(solution)/shard_map/all_to_all | solution.py:211
  101.2 1.3 dynamic_slice.87
  102.6 16.0 %all-to-all-done.block_ref = bf16[32,2,16,512]{3,2,1,0:T(8,128)(2,1)S(1)} async-done(((bf16[32,2,16,512]{3,2,1,0:T(8,128)(2,1)}), bf16[32,2,16,512]{3,2,1,0:T(8,128)(2,1)S(1)}, u32[]{:S(2)}, u32[]{:S(2)}) %all-to-all-start) | async-done | bytes 1048608 | tf_op jit(solution)/shard_map/all_to_all | solution.py:211
  118.6 1.0 copy-done.6
  119.5 11.0 %shard_map.85 = (f32[2,512,512]{2,1,0:T(8,128)}, f32[2,512,512]{2,1,0:T(8,128)}, bf16[32,2,16,512]{3,2,1,0:T(8,128)(2,1)}) custom-call(s32[1]{0:T(128)} %bitcast.count_ref, bf16[32,2,16,512]{3,2,1,0:T(8,128)(2,1)} %copy-done.6, f32[2,512,512]{2,1,0:T(8,128)} %bitcast.153, f32[2,512,512]{2,1,0:T(8,128)} %bitcast.154), custom_call_target="tpu_custom_call" | custom-call | flops 9663676416 | bytes 10485760 | tf_op jit(solution)/shard_map/pallas_call | solution.py:79
  130.5 8.8 %all-to-all-start.1 = ((bf16[32,2,16,512]{3,2,1,0:T(8,128)(2,1)}), bf16[32,2,16,512]{3,2,1,0:T(8,128)(2,1)S(1)}, u32[]{:S(2)}, u32[]{:S(2)}) async-start(bf16[32,2,16,512]{3,2,1,0:T(8,128)(2,1)} %get-tuple-element.8), calls=%async_computation.1 | async-start | bytes 2097152 | tf_op jit(solution)/shard_map/all_to_all | solution.py:214
  139.5 0.7 gather_fusion.1
  140.2 16.5 %all-to-all-done.1 = bf16[32,2,16,512]{3,2,1,0:T(8,128)(2,1)S(1)} async-done(((bf16[32,2,16,512]{3,2,1,0:T(8,128)(2,1)}), bf16[32,2,16,512]{3,2,1,0:T(8,128)(2,1)S(1)}, u32[]{:S(2)}, u32[]{:S(2)}) %all-to-all-start.1) | async-done | bytes 1048608 | tf_op jit(solution)/shard_map/all_to_all | solution.py:214
  156.7 0.6 gather_fusion.2
  157.3 1.3 collective-permute-start.26
  158.6 2.3 %collective-permute-start.28 = (bf16[14,16,512]{2,1,0:T(8,128)(2,1)S(1)}, bf16[14,16,512]{2,1,0:T(8,128)(2,1)S(1)}, u32[]{:S(2)}, u32[]{:S(2)}) collective-permute-start(bf16[14,16,512]{2,1,0:T(8,128)(2,1)S(1)} %get-tuple-element.40), channel_id=1, source_target_pairs={{0,3},{1,0},{2,1},{3,2},{4,7},{5,4},{6,5},{7,6},{8,11},{9,8},{10,9... | collective-permute-start | bytes 688136 | tf_op jit(solution)/shard_map/ppermute | solution.py:178
  160.9 3.2 %collective-permute-start.29 = (bf16[14,16,512]{2,1,0:T(8,128)(2,1)S(1)}, bf16[14,16,512]{2,1,0:T(8,128)(2,1)S(1)}, u32[]{:S(2)}, u32[]{:S(2)}) collective-permute-start(bf16[14,16,512]{2,1,0:T(8,128)(2,1)S(1)} %get-tuple-element.39), channel_id=1, source_target_pairs={{0,3},{1,0},{2,1},{3,2},{4,7},{5,4},{6,5},{7,6},{8,11},{9,8},{10,9... | collective-permute-start | bytes 688136 | tf_op jit(solution)/shard_map/ppermute | solution.py:176
  164.1 0.2 broadcast_in_dim.40
  164.4 2.8 %collective-permute-done.26 = bf16[14,16,512]{2,1,0:T(8,128)(2,1)S(1)} collective-permute-done((bf16[14,16,512]{2,1,0:T(8,128)(2,1)S(1)}, bf16[14,16,512]{2,1,0:T(8,128)(2,1)S(1)}, u32[]{:S(2)}, u32[]{:S(2)}) %collective-permute-start.26) | collective-permute-done | bytes 229408 | tf_op jit(solution)/shard_map/ppermute | solution.py:175
  167.2 3.7 %collective-permute-done.29 = bf16[14,16,512]{2,1,0:T(8,128)(2,1)S(1)} collective-permute-done((bf16[14,16,512]{2,1,0:T(8,128)(2,1)S(1)}, bf16[14,16,512]{2,1,0:T(8,128)(2,1)S(1)}, u32[]{:S(2)}, u32[]{:S(2)}) %collective-permute-start.29) | collective-permute-done | bytes 229408 | tf_op jit(solution)/shard_map/ppermute | solution.py:176
  171.0 3.7 %collective-permute-start.31 = (bf16[14,16,512]{2,1,0:T(8,128)(2,1)S(1)}, bf16[14,16,512]{2,1,0:T(8,128)(2,1)S(1)}, u32[]{:S(2)}, u32[]{:S(2)}) collective-permute-start(bf16[14,16,512]{2,1,0:T(8,128)(2,1)S(1)} %collective-permute-done.29), channel_id=1, source_target_pairs={{0,3},{1,0},{2,1},{3,2},{4,7},{5,4},{6,5},{7,6},{8,11},{9,8},{10,9... | collective-permute-start | bytes 688136 | tf_op jit(solution)/shard_map/ppermute | solution.py:180
  174.8 1.7 collective-permute-done.30
  176.6 2.4 %collective-permute-done.31 = bf16[14,16,512]{2,1,0:T(8,128)(2,1)S(1)} collective-permute-done((bf16[14,16,512]{2,1,0:T(8,128)(2,1)S(1)}, bf16[14,16,512]{2,1,0:T(8,128)(2,1)S(1)}, u32[]{:S(2)}, u32[]{:S(2)}) %collective-permute-start.31) | collective-permute-done | bytes 229408 | tf_op jit(solution)/shard_map/ppermute | solution.py:180
  179.0 1.2 copy-done.5
  (71 shorter events, 1.6 us)
Async XLA Ops:
  0.6 12.0 %copy-start = (s32[4,32]{1,0:T(4,128)S(1)}, s32[4,32]{1,0:T(4,128)}, u32[]{:S(2)}) copy-start(s32[4,32]{1,0:T(4,128)} %param.11) | copy-start | bytes 1540
  4.9 12.3 %collective-permute-start.15 = (bf16[14,4,16,512]{3,2,1,0:T(8,128)(2,1)}, bf16[14,4,16,512]{3,2,1,0:T(8,128)(2,1)}, u32[]{:S(2)}, u32[]{:S(2)}) collective-permute-start(bf16[14,4,16,512]{3,2,1,0:T(8,128)(2,1)} %get-tuple-element.21), channel_id=1, source_target_pairs={{0,4},{4,0},{8,12},{12,8},{16,20},{20,16},{24,28},{28,24},{32,36},... | collective-permute-start | bytes 2752520 | tf_op jit(solution)/shard_map/ppermute | solution.py:113
  4.9 12.9 %collective-permute-start.13 = (bf16[14,4,16,512]{3,2,1,0:T(8,128)(2,1)}, bf16[14,4,16,512]{3,2,1,0:T(8,128)(2,1)}, u32[]{:S(2)}, u32[]{:S(2)}) collective-permute-start(bf16[14,4,16,512]{3,2,1,0:T(8,128)(2,1)} %get-tuple-element.23), channel_id=1, source_target_pairs={{0,4},{4,0},{8,12},{12,8},{16,20},{20,16},{24,28},{28,24},{32,36},... | collective-permute-start | bytes 2752520 | tf_op jit(solution)/shard_map/ppermute | solution.py:113
  5.4 12.5 %collective-permute-start.18 = (bf16[14,4,16,512]{3,2,1,0:T(8,128)(2,1)}, bf16[14,4,16,512]{3,2,1,0:T(8,128)(2,1)}, u32[]{:S(2)}, u32[]{:S(2)}) collective-permute-start(bf16[14,4,16,512]{3,2,1,0:T(8,128)(2,1)} %get-tuple-element.24), channel_id=1, source_target_pairs={{0,4},{4,0},{8,12},{12,8},{16,20},{20,16},{24,28},{28,24},{32,36},... | collective-permute-start | bytes 2752520 | tf_op jit(solution)/shard_map/ppermute | solution.py:113
  5.4 12.9 %collective-permute-start.14 = (bf16[14,4,16,512]{3,2,1,0:T(8,128)(2,1)}, bf16[14,4,16,512]{3,2,1,0:T(8,128)(2,1)}, u32[]{:S(2)}, u32[]{:S(2)}) collective-permute-start(bf16[14,4,16,512]{3,2,1,0:T(8,128)(2,1)} %get-tuple-element.22), channel_id=1, source_target_pairs={{0,4},{4,0},{8,12},{12,8},{16,20},{20,16},{24,28},{28,24},{32,36},... | collective-permute-start | bytes 2752520 | tf_op jit(solution)/shard_map/ppermute | solution.py:113
  12.6 14.9 %collective-permute-start.1 = (bf16[14,4,16,512]{3,2,0,1:T(8,128)(2,1)}, bf16[14,4,16,512]{3,2,0,1:T(8,128)(2,1)}, u32[]{:S(2)}, u32[]{:S(2)}) collective-permute-start(bf16[14,4,16,512]{3,2,0,1:T(8,128)(2,1)} %bitcast.144), channel_id=1, source_target_pairs={{0,4},{4,0},{8,12},{12,8},{16,20},{20,16},{24,28},{28,24},{32,36},... | collective-permute-start | bytes 2752520 | tf_op jit(solution)/shard_map/ppermute | solution.py:113
  12.6 2.4 %copy-start.3 = (bf16[14,4,1,1,16,512]{5,4,3,2,1,0:T(8,128)(2,1)S(1)}, bf16[14,4,1,1,16,512]{5,4,3,2,1,0:T(8,128)(2,1)}, u32[]{:S(2)}) copy-start(bf16[14,4,1,1,16,512]{5,4,3,2,1,0:T(8,128)(2,1)} %get-tuple-element.13) | copy-start | bytes 2752516
  12.7 3.3 %copy-start.2 = (bf16[14,4,1,1,16,512]{5,4,3,2,1,0:T(8,128)(2,1)S(1)}, bf16[14,4,1,1,16,512]{5,4,3,2,1,0:T(8,128)(2,1)}, u32[]{:S(2)}) copy-start(bf16[14,4,1,1,16,512]{5,4,3,2,1,0:T(8,128)(2,1)} %get-tuple-element.14) | copy-start | bytes 2752516
  17.2 17.0 %collective-permute-start = (bf16[14,4,16,512]{3,2,0,1:T(8,128)(2,1)}, bf16[14,4,16,512]{3,2,0,1:T(8,128)(2,1)S(1)}, u32[]{:S(2)}, u32[]{:S(2)}) collective-permute-start(bf16[14,4,16,512]{3,2,0,1:T(8,128)(2,1)} %bitcast.150), channel_id=1, source_target_pairs={{0,4},{4,0},{8,12},{12,8},{16,20},{20,16},{24,28},{28,24},{32,36},... | collective-permute-start | bytes 2752520 | tf_op jit(solution)/shard_map/ppermute | solution.py:113
  17.8 11.5 %collective-permute-start.5 = (bf16[14,4,16,512]{3,2,0,1:T(8,128)(2,1)}, bf16[14,4,16,512]{3,2,0,1:T(8,128)(2,1)S(1)}, u32[]{:S(2)}, u32[]{:S(2)}) collective-permute-start(bf16[14,4,16,512]{3,2,0,1:T(8,128)(2,1)} %bitcast.152), channel_id=1, source_target_pairs={{0,4},{4,0},{8,12},{12,8},{16,20},{20,16},{24,28},{28,24},{32,36},... | collective-permute-start | bytes 2752520 | tf_op jit(solution)/shard_map/ppermute | solution.py:113
  17.9 15.1 %collective-permute-start.2 = (bf16[14,4,16,512]{3,2,0,1:T(8,128)(2,1)}, bf16[14,4,16,512]{3,2,0,1:T(8,128)(2,1)S(1)}, u32[]{:S(2)}, u32[]{:S(2)}) collective-permute-start(bf16[14,4,16,512]{3,2,0,1:T(8,128)(2,1)} %bitcast.151), channel_id=1, source_target_pairs={{0,4},{4,0},{8,12},{12,8},{16,20},{20,16},{24,28},{28,24},{32,36},... | collective-permute-start | bytes 2752520 | tf_op jit(solution)/shard_map/ppermute | solution.py:113
  23.3 15.1 %collective-permute-start.21 = (bf16[7,4,16,512]{3,2,1,0:T(8,128)(2,1)S(1)}, bf16[7,4,16,512]{3,2,1,0:T(8,128)(2,1)S(1)}, u32[]{:S(2)}, u32[]{:S(2)}) collective-permute-start(bf16[7,4,16,512]{3,2,1,0:T(8,128)(2,1)S(1)} %get-tuple-element.37), channel_id=1, source_target_pairs={{0,96},{4,100},{8,104},{12,108},{16,112},{20,116},{24,120},{28,124... | collective-permute-start | bytes 1376264 | tf_op jit(solution)/shard_map/ppermute | solution.py:113
  27.5 27.7 %collective-permute-start.20 = (bf16[7,4,16,512]{3,2,1,0:T(8,128)(2,1)S(1)}, bf16[7,4,16,512]{3,2,1,0:T(8,128)(2,1)S(1)}, u32[]{:S(2)}, u32[]{:S(2)}) collective-permute-start(bf16[7,4,16,512]{3,2,1,0:T(8,128)(2,1)S(1)} %slice.134), channel_id=1, source_target_pairs={{0,32},{4,36},{8,40},{12,44},{16,48},{20,52},{24,56},{28,60},{32,6... | collective-permute-start | bytes 1376264 | tf_op jit(solution)/shard_map/ppermute | solution.py:113
  29.3 27.9 %collective-permute-start.19 = (bf16[7,4,16,512]{3,2,1,0:T(8,128)(2,1)S(1)}, bf16[7,4,16,512]{3,2,1,0:T(8,128)(2,1)S(1)}, u32[]{:S(2)}, u32[]{:S(2)}) collective-permute-start(bf16[7,4,16,512]{3,2,1,0:T(8,128)(2,1)S(1)} %slice.135), channel_id=1, source_target_pairs={{0,96},{4,100},{8,104},{12,108},{16,112},{20,116},{24,120},{28,124... | collective-permute-start | bytes 1376264 | tf_op jit(solution)/shard_map/ppermute | solution.py:113
  32.5 1.2 copy-start.4
  33.0 17.9 %collective-permute-start.16 = (bf16[7,4,16,512]{3,2,1,0:T(8,128)(2,1)S(1)}, bf16[7,4,16,512]{3,2,1,0:T(8,128)(2,1)S(1)}, u32[]{:S(2)}, u32[]{:S(2)}) collective-permute-start(bf16[7,4,16,512]{3,2,1,0:T(8,128)(2,1)S(1)} %get-tuple-element.38), channel_id=1, source_target_pairs={{0,32},{4,36},{8,40},{12,44},{16,48},{20,52},{24,56},{28,60},{32,6... | collective-permute-start | bytes 1376264 | tf_op jit(solution)/shard_map/ppermute | solution.py:113
  34.2 16.9 %collective-permute-start.8 = (bf16[7,4,16,512]{3,2,0,1:T(8,128)(2,1)S(1)}, bf16[7,4,16,512]{3,2,0,1:T(8,128)(2,1)S(1)}, u32[]{:S(2)}, u32[]{:S(2)}) collective-permute-start(bf16[7,4,16,512]{3,2,0,1:T(8,128)(2,1)S(1)} %get-tuple-element.35), channel_id=1, source_target_pairs={{0,24},{4,28},{8,0},{12,4},{16,8},{20,12},{24,16},{28,20},{32,56},... | collective-permute-start | bytes 1376264 | tf_op jit(solution)/shard_map/ppermute | solution.py:113
  38.3 15.0 %collective-permute-start.3 = (bf16[7,4,16,512]{3,2,0,1:T(8,128)(2,1)S(1)}, bf16[7,4,16,512]{3,2,0,1:T(8,128)(2,1)S(1)}, u32[]{:S(2)}, u32[]{:S(2)}) collective-permute-start(bf16[7,4,16,512]{3,2,0,1:T(8,128)(2,1)S(1)} %get-tuple-element.36), channel_id=1, source_target_pairs={{0,8},{4,12},{8,16},{12,20},{16,24},{20,28},{24,0},{28,4},{32,40},... | collective-permute-start | bytes 1376264 | tf_op jit(solution)/shard_map/ppermute | solution.py:113
  50.9 11.4 %collective-permute-start.22 = (bf16[7,4,16,512]{3,2,1,0:T(8,128)(2,1)S(1)}, bf16[7,4,16,512]{3,2,1,0:T(8,128)(2,1)S(1)}, u32[]{:S(2)}, u32[]{:S(2)}) collective-permute-start(bf16[7,4,16,512]{3,2,1,0:T(8,128)(2,1)S(1)} %fusion.2), channel_id=1, source_target_pairs={{0,96},{4,100},{8,104},{12,108},{16,112},{20,116},{24,120},{28,124... | collective-permute-start | bytes 1376264 | tf_op jit(solution)/shard_map/ppermute | solution.py:113
  51.1 12.8 %collective-permute-start.17 = (bf16[7,4,16,512]{3,2,1,0:T(8,128)(2,1)S(1)}, bf16[7,4,16,512]{3,2,1,0:T(8,128)(2,1)S(1)}, u32[]{:S(2)}, u32[]{:S(2)}) collective-permute-start(bf16[7,4,16,512]{3,2,1,0:T(8,128)(2,1)S(1)} %fusion.4), channel_id=1, source_target_pairs={{0,32},{4,36},{8,40},{12,44},{16,48},{20,52},{24,56},{28,60},{32,6... | collective-permute-start | bytes 1376264 | tf_op jit(solution)/shard_map/ppermute | solution.py:113
  53.4 14.2 %collective-permute-start.7 = (bf16[7,4,16,512]{3,2,0,1:T(8,128)(2,1)S(1)}, bf16[7,4,16,512]{3,2,0,1:T(8,128)(2,1)S(1)}, u32[]{:S(2)}, u32[]{:S(2)}) collective-permute-start(bf16[7,4,16,512]{3,2,0,1:T(8,128)(2,1)S(1)} %slice.136), channel_id=1, source_target_pairs={{0,8},{4,12},{8,16},{12,20},{16,24},{20,28},{24,0},{28,4},{32,40},... | collective-permute-start | bytes 1376264 | tf_op jit(solution)/shard_map/ppermute | solution.py:113
  55.2 13.7 %collective-permute-start.6 = (bf16[7,4,16,512]{3,2,0,1:T(8,128)(2,1)S(1)}, bf16[7,4,16,512]{3,2,0,1:T(8,128)(2,1)S(1)}, u32[]{:S(2)}, u32[]{:S(2)}) collective-permute-start(bf16[7,4,16,512]{3,2,0,1:T(8,128)(2,1)S(1)} %slice.137), channel_id=1, source_target_pairs={{0,24},{4,28},{8,0},{12,4},{16,8},{20,12},{24,16},{28,20},{32,56},... | collective-permute-start | bytes 1376264 | tf_op jit(solution)/shard_map/ppermute | solution.py:113
  57.1 24.9 %collective-permute-start.9 = (bf16[7,4,16,512]{3,2,0,1:T(8,128)(2,1)S(1)}, bf16[7,4,16,512]{3,2,0,1:T(8,128)(2,1)S(1)}, u32[]{:S(2)}, u32[]{:S(2)}) collective-permute-start(bf16[7,4,16,512]{3,2,0,1:T(8,128)(2,1)S(1)} %fusion.6), channel_id=1, source_target_pairs={{0,24},{4,28},{8,0},{12,4},{16,8},{20,12},{24,16},{28,20},{32,56},... | collective-permute-start | bytes 1376264 | tf_op jit(solution)/shard_map/ppermute | solution.py:113
  62.3 19.7 %collective-permute-start.4 = (bf16[7,4,16,512]{3,2,0,1:T(8,128)(2,1)S(1)}, bf16[7,4,16,512]{3,2,0,1:T(8,128)(2,1)S(1)}, u32[]{:S(2)}, u32[]{:S(2)}) collective-permute-start(bf16[7,4,16,512]{3,2,0,1:T(8,128)(2,1)S(1)} %fusion.8), channel_id=1, source_target_pairs={{0,8},{4,12},{8,16},{12,20},{16,24},{20,28},{24,0},{28,4},{32,40},... | collective-permute-start | bytes 1376264 | tf_op jit(solution)/shard_map/ppermute | solution.py:113
  64.4 21.5 %collective-permute-start.25 = (bf16[14,16,512]{2,1,0:T(8,128)(2,1)S(1)}, bf16[14,16,512]{2,1,0:T(8,128)(2,1)S(1)}, u32[]{:S(2)}, u32[]{:S(2)}) collective-permute-start(bf16[14,16,512]{2,1,0:T(8,128)(2,1)S(1)} %get-tuple-element.32), channel_id=1, source_target_pairs={{0,16},{4,20},{8,24},{12,28},{16,0},{20,4},{24,8},{28,12},{32,48},... | collective-permute-start | bytes 688136 | tf_op jit(solution)/shard_map/ppermute | solution.py:113
  67.6 18.4 %collective-permute-start.24 = (bf16[14,16,512]{2,1,0:T(8,128)(2,1)S(1)}, bf16[14,16,512]{2,1,0:T(8,128)(2,1)S(1)}, u32[]{:S(2)}, u32[]{:S(2)}) collective-permute-start(bf16[14,16,512]{2,1,0:T(8,128)(2,1)S(1)} %get-tuple-element.31), channel_id=1, source_target_pairs={{0,24},{4,28},{8,0},{12,4},{16,8},{20,12},{24,16},{28,20},{32,56},... | collective-permute-start | bytes 688136 | tf_op jit(solution)/shard_map/ppermute | solution.py:113
  68.9 17.0 %collective-permute-start.23 = (bf16[14,16,512]{2,1,0:T(8,128)(2,1)S(1)}, bf16[14,16,512]{2,1,0:T(8,128)(2,1)S(1)}, u32[]{:S(2)}, u32[]{:S(2)}) collective-permute-start(bf16[14,16,512]{2,1,0:T(8,128)(2,1)S(1)} %get-tuple-element.30), channel_id=1, source_target_pairs={{0,8},{4,12},{8,16},{12,20},{16,24},{20,28},{24,0},{28,4},{32,40},... | collective-permute-start | bytes 688136 | tf_op jit(solution)/shard_map/ppermute | solution.py:113
  82.7 7.6 %collective-permute-start.12 = (bf16[14,16,512]{2,1,0:T(8,128)(2,1)S(1)}, bf16[14,16,512]{2,1,0:T(8,128)(2,1)S(1)}, u32[]{:S(2)}, u32[]{:S(2)}) collective-permute-start(bf16[14,16,512]{2,1,0:T(8,128)(2,1)S(1)} %get-tuple-element.27), channel_id=1, source_target_pairs={{0,64},{4,68},{8,72},{12,76},{16,80},{20,84},{24,88},{28,92},{32,9... | collective-permute-start | bytes 688136 | tf_op jit(solution)/shard_map/ppermute | solution.py:113
  82.8 9.0 %collective-permute-start.11 = (bf16[14,16,512]{2,1,0:T(8,128)(2,1)S(1)}, bf16[14,16,512]{2,1,0:T(8,128)(2,1)S(1)}, u32[]{:S(2)}, u32[]{:S(2)}) collective-permute-start(bf16[14,16,512]{2,1,0:T(8,128)(2,1)S(1)} %get-tuple-element.26), channel_id=1, source_target_pairs={{0,96},{4,100},{8,104},{12,108},{16,112},{20,116},{24,120},{28,124... | collective-permute-start | bytes 688136 | tf_op jit(solution)/shard_map/ppermute | solution.py:113
  85.9 7.2 %collective-permute-start.10 = (bf16[14,16,512]{2,1,0:T(8,128)(2,1)S(1)}, bf16[14,16,512]{2,1,0:T(8,128)(2,1)S(1)}, u32[]{:S(2)}, u32[]{:S(2)}) collective-permute-start(bf16[14,16,512]{2,1,0:T(8,128)(2,1)S(1)} %get-tuple-element.25), channel_id=1, source_target_pairs={{0,32},{4,36},{8,40},{12,44},{16,48},{20,52},{24,56},{28,60},{32,6... | collective-permute-start | bytes 688136 | tf_op jit(solution)/shard_map/ppermute | solution.py:113
  94.9 23.6 %all-to-all-start = ((bf16[32,2,16,512]{3,2,1,0:T(8,128)(2,1)}), bf16[32,2,16,512]{3,2,1,0:T(8,128)(2,1)S(1)}, u32[]{:S(2)}, u32[]{:S(2)}) async-start(bf16[32,2,16,512]{3,2,1,0:T(8,128)(2,1)} %bitcast.27), calls=%async_computation | async-start | bytes 2097152 | tf_op jit(solution)/shard_map/all_to_all | solution.py:211
  118.6 1.0 copy-start.6
  130.5 8.9 %copy-start.7 = (s32[4,28]{1,0:T(4,128)S(1)}, s32[4,28]{1,0:T(4,128)}, u32[]{:S(2)}) copy-start(s32[4,28]{1,0:T(4,128)} %param.9) | copy-start | bytes 1348
  130.5 26.2 %all-to-all-start.1 = ((bf16[32,2,16,512]{3,2,1,0:T(8,128)(2,1)}), bf16[32,2,16,512]{3,2,1,0:T(8,128)(2,1)S(1)}, u32[]{:S(2)}, u32[]{:S(2)}) async-start(bf16[32,2,16,512]{3,2,1,0:T(8,128)(2,1)} %get-tuple-element.8), calls=%async_computation.1 | async-start | bytes 2097152 | tf_op jit(solution)/shard_map/all_to_all | solution.py:214
  157.3 9.9 %collective-permute-start.26 = (bf16[14,16,512]{2,1,0:T(8,128)(2,1)S(1)}, bf16[14,16,512]{2,1,0:T(8,128)(2,1)S(1)}, u32[]{:S(2)}, u32[]{:S(2)}) collective-permute-start(bf16[14,16,512]{2,1,0:T(8,128)(2,1)S(1)} %get-tuple-element.40), channel_id=1, source_target_pairs={{0,1},{1,2},{2,3},{3,0},{4,5},{5,6},{6,7},{7,4},{8,9},{9,10},{10,1... | collective-permute-start | bytes 688136 | tf_op jit(solution)/shard_map/ppermute | solution.py:175
  158.6 16.1 %collective-permute-start.28 = (bf16[14,16,512]{2,1,0:T(8,128)(2,1)S(1)}, bf16[14,16,512]{2,1,0:T(8,128)(2,1)S(1)}, u32[]{:S(2)}, u32[]{:S(2)}) collective-permute-start(bf16[14,16,512]{2,1,0:T(8,128)(2,1)S(1)} %get-tuple-element.40), channel_id=1, source_target_pairs={{0,3},{1,0},{2,1},{3,2},{4,7},{5,4},{6,5},{7,6},{8,11},{9,8},{10,9... | collective-permute-start | bytes 688136 | tf_op jit(solution)/shard_map/ppermute | solution.py:178
  160.9 13.8 %collective-permute-start.27 = (bf16[14,16,512]{2,1,0:T(8,128)(2,1)S(1)}, bf16[14,16,512]{2,1,0:T(8,128)(2,1)S(1)}, u32[]{:S(2)}, u32[]{:S(2)}) collective-permute-start(bf16[14,16,512]{2,1,0:T(8,128)(2,1)S(1)} %get-tuple-element.39), channel_id=1, source_target_pairs={{0,1},{1,2},{2,3},{3,0},{4,5},{5,6},{6,7},{7,4},{8,9},{9,10},{10,1... | collective-permute-start | bytes 688136 | tf_op jit(solution)/shard_map/ppermute | solution.py:177
  160.9 10.1 %collective-permute-start.29 = (bf16[14,16,512]{2,1,0:T(8,128)(2,1)S(1)}, bf16[14,16,512]{2,1,0:T(8,128)(2,1)S(1)}, u32[]{:S(2)}, u32[]{:S(2)}) collective-permute-start(bf16[14,16,512]{2,1,0:T(8,128)(2,1)S(1)} %get-tuple-element.39), channel_id=1, source_target_pairs={{0,3},{1,0},{2,1},{3,2},{4,7},{5,4},{6,5},{7,6},{8,11},{9,8},{10,9... | collective-permute-start | bytes 688136 | tf_op jit(solution)/shard_map/ppermute | solution.py:176
  164.1 16.1 %copy-start.1 = (s32[4,32]{1,0:T(4,128)S(1)}, s32[4,32]{1,0:T(4,128)}, u32[]{:S(2)}) copy-start(s32[4,32]{1,0:T(4,128)} %param.11) | copy-start | bytes 1540
  167.2 9.3 %collective-permute-start.30 = (bf16[14,16,512]{2,1,0:T(8,128)(2,1)S(1)}, bf16[14,16,512]{2,1,0:T(8,128)(2,1)S(1)}, u32[]{:S(2)}, u32[]{:S(2)}) collective-permute-start(bf16[14,16,512]{2,1,0:T(8,128)(2,1)S(1)} %collective-permute-done.26), channel_id=1, source_target_pairs={{0,1},{1,2},{2,3},{3,0},{4,5},{5,6},{6,7},{7,4},{8,9},{9,10},{10,1... | collective-permute-start | bytes 688136 | tf_op jit(solution)/shard_map/ppermute | solution.py:179
  171.0 8.0 %collective-permute-start.31 = (bf16[14,16,512]{2,1,0:T(8,128)(2,1)S(1)}, bf16[14,16,512]{2,1,0:T(8,128)(2,1)S(1)}, u32[]{:S(2)}, u32[]{:S(2)}) collective-permute-start(bf16[14,16,512]{2,1,0:T(8,128)(2,1)S(1)} %collective-permute-done.29), channel_id=1, source_target_pairs={{0,3},{1,0},{2,1},{3,2},{4,7},{5,4},{6,5},{7,6},{8,11},{9,8},{10,9... | collective-permute-start | bytes 688136 | tf_op jit(solution)/shard_map/ppermute | solution.py:180
  179.0 1.2 copy-start.5

commit v2 on v1

--- a/solution.py
+++ b/solution.py
@@ -1,3 +1,5 @@
+import functools
+
 import jax
 import jax.numpy as jnp
 import numpy as np
@@ -9,6 +11,8 @@
 RING = 4
 CORES = 2
 START = 25.0 / 16.0
+VMEM = 47 * 1024 * 1024
+SETS = (10, 4)
 
 
 def tail_coefficients():
@@ -89,7 +93,7 @@
             jax.ShapeDtypeStruct(right.shape, jnp.float32),
             jax.ShapeDtypeStruct(received.shape, jnp.bfloat16),
         ],
-        compiler_params=pltpu.CompilerParams(vmem_limit_bytes=56 * 1024 * 1024),
+        compiler_params=pltpu.CompilerParams(vmem_limit_bytes=VMEM),
         cost_estimate=pl.CostEstimate(
             flops=slots * 18 * 2 * extent**3,
             bytes_accessed=4 * left.size * 4 + 2 * received.size * 2,
@@ -98,98 +102,282 @@
     )(count, received, left, right)
 
 
-def shifted(axis, steps):
+def flat(z, y, core):
+    return (z * RING + y) * CORES + core
+
+
+def places():
+    return [(z, y, core) for z in range(RING) for y in range(RING) for core in range(CORES)]
+
+
+def partner(place, core, step):
+    flipped = place + 1 - 2 * (place % 2)
+    mirrored = RING - 1 - place
+    late = core + step - 2 * core * step
+    return flipped + late * (mirrored - flipped)
+
+
+def chunk(place, core, which):
+    return {
+        0: place,
+        1: partner(place, core, 0),
+        2: partner(place, core, 1),
+        3: (place + RING // 2) % RING,
+    }[which]
+
+
+def exchange(value, axis, step):
     pairs = []
-    for z in range(RING):
-        for y in range(RING):
-            for core in range(CORES):
-                to = [z, y, core]
-                to[axis] = (to[axis] + steps) % (CORES if axis == 2 else RING)
-                pairs.append(((z * RING + y) * CORES + core, (to[0] * RING + to[1]) * CORES + to[2]))
-    return pairs
-
-
-def send(value, axis, steps):
-    return lax.ppermute(value.astype(jnp.bfloat16), "dp", shifted(axis, steps))
-
-
-def reduce_scatter(gradient, z, y, core):
+    for z, y, core in places():
+        to = (partner(z, core, step), y, core) if axis == 0 else (z, partner(y, core, step), core)
+        pairs.append((flat(z, y, core), flat(*to)))
+    return lax.ppermute(value, "dp", pairs)
+
+
+def swap(value):
+    return lax.ppermute(value, "dp", [(flat(z, y, core), flat(z, y, 1 - core)) for z, y, core in places()])
+
+
+def cut_specs(shape, which, half, other=False):
+    _, _, _, _, rows, extent = shape
+    size = SETS[half]
+    start = 2 * sum(SETS[:half]) // size
+
+    def whose(pos):
+        return 1 - pos[2] if other else pos[2]
+
+    def first(i, pos):
+        return (start, 0, chunk(pos[1], whose(pos), which), whose(pos), 0, 0)
+
+    def second(i, pos):
+        return (start + 1, chunk(pos[0], whose(pos), which), 0, whose(pos), 0, 0)
+
+    return [
+        pl.BlockSpec((size, RING, 1, 1, rows, extent), first),
+        pl.BlockSpec((size, 1, RING, 1, rows, extent), second),
+    ]
+
+
+def local_call(body, pos, in_specs, args, out_specs, out_shape, scratch=()):
+    moved = sum(4 * v.size for v in out_shape)
+    return pl.pallas_call(
+        body,
+        grid_spec=pltpu.PrefetchScalarGridSpec(
+            num_scalar_prefetch=1,
+            grid=(1,),
+            in_specs=in_specs,
+            out_specs=out_specs,
+            scratch_shapes=list(scratch),
+        ),
+        out_shape=out_shape,
+        compiler_params=pltpu.CompilerParams(vmem_limit_bytes=VMEM),
+        cost_estimate=pl.CostEstimate(flops=moved, bytes_accessed=2 * moved, transcendentals=0),
+    )(pos, *args)
+
+
+def cut_kernel(count, pos, *refs):
+    ins, outs = refs[: 2 * count], refs[2 * count :]
+    for k in range(count):
+        for part in (0, 1):
+            outs[part][k] = ins[2 * k + part][...].reshape(outs[part].shape[1:])
+
+
+def cut(view, pos, which, half):
+    rows, extent = view.shape[-2:]
+    shape = (len(which), SETS[half], RING, rows, extent)
+    specs = [spec for w in which for spec in cut_specs(view.shape, w, half, other=True)]
+    return local_call(
+        functools.partial(cut_kernel, len(which)),
+        pos,
+        specs,
+        [view] * len(specs),
+        [pl.BlockSpec(shape, lambda i, pos: (0, 0, 0, 0, 0))] * 2,
+        [jax.ShapeDtypeStruct(shape, jnp.bfloat16)] * 2,
+    )
+
+
+def add_up(own_ref, part, others):
+    value = (own_ref[:, :, 0, 0] if part == 0 else own_ref[:, 0, :, 0]).astype(jnp.float32)
+    for other in others:
+        value = value + other.astype(jnp.float32)
+    return value
+
+
+def first_kernel(pos, *refs):
+    views, others, outs = refs[:4], refs[4:6], refs[6:]
+    for part in (0, 1):
+        for k in (0, 1):
+            outs[part][k] = add_up(views[2 * k + part], part, [others[part][k]]).astype(jnp.bfloat16)
+
+
+def first_sums(view, pos, half, others):
+    whole = pl.BlockSpec(others[0].shape, lambda i, pos: (0, 0, 0, 0, 0))
+    specs = [spec for w in (3, 1) for spec in cut_specs(view.shape, w, half)]
+    shape = [jax.ShapeDtypeStruct(others[0].shape, jnp.bfloat16)] * 2
+    return local_call(first_kernel, pos, specs + [whole] * 2, [view] * 4 + list(others), [whole] * 2, shape)
+
+
+def second_kernel(pos, *refs):
+    views, others, arrived, outs = refs[:2], refs[2:4], refs[4:6], refs[6:]
+    for part in (0, 1):
+        outs[part][...] = add_up(views[part], part, [others[part][0], arrived[part][0]]).astype(jnp.bfloat16)
+
+
+def second_sums(view, pos, half, others, arrived):
+    shape = others[0].shape[1:]
+    lead = pl.BlockSpec((1, *shape), lambda i, pos: (0, 0, 0, 0, 0))
+    whole = pl.BlockSpec(shape, lambda i, pos: (0, 0, 0, 0))
+    specs = cut_specs(view.shape, 2, half) + [lead] * 4
+    out = [jax.ShapeDtypeStruct(shape, jnp.bfloat16)] * 2
+    return local_call(second_kernel, pos, specs, [view] * 2 + list(others) + list(arrived), [whole] * 2, out)
+
+
+def last_kernel(pos, *refs):
+    views, others, direct, joined = refs[:2], refs[2:4], refs[4:6], refs[6:8]
+    filled, outs, scratch = refs[8:-7], refs[-7:-1], refs[-1]
+    size = scratch.shape[0]
+    start = outs[1].shape[0] - size
+    for earlier, out_ref in zip(filled, outs):
+        if len(earlier.shape) == 4:
+            out_ref[:, pl.ds(0, start)] = earlier[...]
+        else:
+            out_ref[pl.ds(0, start)] = earlier[...]
+    for part in (0, 1):
+        ahead_ref, later_ref, own_ref = outs[3 * part : 3 * part + 3]
+        scratch[...] = add_up(views[part], part, [others[part][0], direct[part][0], joined[part][...]])
+        place, core = pos[part], pos[2]
+        here = pl.ds(start, size)
+        for k, which in enumerate((3, 1)):
+            ahead_ref[k, here] = scratch[:, chunk(place, core, which)].astype(jnp.bfloat16)
+        later_ref[here] = scratch[:, chunk(place, core, 2)]
+        own_ref[here] = scratch[:, place]
+
+
+def last_sums(view, pos, half, others, direct, joined, filled):
+    rows, extent = view.shape[-2:]
+    shape = (SETS[half], RING, rows, extent)
+    so_far = sum(SETS[: half + 1])
+    tail = pl.BlockSpec((1, *shape), lambda i, pos: (1, 0, 0, 0, 0))
+    whole = pl.BlockSpec(shape, lambda i, pos: (0, 0, 0, 0))
+
+    def pieces(count):
+        ahead = pl.BlockSpec((2, count, rows, extent), lambda i, pos: (0, 0, 0, 0))
+        piece = pl.BlockSpec((count, rows, extent), lambda i, pos: (0, 0, 0))
+        return [ahead, piece, piece] * 2
+
+    return local_call(
+        last_kernel,
+        pos,
+        cut_specs(view.shape, 0, half) + [tail, tail, tail, tail, whole, whole] + pieces(sum(SETS[:half]))[: len(filled)],
+        [view] * 2 + [*others, *direct, *joined, *filled],
+        pieces(so_far),
+        [
+            jax.ShapeDtypeStruct((2, so_far, rows, extent), jnp.bfloat16),
+            jax.ShapeDtypeStruct((so_far, rows, extent), jnp.float32),
+            jax.ShapeDtypeStruct((so_far, rows, extent), jnp.float32),
+        ]
+        * 2,
+        [pltpu.VMEM(shape, jnp.float32)],
+    )
+
+
+def reduce_scatter(gradient, pos):
     blocks, extent = gradient.shape[0], gradient.shape[1]
     rows = extent // (RING * RING * CORES)
+    parts = (0, 1)
+    halves = range(len(SETS))
     view = gradient.reshape(blocks, RING, RING, CORES, rows, extent)
-    part_blocks = blocks // 2
-    mid = part_blocks // 2
-    f32 = jnp.float32
-    where = (z, y)
-
-    def rows_for(part, away, which_core):
-        first = 1 - part
-        starts = [part * part_blocks, 0, 0, which_core, 0, 0]
-        starts[1 + first] = (where[first] + away) % RING
-        sizes = [part_blocks, RING, RING, 1, rows, extent]
-        sizes[1 + first] = 1
-        return lax.dynamic_slice(view, starts, sizes).reshape(part_blocks, RING, rows, extent)
-
-    chip = {}
-    for away in (2, 1, 3, 0):
-        for part in (0, 1):
-            other = send(rows_for(part, away, 1 - core), 2, 1)
-            chip[part, away] = rows_for(part, away, core).astype(f32) + other.astype(f32)
-    ahead, back = {}, {}
-    for part in (0, 1):
-        ahead[part] = send(chip[part, 2][:mid], 1 - part, 1)
-        back[part] = send(chip[part, 2][mid:], 1 - part, -1)
-    ahead_raw, back_raw = {}, {}
-    for part in (0, 1):
-        ahead_raw[part] = send(chip[part, 1][mid:], 1 - part, 1)
-        back_raw[part] = send(chip[part, 3][:mid], 1 - part, -1)
-    ahead_sum, back_sum = {}, {}
-    for part in (0, 1):
-        ahead_sum[part] = send(chip[part, 1][:mid] + ahead[part].astype(f32), 1 - part, 1)
-        back_sum[part] = send(chip[part, 3][mid:] + back[part].astype(f32), 1 - part, -1)
-    results = []
-    for part in (0, 1):
-        own = chip[part, 0]
-        low = own[:mid] + ahead_sum[part].astype(f32) + back_raw[part].astype(f32)
-        top = own[mid:] + ahead_raw[part].astype(f32) + back_sum[part].astype(f32)
-        line = jnp.concatenate([low, top], 0)
-        second = part
-
-        def piece(away):
-            return lax.dynamic_index_in_dim(line, (where[second] + away) % RING, 1, keepdims=False)
-
-        arrived = [send(piece(away), second, away) for away in (1, 3, 2)]
-        total = piece(0)
-        for value in arrived:
-            total = total + value.astype(f32)
-        results.append(total.astype(jnp.bfloat16))
-    return jnp.concatenate(results, 0)
-
-
-def gather_groups(mine, group):
-    count = lax.axis_size("mp")
-    up = [(i, (i + 1) % count) for i in range(count)]
-    down = [(i, (i - 1) % count) for i in range(count)]
+    left, swapped = view, []
+
+    def send_across(left, which, half):
+        pieces = cut(left, pos, which, half)
+        left, *pieces = lax.optimization_barrier((left, *pieces))
+        return left, [swap(v) for v in pieces]
+
+    for which, half in (((3, 1), 0), ((3, 1), 1), ((2, 0), 0)):
+        left, values = send_across(left, which, half)
+        swapped.append(values)
+    direct = []
+    for half in halves:
+        sums = first_sums(left, pos, half, swapped[half])
+        left, *sums = lax.optimization_barrier((left, *sums))
+        direct.append([exchange(v, 1 - part, 0) for part, v in zip(parts, sums)])
+    left, values = send_across(left, (2, 0), 1)
+    late = [swapped[2], values]
+    joined, terms, pieces = [], [], []
+    for half in halves:
+        sums = second_sums(left, pos, half, late[half], direct[half])
+        joined.append([exchange(v, 1 - part, 1) for part, v in zip(parts, sums)])
+    for half in halves:
+        pieces = last_sums(left, pos, half, late[half], direct[half], joined[half], pieces)
+        left, *pieces = lax.optimization_barrier((left, *pieces))
+    for part in parts:
+        ahead, later, own = pieces[3 * part : 3 * part + 3]
+        arrived = exchange(ahead, part, 0)
+        more = exchange((later + arrived[0].astype(jnp.float32)).astype(jnp.bfloat16), part, 1)
+        terms += [own, arrived, more]
+    return terms
+
+
+def place_kernel(wanted, *refs):
+    *terms, out_ref, summed = refs
+    for part, (own, arrived, more) in enumerate(zip(terms[::3], terms[1::3], terms[2::3])):
+        value = own[...] + arrived[0].astype(jnp.float32) + more[...].astype(jnp.float32)
+        value = value.astype(jnp.bfloat16)
+        for half, size in enumerate(SETS):
+            start = sum(SETS[:half])
+            summed[pl.ds(2 * start + part * size, size)] = value[start : start + size]
+
+    def copy(i, carry):
+        out_ref[i] = summed[wanted[i]]
+        return carry
+
+    lax.fori_loop(0, out_ref.shape[0], copy, 0)
+
+
+def to_slots(terms, wanted):
+    rows, extent = terms[0].shape[1:]
+    shape = (wanted.shape[0], rows, extent)
+    specs = []
+    for own in terms[::3]:
+        piece = pl.BlockSpec(own.shape, lambda i, wanted: (0, 0, 0))
+        lead = pl.BlockSpec((1, *own.shape), lambda i, wanted: (1, 0, 0, 0))
+        specs += [piece, lead, piece]
+    (out,) = local_call(
+        place_kernel,
+        wanted,
+        specs,
+        terms,
+        [pl.BlockSpec(shape, lambda i, wanted: (0, 0, 0))],
+        [jax.ShapeDtypeStruct(shape, jnp.bfloat16)],
+        [pltpu.VMEM((2 * sum(SETS), rows, extent), jnp.bfloat16)],
+    )
+    return out
+
+
+def send_group(value, steps):
+    groups = lax.axis_size("mp")
+    pairs = []
+    for z, y, core in places():
+        for group in range(groups):
+            ahead = -steps if core else steps
+            pairs.append((flat(z, y, core) * groups + group, flat(z, y, core) * groups + (group + ahead) % groups))
+    return lax.ppermute(value, ("dp", "mp"), pairs)
+
+
+def gather_groups(mine, group, core):
+    groups = lax.axis_size("mp")
+    sign = 1 - 2 * core
     mid = mine.shape[0] // 2
-    low, top = mine[:mid], mine[mid:]
-    below_low = lax.ppermute(low, "mp", up)
-    above_top = lax.ppermute(top, "mp", down)
-    below_top = lax.ppermute(top, "mp", up)
-    above_low = lax.ppermute(low, "mp", down)
-    far_low = lax.ppermute(below_low, "mp", up)
-    far_top = lax.ppermute(above_top, "mp", down)
-    out = jnp.zeros((count,) + mine.shape, mine.dtype)
-    for away, part, value in (
-        (0, 0, low),
-        (0, mid, top),
-        (-1, 0, below_low),
-        (-1, mid, below_top),
-        (1, 0, above_low),
-        (1, mid, above_top),
-        (2, 0, far_low),
-        (2, mid, far_top),
-    ):
-        out = lax.dynamic_update_slice(out, value[None], ((group + away) % count, part, 0, 0))
+    behind = [send_group(mine[:mid], 1), send_group(mine[mid:], 1)]
+    before = send_group(mine, -1)
+    opposite = [send_group(v, 1) for v in behind]
+    out = jnp.zeros((groups,) + mine.shape, mine.dtype)
+    for away, values in ((0, [mine]), (-1, behind), (2, opposite), (1, [before])):
+        start = 0
+        for value in values:
+            out = lax.dynamic_update_slice(out, value[None], ((group + sign * away + groups) % groups, start, 0, 0))
+            start += mid
     return out
 
 
@@ -207,15 +395,16 @@
     slot_ids = jnp.arange(slots, dtype=jnp.int32)
     wanted = jnp.minimum(offsets_row[:, None] + slot_ids[None, :], blocks - 1)
 
-    summed = reduce_scatter(gradients[0, 0], z, y, core)
-    received = lax.all_to_all(summed[wanted], "dp", split_axis=0, concat_axis=0, tiled=True)
+    terms = reduce_scatter(gradients[0, 0], jnp.stack([z, y, core]).astype(jnp.int32))
+    outgoing = to_slots(terms, wanted.reshape(-1)).reshape(-1, slots, *terms[0].shape[1:])
+    received = lax.all_to_all(outgoing, "dp", split_axis=0, concat_axis=0, tiled=True)
     own_count = lax.dynamic_slice(counts_row, (owner,), (1,))
     new_left, new_right, updates = slot_step(own_count, received, left_stats[0], right_stats[0])
     returned = lax.all_to_all(updates, "dp", split_axis=0, concat_axis=0, tiled=True)
     returned = returned.reshape(-1, *returned.shape[2:])
     slot_of_block = jnp.arange(blocks, dtype=jnp.int32) - offsets_row[owners_row]
     placed = returned[owners_row * slots + slot_of_block]
-    return new_left[None], new_right[None], gather_groups(placed, group)
+    return new_left[None], new_right[None], gather_groups(placed, group, core)
 
 
 def solution(mesh):

time: 181 us -> 164 us (0.906)
  Pallas kernels: 11 us -> 29 us
  local copies, waits for them, and re-layouts: 23.2 us -> 5.9 us
  other arithmetic: 9.73 us -> 0.3 us
  starting transfers between devices: 58.2 us -> 52.8 us
  waiting for transfers between devices: 76.8 us -> 74.1 us
    pallas_call x0 -> x11, Pallas kernels: none -> 25.8 us  [local_call(): pl.pallas_call(body, grid_spec=pltpu.PrefetchScalarGridSpec(num_scalar_pr...]
    dynamic_slice x5 -> x0, local copies, waits for them, and re-layouts: 11.1 us -> none  [rows_for(): lax.dynamic_slice(view, starts, sizes)]
    ppermute x32 -> x25, starting transfers between devices: 43.1 us -> 33.3 us  [the longest x12 24.4 us: exchange(): return lax.ppermute(value, 'dp', pairs)]
    pallas_call x1, Pallas kernels: 11 us -> 3.18 us  [slot_step(): pl.pallas_call(slot_kernel, grid_spec=pltpu.PrefetchScalarGridSpec(num_sc...]
    all_to_all x1, starting transfers between devices: 8.84 us -> 15.2 us  [per_device(): lax.all_to_all(updates, 'dp', split_axis=0, concat_axis=0, tiled=True)]
    another operation x2 -> x1, other arithmetic: 5.25 us -> 0.08 us  [per_device(): jnp.stack([z, y, core]).astype(jnp.int32)]
    reshape x1 -> x0, local copies, waits for them, and re-layouts: 4.1 us -> none  [rows_for(): lax.dynamic_slice(view, starts, sizes)]
    add x5 -> x0, other arithmetic: 3.16 us -> none  [the longest x3 2.14 us: reduce_scatter(): rows_for(part, away, core).astype(f32) + other.astype(f32)]
  transfers between devices with their start and end apart: 34 -> 27, of which waited for: 14 -> 12; matrix products, arithmetic and copies ran while one was open for 13% -> 2% of each run, Pallas kernels for 0% -> 11%
where the time goes in v2:
time: 164 us; the launch traced here: 163 us
  waiting for transfers between devices  74.1 us (45%)
  starting transfers between devices  52.8 us (32%)
  Pallas kernels  29 us (18%)
  local copies, waits for them, and re-layouts  5.9 us (4%)
    pallas_call x11, Pallas kernels, local_call(): pl.pallas_call(body, grid_spec=pltpu.PrefetchScalarGridSpec(num_scalar_pr...  25.8 us
    ppermute x12, starting transfers between devices, exchange(): return lax.ppermute(value, 'dp', pairs)  24.4 us
    ppermute x12, waiting for transfers between devices, exchange(): return lax.ppermute(value, 'dp', pairs)  23 us
    ppermute x5, waiting for transfers between devices, send_group(): return lax.ppermute(value, ('dp', 'mp'), pairs)  17.1 us
    all_to_all x1, waiting for transfers between devices, per_device(): lax.all_to_all(updates, 'dp', split_axis=0, concat_axis=0, tiled=True)  16.5 us
    all_to_all x1, waiting for transfers between devices, per_device(): lax.all_to_all(outgoing, 'dp', split_axis=0, concat_axis=0, tiled=True)  15.9 us
    all_to_all x1, starting transfers between devices, per_device(): lax.all_to_all(updates, 'dp', split_axis=0, concat_axis=0, tiled=True)  15.2 us
    ppermute x8, starting transfers between devices, swap(): lax.ppermute(value, 'dp', [(flat(z, y, core), flat(z, y, 1 - core)) for z...  5.35 us
  transfers between devices with their start and end apart: 27, of which 12 were waited for; matrix products, arithmetic and copies ran while one was open for 2% of the time, Pallas kernels for 11%

profile of v2, /device:TPU:0, one launch (start us, length us, event | category | flops | bytes accessed | tf_op | source)
XLA Modules:
  0.0 163.0 jit_solution(5069596604123976744)
XLA Ops:
  0.6 0.0 copy-start
  0.7 0.1 pad_add_fusion.pos
  0.8 2.4 %shard_map.85 = (bf16[2,10,4,16,512]{4,3,2,1,0:T(8,128)(2,1)S(1)}, bf16[2,10,4,16,512]{4,3,2,1,0:T(8,128)(2,1)S(1)}) custom-call(s32[3]{0:T(128)S(1)} %pad_add_fusion.pos, bf16[28,4,4,2,16,512]{5,4,3,2,1,0:T(8,128)(2,1)} %bitcast.53, bf16[28,4,4,2,16,512]{5,4,3,2,1,0:T(8,128)(2,1)} %bitcast.54, bf16[28,4,4,2,16,512]{5,4,3,2,1,0:T(8,128)(2,1)} %bitcast.55, ...), custom_call_target="tpu_custom_call" | custom-call | flops 5242880 | bytes 10485760 | tf_op jit(solution)/shard_map/pallas_call | solution.py:163
  3.2 0.1 collective-permute-start
  3.3 0.5 collective-permute-start.1
  3.8 1.8 %shard_map.86 = (bf16[2,4,4,16,512]{4,3,2,1,0:T(8,128)(2,1)S(1)}, bf16[2,4,4,16,512]{4,3,2,1,0:T(8,128)(2,1)S(1)}) custom-call(s32[3]{0:T(128)S(1)} %pad_add_fusion.pos, bf16[28,4,4,2,16,512]{5,4,3,2,1,0:T(8,128)(2,1)} %bitcast.57, bf16[28,4,4,2,16,512]{5,4,3,2,1,0:T(8,128)(2,1)} %bitcast.58, bf16[28,4,4,2,16,512]{5,4,3,2,1,0:T(8,128)(2,1)} %bitcast.59, ...), custom_call_target="tpu_custom_call" | custom-call | flops 2097152 | bytes 4194304 | tf_op jit(solution)/shard_map/pallas_call | solution.py:163
  5.6 0.2 collective-permute-start.2
  5.8 2.4 %shard_map.87 = (bf16[2,10,4,16,512]{4,3,2,1,0:T(8,128)(2,1)S(1)}, bf16[2,10,4,16,512]{4,3,2,1,0:T(8,128)(2,1)S(1)}) custom-call(s32[3]{0:T(128)S(1)} %pad_add_fusion.pos, bf16[28,4,4,2,16,512]{5,4,3,2,1,0:T(8,128)(2,1)} %bitcast.61, bf16[28,4,4,2,16,512]{5,4,3,2,1,0:T(8,128)(2,1)} %bitcast.62, bf16[28,4,4,2,16,512]{5,4,3,2,1,0:T(8,128)(2,1)} %bitcast.63, ...), custom_call_target="tpu_custom_call" | custom-call | flops 5242880 | bytes 10485760 | tf_op jit(solution)/shard_map/pallas_call | solution.py:163
  8.2 0.5 collective-permute-start.4
  8.7 0.1 collective-permute-start.5
  8.8 0.0 collective-permute-done.refs_4_
  8.8 0.0 collective-permute-done.1.refs_5_
  8.8 2.9 %shard_map.88 = (bf16[2,10,4,16,512]{4,3,2,1,0:T(8,128)(2,1)S(1)}, bf16[2,10,4,16,512]{4,3,2,1,0:T(8,128)(2,1)S(1)}) custom-call(s32[3]{0:T(128)S(1)} %pad_add_fusion.pos, bf16[28,4,4,2,16,512]{5,4,3,2,1,0:T(8,128)(2,1)} %bitcast.68, bf16[28,4,4,2,16,512]{5,4,3,2,1,0:T(8,128)(2,1)} %bitcast.66, bf16[28,4,4,2,16,512]{5,4,3,2,1,0:T(8,128)(2,1)} %bitcast.67, ...), custom_call_target="tpu_custom_call" | custom-call | flops 5242880 | bytes 10485760 | tf_op jit(solution)/shard_map/pallas_call | solution.py:163
  11.7 1.7 %collective-permute-start.6 = (bf16[2,10,4,16,512]{4,3,2,1,0:T(8,128)(2,1)S(1)}, bf16[2,10,4,16,512]{4,3,2,1,0:T(8,128)(2,1)S(1)}, u32[]{:S(2)}, u32[]{:S(2)}) collective-permute-start(bf16[2,10,4,16,512]{4,3,2,1,0:T(8,128)(2,1)S(1)} %get-tuple-element.89), channel_id=1, source_target_pairs={{0,8},{4,28},{8,0},{12,20},{16,24},{20,12},{24,16},{28,4},{32,40},... | collective-permute-start | bytes 3932168 | tf_op jit(solution)/shard_map/ppermute | solution.py:134
  13.5 1.9 %collective-permute-start.7 = (bf16[2,10,4,16,512]{4,3,2,1,0:T(8,128)(2,1)S(1)}, bf16[2,10,4,16,512]{4,3,2,1,0:T(8,128)(2,1)S(1)}, u32[]{:S(2)}, u32[]{:S(2)}) collective-permute-start(bf16[2,10,4,16,512]{4,3,2,1,0:T(8,128)(2,1)S(1)} %get-tuple-element.90), channel_id=1, source_target_pairs={{0,32},{4,100},{8,40},{12,108},{16,48},{20,116},{24,56},{28,124},{... | collective-permute-start | bytes 3932168 | tf_op jit(solution)/shard_map/ppermute | solution.py:134
  15.4 3.4 %collective-permute-start.3 = (bf16[2,4,4,16,512]{4,3,2,1,0:T(8,128)(2,1)S(1)}, bf16[2,4,4,16,512]{4,3,2,1,0:T(8,128)(2,1)S(1)}, u32[]{:S(2)}, u32[]{:S(2)}) collective-permute-start(bf16[2,4,4,16,512]{4,3,2,1,0:T(8,128)(2,1)S(1)} %get-tuple-element.80), channel_id=1, source_target_pairs={{0,4},{4,0},{8,12},{12,8},{16,20},{20,16},{24,28},{28,24},{32,36},... | collective-permute-start | bytes 1572872 | tf_op jit(solution)/shard_map/ppermute | solution.py:138
  18.8 1.5 collective-permute-done.3.refs_5_
  20.3 2.0 %shard_map.89 = (bf16[2,4,4,16,512]{4,3,2,1,0:T(8,128)(2,1)S(1)}, bf16[2,4,4,16,512]{4,3,2,1,0:T(8,128)(2,1)S(1)}) custom-call(s32[3]{0:T(128)S(1)} %pad_add_fusion.pos, bf16[28,4,4,2,16,512]{5,4,3,2,1,0:T(8,128)(2,1)} %bitcast.69, bf16[28,4,4,2,16,512]{5,4,3,2,1,0:T(8,128)(2,1)} %bitcast.70, bf16[28,4,4,2,16,512]{5,4,3,2,1,0:T(8,128)(2,1)} %bitcast.71, ...), custom_call_target="tpu_custom_call" | custom-call | flops 2097152 | bytes 4194304 | tf_op jit(solution)/shard_map/pallas_call | solution.py:163
  22.4 1.8 %shard_map.90 = (bf16[2,4,4,16,512]{4,3,2,1,0:T(8,128)(2,1)S(1)}, bf16[2,4,4,16,512]{4,3,2,1,0:T(8,128)(2,1)S(1)}) custom-call(s32[3]{0:T(128)S(1)} %pad_add_fusion.pos, bf16[28,4,4,2,16,512]{5,4,3,2,1,0:T(8,128)(2,1)} %bitcast.73, bf16[28,4,4,2,16,512]{5,4,3,2,1,0:T(8,128)(2,1)} %bitcast.74, bf16[28,4,4,2,16,512]{5,4,3,2,1,0:T(8,128)(2,1)} %bitcast.75, ...), custom_call_target="tpu_custom_call" | custom-call | flops 2097152 | bytes 4194304 | tf_op jit(solution)/shard_map/pallas_call | solution.py:163
  24.2 0.5 collective-permute-start.10
  24.6 0.0 collective-permute-done.4.refs_2_
  24.7 0.1 collective-permute-start.11
  24.8 0.1 collective-permute-start.12
  24.9 4.5 %collective-permute-done.6.refs_4_ = bf16[2,10,4,16,512]{4,3,2,1,0:T(8,128)(2,1)S(1)} collective-permute-done((bf16[2,10,4,16,512]{4,3,2,1,0:T(8,128)(2,1)S(1)}, bf16[2,10,4,16,512]{4,3,2,1,0:T(8,128)(2,1)S(1)}, u32[]{:S(2)}, u32[]{:S(2)}) %collective-permute-start.6) | collective-permute-done | bytes 1310752 | tf_op jit(solution)/shard_map/ppermute | solution.py:134
  29.4 2.0 %collective-permute-start.13 = (bf16[2,4,4,16,512]{4,3,2,1,0:T(8,128)(2,1)S(1)}, bf16[2,4,4,16,512]{4,3,2,1,0:T(8,128)(2,1)S(1)}, u32[]{:S(2)}, u32[]{:S(2)}) collective-permute-start(bf16[2,4,4,16,512]{4,3,2,1,0:T(8,128)(2,1)S(1)} %get-tuple-element.103), channel_id=1, source_target_pairs={{0,32},{4,100},{8,40},{12,108},{16,48},{20,116},{24,56},{28,124},{... | collective-permute-start | bytes 1572872 | tf_op jit(solution)/shard_map/ppermute | solution.py:134
  31.4 2.4 %shard_map.91 = (bf16[10,4,16,512]{3,2,1,0:T(8,128)(2,1)S(1)}, bf16[10,4,16,512]{3,2,1,0:T(8,128)(2,1)S(1)}) custom-call(s32[3]{0:T(128)S(1)} %pad_add_fusion.pos, bf16[28,4,4,2,16,512]{5,4,3,2,1,0:T(8,128)(2,1)} %bitcast.77, bf16[28,4,4,2,16,512]{5,4,3,2,1,0:T(8,128)(2,1)} %bitcast.78, bf16[2,10,4,16,512]{4,3,2,1,0:T(8,128)(2,1)S(1)} %collective-permute-done.4.refs_2_, ...), custom_call_target="tpu_custom_call" | custom-call | flops 2621440 | bytes 5242880 | tf_op jit(solution)/shard_map/pallas_call | solution.py:163
  33.8 3.1 %collective-permute-start.8 = (bf16[10,4,16,512]{3,2,1,0:T(8,128)(2,1)S(1)}, bf16[10,4,16,512]{3,2,1,0:T(8,128)(2,1)S(1)}, u32[]{:S(2)}, u32[]{:S(2)}) collective-permute-start(bf16[10,4,16,512]{3,2,1,0:T(8,128)(2,1)S(1)} %get-tuple-element.91), channel_id=1, source_target_pairs={{0,24},{4,12},{8,16},{12,4},{16,8},{20,28},{24,0},{28,20},{32,56},... | collective-permute-start | bytes 1966088 | tf_op jit(solution)/shard_map/ppermute | solution.py:134
  36.9 0.0 collective-permute-done.10.refs_2_
  36.9 2.9 %collective-permute-start.9 = (bf16[10,4,16,512]{3,2,1,0:T(8,128)(2,1)S(1)}, bf16[10,4,16,512]{3,2,1,0:T(8,128)(2,1)S(1)}, u32[]{:S(2)}, u32[]{:S(2)}) collective-permute-start(bf16[10,4,16,512]{3,2,1,0:T(8,128)(2,1)S(1)} %get-tuple-element.92), channel_id=1, source_target_pairs={{0,96},{4,36},{8,104},{12,44},{16,112},{20,52},{24,120},{28,60},{3... | collective-permute-start | bytes 1966088 | tf_op jit(solution)/shard_map/ppermute | solution.py:134
  39.8 0.0 copy-start.2
  39.8 1.8 %shard_map.93 = (bf16[4,4,16,512]{3,2,1,0:T(8,128)(2,1)S(1)}, bf16[4,4,16,512]{3,2,1,0:T(8,128)(2,1)S(1)}) custom-call(s32[3]{0:T(128)S(1)} %pad_add_fusion.pos, bf16[28,4,4,2,16,512]{5,4,3,2,1,0:T(8,128)(2,1)} %bitcast.79, bf16[28,4,4,2,16,512]{5,4,3,2,1,0:T(8,128)(2,1)} %bitcast.80, bf16[2,4,4,16,512]{4,3,2,1,0:T(8,128)(2,1)S(1)} %collective-permute-done.10.refs_2_, ...), custom_call_target="tpu_custom_call" | custom-call | flops 1048576 | bytes 2097152 | tf_op jit(solution)/shard_map/pallas_call | solution.py:163
  41.6 2.8 %collective-permute-start.14 = (bf16[4,4,16,512]{3,2,1,0:T(8,128)(2,1)S(1)}, bf16[4,4,16,512]{3,2,1,0:T(8,128)(2,1)S(1)}, u32[]{:S(2)}, u32[]{:S(2)}) collective-permute-start(bf16[4,4,16,512]{3,2,1,0:T(8,128)(2,1)S(1)} %get-tuple-element.104), channel_id=1, source_target_pairs={{0,24},{4,12},{8,16},{12,4},{16,8},{20,28},{24,0},{28,20},{32,56},... | collective-permute-start | bytes 786440 | tf_op jit(solution)/shard_map/ppermute | solution.py:134
  44.4 6.2 %collective-permute-start.15 = (bf16[4,4,16,512]{3,2,1,0:T(8,128)(2,1)S(1)}, bf16[4,4,16,512]{3,2,1,0:T(8,128)(2,1)S(1)}, u32[]{:S(2)}, u32[]{:S(2)}) collective-permute-start(bf16[4,4,16,512]{3,2,1,0:T(8,128)(2,1)S(1)} %get-tuple-element.105), channel_id=1, source_target_pairs={{0,96},{4,36},{8,104},{12,44},{16,112},{20,52},{24,120},{28,60},{3... | collective-permute-start | bytes 786440 | tf_op jit(solution)/shard_map/ppermute | solution.py:134
  50.6 3.3 %shard_map.92 = (bf16[2,10,16,512]{3,2,1,0:T(8,128)(2,1)S(1)}, f32[10,16,512]{2,1,0:T(8,128)S(1)}, f32[10,16,512]{2,1,0:T(8,128)S(1)}, bf16[2,10,16,512]{3,2,1,0...) custom-call(s32[3]{0:T(128)S(1)} %pad_add_fusion.pos, ...), custom_call_target="tpu_custom_call" | custom-call | flops 2621440 | bytes 5242880 | tf_op jit(solution)/shard_map/pallas_call | solution.py:163
  53.9 1.0 collective-permute-done.15.refs_7_
  54.9 2.8 %shard_map.94 = (bf16[2,14,16,512]{3,2,1,0:T(8,128)(2,1)}, f32[14,16,512]{2,1,0:T(8,128)S(1)}, f32[14,16,512]{2,1,0:T(8,128)S(1)}, bf16[2,14,16,512]{3,2,1,0:T(8...) custom-call(s32[3]{0:T(128)S(1)} %pad_add_fusion.pos, bf16[28,4,4,2,16,512]{5,4,3,2,1,0:T(8,128)(2,1)} %bitcast.83, ...), custom_call_target="tpu_custom_call" | custom-call | flops 3670016 | bytes 7340032 | tf_op jit(solution)/shard_map/pallas_call | solution.py:163
  57.8 10.5 %collective-permute-done.16.refs_1_ = bf16[2,14,16,512]{3,2,1,0:T(8,128)(2,1)S(1)} collective-permute-done((bf16[2,14,16,512]{3,2,1,0:T(8,128)(2,1)}, bf16[2,14,16,512]{3,2,1,0:T(8,128)(2,1)S(1)}, u32[]{:S(2)}, u32[]{:S(2)}) %collective-permute-start.16) | collective-permute-done | bytes 458784 | tf_op jit(solution)/shard_map/ppermute | solution.py:134
  68.2 0.1 fusion.1
  68.3 3.6 %collective-permute-start.17 = (bf16[14,16,512]{2,1,0:T(8,128)(2,1)S(1)}, bf16[14,16,512]{2,1,0:T(8,128)(2,1)S(1)}, u32[]{:S(2)}, u32[]{:S(2)}) collective-permute-start(bf16[14,16,512]{2,1,0:T(8,128)(2,1)S(1)} %fusion.1), channel_id=1, source_target_pairs={{0,96},{4,36},{8,104},{12,44},{16,112},{20,52},{24,120},{28,60},{3... | collective-permute-start | bytes 688136 | tf_op jit(solution)/shard_map/ppermute | solution.py:134
  71.9 0.1 fusion
  72.0 0.1 collective-permute-start.19
  72.1 0.1 add_minimum_fusion
  72.2 0.1 min.12.wanted
  72.3 3.6 %collective-permute-done.17.refs_2_ = bf16[14,16,512]{2,1,0:T(8,128)(2,1)S(1)} collective-permute-done((bf16[14,16,512]{2,1,0:T(8,128)(2,1)S(1)}, bf16[14,16,512]{2,1,0:T(8,128)(2,1)S(1)}, u32[]{:S(2)}, u32[]{:S(2)}) %collective-permute-start.17) | collective-permute-done | bytes 229408 | tf_op jit(solution)/shard_map/ppermute | solution.py:134
  75.9 3.4 %collective-permute-done.19.refs_5_ = bf16[14,16,512]{2,1,0:T(8,128)(2,1)S(1)} collective-permute-done((bf16[14,16,512]{2,1,0:T(8,128)(2,1)S(1)}, bf16[14,16,512]{2,1,0:T(8,128)(2,1)S(1)}, u32[]{:S(2)}, u32[]{:S(2)}) %collective-permute-start.19) | collective-permute-done | bytes 229408 | tf_op jit(solution)/shard_map/ppermute | solution.py:134
  79.3 2.0 %shard_map.95 = bf16[64,16,512]{2,1,0:T(8,128)(2,1)} custom-call(s32[64]{0:T(128)S(1)} %min.12.wanted, f32[14,16,512]{2,1,0:T(8,128)S(1)} %get-tuple-element.118.refs_0_, bf16[2,14,16,512]{3,2,1,0:T(8,128)(2,1)S(1)} %collective-permute-done.16.refs_1_, bf16[14,16,512]{2,1,0:T(8,128)(2,1)S(1)} %collective-permute-done.17.refs_2_, ...), custom_call_target="tpu_custom_call" | custom-call | flops 2097152 | bytes 4194304 | tf_op jit(solution)/shard_map/pallas_call | solution.py:163
  81.3 4.2 %all-to-all-start = ((bf16[32,2,16,512]{3,2,1,0:T(8,128)(2,1)}), bf16[32,2,16,512]{3,2,1,0:T(8,128)(2,1)S(1)}, u32[]{:S(2)}, u32[]{:S(2)}) async-start(bf16[32,2,16,512]{3,2,1,0:T(8,128)(2,1)} %bitcast.8), calls=%async_computation | async-start | bytes 2097152 | tf_op jit(solution)/shard_map/all_to_all | solution.py:400
  85.6 1.2 dynamic_slice.14
  86.8 15.9 %all-to-all-done.block_ref = bf16[32,2,16,512]{3,2,1,0:T(8,128)(2,1)S(1)} async-done(((bf16[32,2,16,512]{3,2,1,0:T(8,128)(2,1)}), bf16[32,2,16,512]{3,2,1,0:T(8,128)(2,1)S(1)}, u32[]{:S(2)}, u32[]{:S(2)}) %all-to-all-start) | async-done | bytes 1048608 | tf_op jit(solution)/shard_map/all_to_all | solution.py:400
  102.7 1.6 copy-done.4
  104.3 3.2 %shard_map.96 = (f32[2,512,512]{2,1,0:T(8,128)}, f32[2,512,512]{2,1,0:T(8,128)}, bf16[32,2,16,512]{3,2,1,0:T(8,128)(2,1)}) custom-call(s32[1]{0:T(128)} %bitcast.count_ref, bf16[32,2,16,512]{3,2,1,0:T(8,128)(2,1)S(1)} %all-to-all-done.block_ref, f32[2,512,512]{2,1,0:T(8,128)S(1)} %bitcast.51, f32[2,512,512]{2,1,0:T(8,128)S(1)} %bitcast.52), custom_call_target="tpu_custom_call" | custom-call | flops 9663676416 | bytes 10485760 | tf_op jit(solution)/shard_map/pallas_call | solution.py:83
  107.5 15.2 %all-to-all-start.1 = ((bf16[32,2,16,512]{3,2,1,0:T(8,128)(2,1)}), bf16[32,2,16,512]{3,2,1,0:T(8,128)(2,1)S(1)}, u32[]{:S(2)}, u32[]{:S(2)}) async-start(bf16[32,2,16,512]{3,2,1,0:T(8,128)(2,1)} %get-tuple-element.126), calls=%async_computation.1 | async-start | bytes 2097152 | tf_op jit(solution)/shard_map/all_to_all | solution.py:403
  122.8 0.7 gather_fusion
  123.6 16.5 %all-to-all-done.1 = bf16[32,2,16,512]{3,2,1,0:T(8,128)(2,1)S(1)} async-done(((bf16[32,2,16,512]{3,2,1,0:T(8,128)(2,1)}), bf16[32,2,16,512]{3,2,1,0:T(8,128)(2,1)S(1)}, u32[]{:S(2)}, u32[]{:S(2)}) %all-to-all-start.1) | async-done | bytes 1048608 | tf_op jit(solution)/shard_map/all_to_all | solution.py:403
  140.0 0.6 gather_fusion.1
  140.7 2.8 %collective-permute-start.24 = (bf16[28,16,512]{2,1,0:T(8,128)(2,1)S(1)}, bf16[28,16,512]{2,1,0:T(8,128)(2,1)S(1)}, u32[]{:S(2)}, u32[]{:S(2)}) collective-permute-start(bf16[28,16,512]{2,1,0:T(8,128)(2,1)S(1)} %gather_fusion.1), channel_id=1, source_target_pairs={{0,3},{1,0},{2,1},{3,2},{4,5},{5,6},{6,7},{7,4},{8,11},{9,8},{10,9... | collective-permute-start | bytes 1376264 | tf_op jit(solution)/shard_map/ppermute | solution.py:365
  143.5 0.7 collective-permute-start.21
  144.2 0.2 broadcast_in_dim.33
  144.5 7.5 %collective-permute-done.20 = bf16[14,16,512]{2,1,0:T(8,128)(2,1)S(1)} collective-permute-done((bf16[14,16,512]{2,1,0:T(8,128)(2,1)S(1)}, bf16[14,16,512]{2,1,0:T(8,128)(2,1)S(1)}, u32[]{:S(2)}, u32[]{:S(2)}) %collective-permute-start.20) | collective-permute-done | bytes 229408 | tf_op jit(solution)/shard_map/ppermute | solution.py:365
  152.0 2.5 %collective-permute-done.21 = bf16[14,16,512]{2,1,0:T(8,128)(2,1)S(1)} collective-permute-done((bf16[14,16,512]{2,1,0:T(8,128)(2,1)S(1)}, bf16[14,16,512]{2,1,0:T(8,128)(2,1)S(1)}, u32[]{:S(2)}, u32[]{:S(2)}) %collective-permute-start.21) | collective-permute-done | bytes 229408 | tf_op jit(solution)/shard_map/ppermute | solution.py:365
  154.5 4.7 %collective-permute-done.22 = bf16[14,16,512]{2,1,0:T(8,128)(2,1)S(1)} collective-permute-done((bf16[14,16,512]{2,1,0:T(8,128)(2,1)S(1)}, bf16[14,16,512]{2,1,0:T(8,128)(2,1)S(1)}, u32[]{:S(2)}, u32[]{:S(2)}) %collective-permute-start.22) | collective-permute-done | bytes 229408 | tf_op jit(solution)/shard_map/ppermute | solution.py:365
  159.3 2.4 %collective-permute-done.23 = bf16[14,16,512]{2,1,0:T(8,128)(2,1)S(1)} collective-permute-done((bf16[14,16,512]{2,1,0:T(8,128)(2,1)S(1)}, bf16[14,16,512]{2,1,0:T(8,128)(2,1)S(1)}, u32[]{:S(2)}, u32[]{:S(2)}) %collective-permute-start.23) | collective-permute-done | bytes 229408 | tf_op jit(solution)/shard_map/ppermute | solution.py:365
  161.8 0.0 copy-start.5
  161.8 1.2 copy-done.5
  (37 shorter events, 0.3 us)
Async XLA Ops:
  0.6 71.4 %copy-start = (s32[4,32]{1,0:T(4,128)S(1)}, s32[4,32]{1,0:T(4,128)}, u32[]{:S(2)}) copy-start(s32[4,32]{1,0:T(4,128)} %param.11) | copy-start | bytes 1540
  3.2 5.6 %collective-permute-start = (bf16[2,10,4,16,512]{4,3,2,1,0:T(8,128)(2,1)S(1)}, bf16[2,10,4,16,512]{4,3,2,1,0:T(8,128)(2,1)S(1)}, u32[]{:S(2)}, u32[]{:S(2)}) collective-permute-start(bf16[2,10,4,16,512]{4,3,2,1,0:T(8,128)(2,1)S(1)} %get-tuple-element.74), channel_id=1, source_target_pairs={{0,4},{4,0},{8,12},{12,8},{16,20},{20,16},{24,28},{28,24},{32,36},... | collective-permute-start | bytes 3932168 | tf_op jit(solution)/shard_map/ppermute | solution.py:138
  3.3 5.5 %collective-permute-start.1 = (bf16[2,10,4,16,512]{4,3,2,1,0:T(8,128)(2,1)S(1)}, bf16[2,10,4,16,512]{4,3,2,1,0:T(8,128)(2,1)S(1)}, u32[]{:S(2)}, u32[]{:S(2)}) collective-permute-start(bf16[2,10,4,16,512]{4,3,2,1,0:T(8,128)(2,1)S(1)} %get-tuple-element.75), channel_id=1, source_target_pairs={{0,4},{4,0},{8,12},{12,8},{16,20},{20,16},{24,28},{28,24},{32,36},... | collective-permute-start | bytes 3932168 | tf_op jit(solution)/shard_map/ppermute | solution.py:138
  5.6 9.8 %collective-permute-start.2 = (bf16[2,4,4,16,512]{4,3,2,1,0:T(8,128)(2,1)S(1)}, bf16[2,4,4,16,512]{4,3,2,1,0:T(8,128)(2,1)S(1)}, u32[]{:S(2)}, u32[]{:S(2)}) collective-permute-start(bf16[2,4,4,16,512]{4,3,2,1,0:T(8,128)(2,1)S(1)} %get-tuple-element.79), channel_id=1, source_target_pairs={{0,4},{4,0},{8,12},{12,8},{16,20},{20,16},{24,28},{28,24},{32,36},... | collective-permute-start | bytes 1572872 | tf_op jit(solution)/shard_map/ppermute | solution.py:138
  8.2 16.5 %collective-permute-start.4 = (bf16[2,10,4,16,512]{4,3,2,1,0:T(8,128)(2,1)S(1)}, bf16[2,10,4,16,512]{4,3,2,1,0:T(8,128)(2,1)S(1)}, u32[]{:S(2)}, u32[]{:S(2)}) collective-permute-start(bf16[2,10,4,16,512]{4,3,2,1,0:T(8,128)(2,1)S(1)} %get-tuple-element.87), channel_id=1, source_target_pairs={{0,4},{4,0},{8,12},{12,8},{16,20},{20,16},{24,28},{28,24},{32,36},... | collective-permute-start | bytes 3932168 | tf_op jit(solution)/shard_map/ppermute | solution.py:138
  8.7 16.1 %collective-permute-start.5 = (bf16[2,10,4,16,512]{4,3,2,1,0:T(8,128)(2,1)S(1)}, bf16[2,10,4,16,512]{4,3,2,1,0:T(8,128)(2,1)S(1)}, u32[]{:S(2)}, u32[]{:S(2)}) collective-permute-start(bf16[2,10,4,16,512]{4,3,2,1,0:T(8,128)(2,1)S(1)} %get-tuple-element.88), channel_id=1, source_target_pairs={{0,4},{4,0},{8,12},{12,8},{16,20},{20,16},{24,28},{28,24},{32,36},... | collective-permute-start | bytes 3932168 | tf_op jit(solution)/shard_map/ppermute | solution.py:138
  11.7 17.7 %collective-permute-start.6 = (bf16[2,10,4,16,512]{4,3,2,1,0:T(8,128)(2,1)S(1)}, bf16[2,10,4,16,512]{4,3,2,1,0:T(8,128)(2,1)S(1)}, u32[]{:S(2)}, u32[]{:S(2)}) collective-permute-start(bf16[2,10,4,16,512]{4,3,2,1,0:T(8,128)(2,1)S(1)} %get-tuple-element.89), channel_id=1, source_target_pairs={{0,8},{4,28},{8,0},{12,20},{16,24},{20,12},{24,16},{28,4},{32,40},... | collective-permute-start | bytes 3932168 | tf_op jit(solution)/shard_map/ppermute | solution.py:134
  13.5 18.0 %collective-permute-start.7 = (bf16[2,10,4,16,512]{4,3,2,1,0:T(8,128)(2,1)S(1)}, bf16[2,10,4,16,512]{4,3,2,1,0:T(8,128)(2,1)S(1)}, u32[]{:S(2)}, u32[]{:S(2)}) collective-permute-start(bf16[2,10,4,16,512]{4,3,2,1,0:T(8,128)(2,1)S(1)} %get-tuple-element.90), channel_id=1, source_target_pairs={{0,32},{4,100},{8,40},{12,108},{16,48},{20,116},{24,56},{28,124},{... | collective-permute-start | bytes 3932168 | tf_op jit(solution)/shard_map/ppermute | solution.py:134
  15.4 5.0 %collective-permute-start.3 = (bf16[2,4,4,16,512]{4,3,2,1,0:T(8,128)(2,1)S(1)}, bf16[2,4,4,16,512]{4,3,2,1,0:T(8,128)(2,1)S(1)}, u32[]{:S(2)}, u32[]{:S(2)}) collective-permute-start(bf16[2,4,4,16,512]{4,3,2,1,0:T(8,128)(2,1)S(1)} %get-tuple-element.80), channel_id=1, source_target_pairs={{0,4},{4,0},{8,12},{12,8},{16,20},{20,16},{24,28},{28,24},{32,36},... | collective-permute-start | bytes 1572872 | tf_op jit(solution)/shard_map/ppermute | solution.py:138
  24.2 12.7 %collective-permute-start.10 = (bf16[2,4,4,16,512]{4,3,2,1,0:T(8,128)(2,1)S(1)}, bf16[2,4,4,16,512]{4,3,2,1,0:T(8,128)(2,1)S(1)}, u32[]{:S(2)}, u32[]{:S(2)}) collective-permute-start(bf16[2,4,4,16,512]{4,3,2,1,0:T(8,128)(2,1)S(1)} %get-tuple-element.100), channel_id=1, source_target_pairs={{0,4},{4,0},{8,12},{12,8},{16,20},{20,16},{24,28},{28,24},{32,36},... | collective-permute-start | bytes 1572872 | tf_op jit(solution)/shard_map/ppermute | solution.py:138
  24.7 15.1 %collective-permute-start.11 = (bf16[2,4,4,16,512]{4,3,2,1,0:T(8,128)(2,1)S(1)}, bf16[2,4,4,16,512]{4,3,2,1,0:T(8,128)(2,1)S(1)}, u32[]{:S(2)}, u32[]{:S(2)}) collective-permute-start(bf16[2,4,4,16,512]{4,3,2,1,0:T(8,128)(2,1)S(1)} %get-tuple-element.101), channel_id=1, source_target_pairs={{0,4},{4,0},{8,12},{12,8},{16,20},{20,16},{24,28},{28,24},{32,36},... | collective-permute-start | bytes 1572872 | tf_op jit(solution)/shard_map/ppermute | solution.py:138
  24.8 15.0 %collective-permute-start.12 = (bf16[2,4,4,16,512]{4,3,2,1,0:T(8,128)(2,1)S(1)}, bf16[2,4,4,16,512]{4,3,2,1,0:T(8,128)(2,1)S(1)}, u32[]{:S(2)}, u32[]{:S(2)}) collective-permute-start(bf16[2,4,4,16,512]{4,3,2,1,0:T(8,128)(2,1)S(1)} %get-tuple-element.102), channel_id=1, source_target_pairs={{0,8},{4,28},{8,0},{12,20},{16,24},{20,12},{24,16},{28,4},{32,40},... | collective-permute-start | bytes 1572872 | tf_op jit(solution)/shard_map/ppermute | solution.py:134
  29.4 10.3 %collective-permute-start.13 = (bf16[2,4,4,16,512]{4,3,2,1,0:T(8,128)(2,1)S(1)}, bf16[2,4,4,16,512]{4,3,2,1,0:T(8,128)(2,1)S(1)}, u32[]{:S(2)}, u32[]{:S(2)}) collective-permute-start(bf16[2,4,4,16,512]{4,3,2,1,0:T(8,128)(2,1)S(1)} %get-tuple-element.103), channel_id=1, source_target_pairs={{0,32},{4,100},{8,40},{12,108},{16,48},{20,116},{24,56},{28,124},{... | collective-permute-start | bytes 1572872 | tf_op jit(solution)/shard_map/ppermute | solution.py:134
  31.4 2.4 %copy-start.1 = (bf16[2,10,4,16,512]{4,3,2,1,0:T(8,128)(2,1)}, bf16[2,10,4,16,512]{4,3,2,1,0:T(8,128)(2,1)S(1)}, u32[]{:S(2)}) copy-start(bf16[2,10,4,16,512]{4,3,2,1,0:T(8,128)(2,1)S(1)} %collective-permute-done.7.refs_5_) | copy-start | bytes 3932164
  33.8 16.8 %collective-permute-start.8 = (bf16[10,4,16,512]{3,2,1,0:T(8,128)(2,1)S(1)}, bf16[10,4,16,512]{3,2,1,0:T(8,128)(2,1)S(1)}, u32[]{:S(2)}, u32[]{:S(2)}) collective-permute-start(bf16[10,4,16,512]{3,2,1,0:T(8,128)(2,1)S(1)} %get-tuple-element.91), channel_id=1, source_target_pairs={{0,24},{4,12},{8,16},{12,4},{16,8},{20,28},{24,0},{28,20},{32,56},... | collective-permute-start | bytes 1966088 | tf_op jit(solution)/shard_map/ppermute | solution.py:134
  36.9 13.7 %collective-permute-start.9 = (bf16[10,4,16,512]{3,2,1,0:T(8,128)(2,1)S(1)}, bf16[10,4,16,512]{3,2,1,0:T(8,128)(2,1)S(1)}, u32[]{:S(2)}, u32[]{:S(2)}) collective-permute-start(bf16[10,4,16,512]{3,2,1,0:T(8,128)(2,1)S(1)} %get-tuple-element.92), channel_id=1, source_target_pairs={{0,96},{4,36},{8,104},{12,44},{16,112},{20,52},{24,120},{28,60},{3... | collective-permute-start | bytes 1966088 | tf_op jit(solution)/shard_map/ppermute | solution.py:134
  39.8 1.8 %copy-start.2 = (bf16[2,4,4,16,512]{4,3,2,1,0:T(8,128)(2,1)}, bf16[2,4,4,16,512]{4,3,2,1,0:T(8,128)(2,1)S(1)}, u32[]{:S(2)}) copy-start(bf16[2,4,4,16,512]{4,3,2,1,0:T(8,128)(2,1)S(1)} %collective-permute-done.13.refs_5_) | copy-start | bytes 1572868
  41.6 12.3 %collective-permute-start.14 = (bf16[4,4,16,512]{3,2,1,0:T(8,128)(2,1)S(1)}, bf16[4,4,16,512]{3,2,1,0:T(8,128)(2,1)S(1)}, u32[]{:S(2)}, u32[]{:S(2)}) collective-permute-start(bf16[4,4,16,512]{3,2,1,0:T(8,128)(2,1)S(1)} %get-tuple-element.104), channel_id=1, source_target_pairs={{0,24},{4,12},{8,16},{12,4},{16,8},{20,28},{24,0},{28,20},{32,56},... | collective-permute-start | bytes 786440 | tf_op jit(solution)/shard_map/ppermute | solution.py:134
  44.4 10.5 %collective-permute-start.15 = (bf16[4,4,16,512]{3,2,1,0:T(8,128)(2,1)S(1)}, bf16[4,4,16,512]{3,2,1,0:T(8,128)(2,1)S(1)}, u32[]{:S(2)}, u32[]{:S(2)}) collective-permute-start(bf16[4,4,16,512]{3,2,1,0:T(8,128)(2,1)S(1)} %get-tuple-element.105), channel_id=1, source_target_pairs={{0,96},{4,36},{8,104},{12,44},{16,112},{20,52},{24,120},{28,60},{3... | collective-permute-start | bytes 786440 | tf_op jit(solution)/shard_map/ppermute | solution.py:134
  57.7 10.5 %collective-permute-start.16 = (bf16[2,14,16,512]{3,2,1,0:T(8,128)(2,1)}, bf16[2,14,16,512]{3,2,1,0:T(8,128)(2,1)S(1)}, u32[]{:S(2)}, u32[]{:S(2)}) collective-permute-start(bf16[2,14,16,512]{3,2,1,0:T(8,128)(2,1)} %get-tuple-element.119), channel_id=1, source_target_pairs={{0,32},{4,100},{8,40},{12,108},{16,48},{20,116},{24,56},{28,124},{... | collective-permute-start | bytes 1376264 | tf_op jit(solution)/shard_map/ppermute | solution.py:134
  57.8 14.2 %collective-permute-start.18 = (bf16[2,14,16,512]{3,2,1,0:T(8,128)(2,1)S(1)}, bf16[2,14,16,512]{3,2,1,0:T(8,128)(2,1)S(1)}, u32[]{:S(2)}, u32[]{:S(2)}) collective-permute-start(bf16[2,14,16,512]{3,2,1,0:T(8,128)(2,1)S(1)} %get-tuple-element.122), channel_id=1, source_target_pairs={{0,8},{4,28},{8,0},{12,20},{16,24},{20,12},{24,16},{28,4},{32,40},... | collective-permute-start | bytes 1376264 | tf_op jit(solution)/shard_map/ppermute | solution.py:134
  68.3 7.6 %collective-permute-start.17 = (bf16[14,16,512]{2,1,0:T(8,128)(2,1)S(1)}, bf16[14,16,512]{2,1,0:T(8,128)(2,1)S(1)}, u32[]{:S(2)}, u32[]{:S(2)}) collective-permute-start(bf16[14,16,512]{2,1,0:T(8,128)(2,1)S(1)} %fusion.1), channel_id=1, source_target_pairs={{0,96},{4,36},{8,104},{12,44},{16,112},{20,52},{24,120},{28,60},{3... | collective-permute-start | bytes 688136 | tf_op jit(solution)/shard_map/ppermute | solution.py:134
  72.0 7.3 %collective-permute-start.19 = (bf16[14,16,512]{2,1,0:T(8,128)(2,1)S(1)}, bf16[14,16,512]{2,1,0:T(8,128)(2,1)S(1)}, u32[]{:S(2)}, u32[]{:S(2)}) collective-permute-start(bf16[14,16,512]{2,1,0:T(8,128)(2,1)S(1)} %fusion), channel_id=1, source_target_pairs={{0,24},{4,12},{8,16},{12,4},{16,8},{20,28},{24,0},{28,20},{32,56},... | collective-permute-start | bytes 688136 | tf_op jit(solution)/shard_map/ppermute | solution.py:134
  81.3 21.4 %copy-start.3 = (f32[1,2,512,512]{3,2,1,0:T(8,128)S(1)}, f32[1,2,512,512]{3,2,1,0:T(8,128)}, u32[]{:S(2)}) copy-start(f32[1,2,512,512]{3,2,1,0:T(8,128)} %param.7) | copy-start | bytes 6291460
  81.3 21.4 %all-to-all-start = ((bf16[32,2,16,512]{3,2,1,0:T(8,128)(2,1)}), bf16[32,2,16,512]{3,2,1,0:T(8,128)(2,1)S(1)}, u32[]{:S(2)}, u32[]{:S(2)}) async-start(bf16[32,2,16,512]{3,2,1,0:T(8,128)(2,1)} %bitcast.8), calls=%async_computation | async-start | bytes 2097152 | tf_op jit(solution)/shard_map/all_to_all | solution.py:400
  102.7 1.6 copy-start.4
  107.5 15.3 %copy-start.6 = (s32[4,28]{1,0:T(4,128)S(1)}, s32[4,28]{1,0:T(4,128)}, u32[]{:S(2)}) copy-start(s32[4,28]{1,0:T(4,128)} %param.9) | copy-start | bytes 1348
  107.5 32.5 %all-to-all-start.1 = ((bf16[32,2,16,512]{3,2,1,0:T(8,128)(2,1)}), bf16[32,2,16,512]{3,2,1,0:T(8,128)(2,1)S(1)}, u32[]{:S(2)}, u32[]{:S(2)}) async-start(bf16[32,2,16,512]{3,2,1,0:T(8,128)(2,1)} %get-tuple-element.126), calls=%async_computation.1 | async-start | bytes 2097152 | tf_op jit(solution)/shard_map/all_to_all | solution.py:403
  140.7 21.1 %collective-permute-start.24 = (bf16[28,16,512]{2,1,0:T(8,128)(2,1)S(1)}, bf16[28,16,512]{2,1,0:T(8,128)(2,1)S(1)}, u32[]{:S(2)}, u32[]{:S(2)}) collective-permute-start(bf16[28,16,512]{2,1,0:T(8,128)(2,1)S(1)} %gather_fusion.1), channel_id=1, source_target_pairs={{0,3},{1,0},{2,1},{3,2},{4,5},{5,6},{6,7},{7,4},{8,11},{9,8},{10,9... | collective-permute-start | bytes 1376264 | tf_op jit(solution)/shard_map/ppermute | solution.py:365
  143.5 8.5 %collective-permute-start.20 = (bf16[14,16,512]{2,1,0:T(8,128)(2,1)S(1)}, bf16[14,16,512]{2,1,0:T(8,128)(2,1)S(1)}, u32[]{:S(2)}, u32[]{:S(2)}) collective-permute-start(bf16[14,16,512]{2,1,0:T(8,128)(2,1)S(1)} %get-tuple-element.128), channel_id=1, source_target_pairs={{0,1},{1,2},{2,3},{3,0},{4,7},{5,4},{6,5},{7,6},{8,9},{9,10},{10,1... | collective-permute-start | bytes 688136 | tf_op jit(solution)/shard_map/ppermute | solution.py:365
  143.5 11.0 %collective-permute-start.21 = (bf16[14,16,512]{2,1,0:T(8,128)(2,1)S(1)}, bf16[14,16,512]{2,1,0:T(8,128)(2,1)S(1)}, u32[]{:S(2)}, u32[]{:S(2)}) collective-permute-start(bf16[14,16,512]{2,1,0:T(8,128)(2,1)S(1)} %get-tuple-element.127), channel_id=1, source_target_pairs={{0,1},{1,2},{2,3},{3,0},{4,7},{5,4},{6,5},{7,6},{8,9},{9,10},{10,1... | collective-permute-start | bytes 688136 | tf_op jit(solution)/shard_map/ppermute | solution.py:365
  152.0 7.2 %collective-permute-start.22 = (bf16[14,16,512]{2,1,0:T(8,128)(2,1)S(1)}, bf16[14,16,512]{2,1,0:T(8,128)(2,1)S(1)}, u32[]{:S(2)}, u32[]{:S(2)}) collective-permute-start(bf16[14,16,512]{2,1,0:T(8,128)(2,1)S(1)} %collective-permute-done.20), channel_id=1, source_target_pairs={{0,1},{1,2},{2,3},{3,0},{4,7},{5,4},{6,5},{7,6},{8,9},{9,10},{10,1... | collective-permute-start | bytes 688136 | tf_op jit(solution)/shard_map/ppermute | solution.py:365
  154.5 7.2 %collective-permute-start.23 = (bf16[14,16,512]{2,1,0:T(8,128)(2,1)S(1)}, bf16[14,16,512]{2,1,0:T(8,128)(2,1)S(1)}, u32[]{:S(2)}, u32[]{:S(2)}) collective-permute-start(bf16[14,16,512]{2,1,0:T(8,128)(2,1)S(1)} %collective-permute-done.21), channel_id=1, source_target_pairs={{0,1},{1,2},{2,3},{3,0},{4,7},{5,4},{6,5},{7,6},{8,9},{9,10},{10,1... | collective-permute-start | bytes 688136 | tf_op jit(solution)/shard_map/ppermute | solution.py:365
  161.8 1.2 copy-start.5

commit v3 on v2

--- a/solution.py
+++ b/solution.py
@@ -34,66 +34,106 @@
     )
 
 
+def mirrored(pair):
+    top, low = (part.astype(jnp.bfloat16) for part in pair)
+    half = low.shape[0]
+    return jnp.concatenate([top, jnp.concatenate([top[:, half:].T, low], axis=1)], axis=0)
+
+
+def product(first, second):
+    half = first.shape[0] // 2
+    return dot(first[:half], second), dot(first[half:], second[:, half:])
+
+
+def mix(*terms):
+    return tuple(sum(factor * pair[k] for factor, pair in terms) for k in (0, 1))
+
+
 def roots(statistics):
     both = range(len(statistics))
+    half = statistics[0].shape[0] // 2
     scales = [jnp.max(jnp.sum(jnp.abs(a), axis=0, keepdims=True), axis=1, keepdims=True) + 1e-06 for a in statistics]
-    z = [statistics[i] * (1.0 / scales[i]) for i in both]
-    zb = [z[i].astype(jnp.bfloat16) for i in both]
-    square = [dot(zb[i], zb[i]) for i in both]
-    e = [(0.0625 * square[i] - 0.625 * z[i]).astype(jnp.bfloat16) for i in both]
-    t = [START * z[i] + dot(e[i], zb[i]) for i in both]
-    y = [START * t[i] + dot(e[i], t[i]) for i in both]
-    yb = [y[i].astype(jnp.bfloat16) for i in both]
-    y2 = [dot(yb[i], yb[i]) for i in both]
-    y3 = [dot(y2[i], yb[i]) for i in both]
-    y3b = [y3[i].astype(jnp.bfloat16) for i in both]
-    high = [(TAIL[6] * y3[i] + TAIL[5] * y2[i] + TAIL[4] * y[i]).astype(jnp.bfloat16) for i in both]
-    q = [TAIL[1] * y[i] + TAIL[2] * y2[i] + TAIL[3] * y3[i] + dot(high[i], y3b[i]) for i in both]
-    f = [1.25 * q[i] - (0.25 * TAIL[0]) * z[i] - 0.25 * dot(zb[i], q[i]) for i in both]
+    z = [tuple(v * (1.0 / scales[i]) for v in (statistics[i][:half], statistics[i][half:, half:])) for i in both]
+    zb = [mirrored(z[i]) for i in both]
+    square = [product(zb[i], zb[i]) for i in both]
+    e = [mirrored(mix((0.0625, square[i]), (-0.625, z[i]))) for i in both]
+    t = [mix((START, z[i]), (1.0, product(e[i], zb[i]))) for i in both]
+    tb = [mirrored(t[i]) for i in both]
+    y = [mix((START, t[i]), (1.0, product(e[i], tb[i]))) for i in both]
+    yb = [mirrored(y[i]) for i in both]
+    y2 = [product(yb[i], yb[i]) for i in both]
+    y2b = [mirrored(y2[i]) for i in both]
+    y3 = [product(y2b[i], yb[i]) for i in both]
+    y3b = [mirrored(y3[i]) for i in both]
+    high = [mirrored(mix((TAIL[6], y3[i]), (TAIL[5], y2[i]), (TAIL[4], y[i]))) for i in both]
+    q = [mix((TAIL[1], y[i]), (TAIL[2], y2[i]), (TAIL[3], y3[i]), (1.0, product(high[i], y3b[i]))) for i in both]
+    qb = [mirrored(q[i]) for i in both]
+    f = [mirrored(mix((1.25, q[i]), (-0.25 * TAIL[0], z[i]), (-0.25, product(zb[i], qb[i])))) for i in both]
     return f, [1.0 / jnp.sqrt(jnp.sqrt(s)) for s in scales]
 
 
-def slot_kernel(count_ref, block_ref, left_ref, right_ref, new_left_ref, new_right_ref, update_ref):
-    alive = pl.program_id(0) < count_ref[0]
+def slot_kernel(count_ref, block_ref, left_ref, right_ref, new_left_ref, new_right_ref, update_ref, held, sems):
+    slot = pl.program_id(0)
+    alive = slot < count_ref[0]
     extent = left_ref.shape[-1]
+    outs = (new_left_ref, new_right_ref)
 
     @pl.when(jnp.logical_not(alive))
     def _():
-        new_left_ref[...] = left_ref[...]
-        new_right_ref[...] = right_ref[...]
+        held[0] = left_ref[0]
+        held[1] = right_ref[0]
         update_ref[...] = jnp.zeros_like(update_ref)
 
     @pl.when(alive)
     def _():
         block = block_ref[:, 0].reshape(extent, extent)
-        fresh_left = 0.9 * left_ref[0] + (0.1 / extent) * dot(block, block, ((1,), (1,)))
-        fresh_right = 0.9 * right_ref[0] + (0.1 / extent) * dot(block, block, ((0,), (0,)))
-        new_left_ref[0] = fresh_left
-        new_right_ref[0] = fresh_right
-        (f_left, f_right), (c_left, c_right) = roots([fresh_left, fresh_right])
+        low = pl.ds(extent // 2, extent // 2)
+        top = pl.ds(0, extent // 2)
+        rows, turned = block[: extent // 2], block[:, : extent // 2]
+        held[0, top] = 0.9 * left_ref[0, top] + (0.1 / extent) * dot(rows, block, ((1,), (1,)))
+        held[1, top] = 0.9 * right_ref[0, top] + (0.1 / extent) * dot(turned, block, ((0,), (0,)))
+        rows, turned = block[extent // 2 :], block[:, extent // 2 :]
+        held[0, low, low] = 0.9 * left_ref[0, low, low] + (0.1 / extent) * dot(rows, rows, ((1,), (1,)))
+        held[1, low, low] = 0.9 * right_ref[0, low, low] + (0.1 / extent) * dot(turned, turned, ((0,), (0,)))
+        held[0, low, top] = held[0, top, low].T
+        held[1, low, top] = held[1, top, low].T
+
+    stores = [pltpu.make_async_copy(held.at[k], outs[k].at[slot], sems.at[k]) for k in (0, 1)]
+    for store in stores:
+        store.start()
+
+    @pl.when(alive)
+    def _():
+        block = block_ref[:, 0].reshape(extent, extent)
+        (f_left, f_right), (c_left, c_right) = roots([held[0], held[1]])
         half = EYE_PART * block.astype(jnp.float32) + dot(block, f_right)
         result = (EYE_PART * half + dot(f_left, half)) * (c_left * c_right)
         update_ref[:, 0] = result.astype(jnp.bfloat16).reshape(update_ref.shape[0], update_ref.shape[2], extent)
+
+    for store in stores:
+        store.wait()
 
 
 def slot_step(count, received, left, right):
     owners, slots, rows, extent = received.shape
     spread = pl.BlockSpec((owners, 1, rows, extent), lambda s, count: (0, s, 0, 0))
     whole = pl.BlockSpec((1, extent, extent), lambda s, count: (s, 0, 0))
+    anywhere = pl.BlockSpec(memory_space=pl.ANY)
     return pl.pallas_call(
         slot_kernel,
         grid_spec=pltpu.PrefetchScalarGridSpec(
             num_scalar_prefetch=1,
             grid=(slots,),
             in_specs=[spread, whole, whole],
-            out_specs=[whole, whole, spread],
+            out_specs=[anywhere, anywhere, spread],
+            scratch_shapes=[pltpu.VMEM((2, extent, extent), jnp.float32), pltpu.SemaphoreType.DMA((2,))],
         ),
         out_shape=[
             jax.ShapeDtypeStruct(left.shape, jnp.float32),
             jax.ShapeDtypeStruct(right.shape, jnp.float32),
             jax.ShapeDtypeStruct(received.shape, jnp.bfloat16),
         ],
-        compiler_params=pltpu.CompilerParams(vmem_limit_bytes=VMEM),
+        compiler_params=pltpu.CompilerParams(vmem_limit_bytes=47 * 1024 * 1024),
         cost_estimate=pl.CostEstimate(
             flops=slots * 18 * 2 * extent**3,
             bytes_accessed=4 * left.size * 4 + 2 * received.size * 2,
@@ -232,9 +272,24 @@
     return local_call(second_kernel, pos, specs, [view] * 2 + list(others) + list(arrived), [whole] * 2, out)
 
 
+def rest_kernel(pos, *refs):
+    views, others, direct, outs = refs[:2], refs[2:4], refs[4:6], refs[6:]
+    for part in (0, 1):
+        outs[part][...] = add_up(views[part], part, [others[part][0], direct[part][0]])
+
+
+def rest_sums(view, pos, half, others, direct):
+    shape = (SETS[half], RING, *view.shape[-2:])
+    tail = pl.BlockSpec((1, *shape), lambda i, pos: (1, 0, 0, 0, 0))
+    whole = pl.BlockSpec(shape, lambda i, pos: (0, 0, 0, 0))
+    out = [jax.ShapeDtypeStruct(shape, jnp.float32)] * 2
+    specs = cut_specs(view.shape, 0, half) + [tail] * 4
+    return local_call(rest_kernel, pos, specs, [view] * 2 + [*others, *direct], [whole] * 2, out)
+
+
 def last_kernel(pos, *refs):
-    views, others, direct, joined = refs[:2], refs[2:4], refs[4:6], refs[6:8]
-    filled, outs, scratch = refs[8:-7], refs[-7:-1], refs[-1]
+    rest, joined = refs[:2], refs[2:4]
+    filled, outs, scratch = refs[4:-7], refs[-7:-1], refs[-1]
     size = scratch.shape[0]
     start = outs[1].shape[0] - size
     for earlier, out_ref in zip(filled, outs):
@@ -244,7 +299,7 @@
             out_ref[pl.ds(0, start)] = earlier[...]
     for part in (0, 1):
         ahead_ref, later_ref, own_ref = outs[3 * part : 3 * part + 3]
-        scratch[...] = add_up(views[part], part, [others[part][0], direct[part][0], joined[part][...]])
+        scratch[...] = rest[part][...] + joined[part][...].astype(jnp.float32)
         place, core = pos[part], pos[2]
         here = pl.ds(start, size)
         for k, which in enumerate((3, 1)):
@@ -253,11 +308,10 @@
         own_ref[here] = scratch[:, place]
 
 
-def last_sums(view, pos, half, others, direct, joined, filled):
+def last_sums(view, pos, half, rest, joined, filled):
     rows, extent = view.shape[-2:]
     shape = (SETS[half], RING, rows, extent)
     so_far = sum(SETS[: half + 1])
-    tail = pl.BlockSpec((1, *shape), lambda i, pos: (1, 0, 0, 0, 0))
     whole = pl.BlockSpec(shape, lambda i, pos: (0, 0, 0, 0))
 
     def pieces(count):
@@ -268,8 +322,8 @@
     return local_call(
         last_kernel,
         pos,
-        cut_specs(view.shape, 0, half) + [tail, tail, tail, tail, whole, whole] + pieces(sum(SETS[:half]))[: len(filled)],
-        [view] * 2 + [*others, *direct, *joined, *filled],
+        [whole] * 4 + pieces(sum(SETS[:half]))[: len(filled)],
+        [*rest, *joined, *filled],
         pieces(so_far),
         [
             jax.ShapeDtypeStruct((2, so_far, rows, extent), jnp.bfloat16),
@@ -307,10 +361,14 @@
     joined, terms, pieces = [], [], []
     for half in halves:
         sums = second_sums(left, pos, half, late[half], direct[half])
+        if half + 1 < len(SETS):
+            count = len(sums)
+            both = lax.optimization_barrier((*sums, *direct[half + 1]))
+            sums, direct[half + 1] = both[:count], both[count:]
         joined.append([exchange(v, 1 - part, 1) for part, v in zip(parts, sums)])
+    rest = [rest_sums(left, pos, half, late[half], direct[half]) for half in halves]
     for half in halves:
-        pieces = last_sums(left, pos, half, late[half], direct[half], joined[half], pieces)
-        left, *pieces = lax.optimization_barrier((left, *pieces))
+        pieces = last_sums(left, pos, half, rest[half], joined[half], pieces)
     for part in parts:
         ahead, later, own = pieces[3 * part : 3 * part + 3]
         arrived = exchange(ahead, part, 0)

time: 164 us -> 156 us (0.951)
  starting transfers between devices: 52.8 us -> 42.8 us
  Pallas kernels: 29 us -> 30.9 us
    ppermute x12, starting transfers between devices: 24.4 us -> 16.4 us  [exchange(): return lax.ppermute(value, 'dp', pairs)]
    all_to_all x1, starting transfers between devices: 15.2 us -> 9.84 us  [per_device(): lax.all_to_all(updates, 'dp', split_axis=0, concat_axis=0, tiled=True)]
    ppermute x5, starting transfers between devices: 3.57 us -> 5.89 us  [send_group(): return lax.ppermute(value, ('dp', 'mp'), pairs)]
    ppermute x5, waiting for transfers between devices: 17.1 us -> 14.8 us  [send_group(): return lax.ppermute(value, ('dp', 'mp'), pairs)]
    ppermute x12, waiting for transfers between devices: 23 us -> 25.2 us  [exchange(): return lax.ppermute(value, 'dp', pairs)]
    pallas_call x11 -> x13, Pallas kernels: 25.8 us -> 26.4 us  [local_call(): pl.pallas_call(body, grid_spec=pltpu.PrefetchScalarGridSpec(num_scalar_pr...]
  transfers between devices with their start and end apart: 27 -> 27, of which waited for: 12 -> 16; matrix products, arithmetic and copies ran while one was open for 2% -> 2% of each run, Pallas kernels for 11% -> 13%
where the time goes in v3:
time: 156 us; the launch traced here: 155 us
  waiting for transfers between devices  73.9 us (47%)
  starting transfers between devices  42.8 us (27%)
  Pallas kernels  30.9 us (20%)
  local copies, waits for them, and re-layouts  5.94 us (4%)
    pallas_call x13, Pallas kernels, local_call(): pl.pallas_call(body, grid_spec=pltpu.PrefetchScalarGridSpec(num_scalar_pr...  26.4 us
    ppermute x12, waiting for transfers between devices, exchange(): return lax.ppermute(value, 'dp', pairs)  25.2 us
    all_to_all x1, waiting for transfers between devices, per_device(): lax.all_to_all(updates, 'dp', split_axis=0, concat_axis=0, tiled=True)  16.5 us
    ppermute x12, starting transfers between devices, exchange(): return lax.ppermute(value, 'dp', pairs)  16.4 us
    all_to_all x1, waiting for transfers between devices, per_device(): lax.all_to_all(outgoing, 'dp', split_axis=0, concat_axis=0, tiled=True)  15.8 us
    ppermute x5, waiting for transfers between devices, send_group(): return lax.ppermute(value, ('dp', 'mp'), pairs)  14.8 us
    all_to_all x1, starting transfers between devices, per_device(): lax.all_to_all(updates, 'dp', split_axis=0, concat_axis=0, tiled=True)  9.84 us
    ppermute x8, starting transfers between devices, swap(): lax.ppermute(value, 'dp', [(flat(z, y, core), flat(z, y, 1 - core)) for z...  6.48 us
  transfers between devices with their start and end apart: 27, of which 16 were waited for; matrix products, arithmetic and copies ran while one was open for 2% of the time, Pallas kernels for 13%

profile of v3, /device:TPU:0, one launch (start us, length us, event | category | flops | bytes accessed | tf_op | source)
XLA Modules:
  0.0 155.0 jit_solution(12100130694527079566)
XLA Ops:
  0.7 0.1 pad_add_fusion.pos
  0.8 2.4 %shard_map.85 = (bf16[2,10,4,16,512]{4,3,2,1,0:T(8,128)(2,1)S(1)}, bf16[2,10,4,16,512]{4,3,2,1,0:T(8,128)(2,1)S(1)}) custom-call(s32[3]{0:T(128)S(1)} %pad_add_fusion.pos, bf16[28,4,4,2,16,512]{5,4,3,2,1,0:T(8,128)(2,1)} %bitcast.53, bf16[28,4,4,2,16,512]{5,4,3,2,1,0:T(8,128)(2,1)} %bitcast.54, bf16[28,4,4,2,16,512]{5,4,3,2,1,0:T(8,128)(2,1)} %bitcast.55, ...), custom_call_target="tpu_custom_call" | custom-call | flops 5242880 | bytes 10485760 | tf_op jit(solution)/shard_map/pallas_call | solution.py:203
  3.2 0.1 collective-permute-start
  3.3 0.5 collective-permute-start.1
  3.8 1.8 %shard_map.86 = (bf16[2,4,4,16,512]{4,3,2,1,0:T(8,128)(2,1)S(1)}, bf16[2,4,4,16,512]{4,3,2,1,0:T(8,128)(2,1)S(1)}) custom-call(s32[3]{0:T(128)S(1)} %pad_add_fusion.pos, bf16[28,4,4,2,16,512]{5,4,3,2,1,0:T(8,128)(2,1)} %bitcast.57, bf16[28,4,4,2,16,512]{5,4,3,2,1,0:T(8,128)(2,1)} %bitcast.58, bf16[28,4,4,2,16,512]{5,4,3,2,1,0:T(8,128)(2,1)} %bitcast.59, ...), custom_call_target="tpu_custom_call" | custom-call | flops 2097152 | bytes 4194304 | tf_op jit(solution)/shard_map/pallas_call | solution.py:203
  5.6 2.4 %shard_map.87 = (bf16[2,10,4,16,512]{4,3,2,1,0:T(8,128)(2,1)S(1)}, bf16[2,10,4,16,512]{4,3,2,1,0:T(8,128)(2,1)S(1)}) custom-call(s32[3]{0:T(128)S(1)} %pad_add_fusion.pos, bf16[28,4,4,2,16,512]{5,4,3,2,1,0:T(8,128)(2,1)} %bitcast.61, bf16[28,4,4,2,16,512]{5,4,3,2,1,0:T(8,128)(2,1)} %bitcast.62, bf16[28,4,4,2,16,512]{5,4,3,2,1,0:T(8,128)(2,1)} %bitcast.63, ...), custom_call_target="tpu_custom_call" | custom-call | flops 5242880 | bytes 10485760 | tf_op jit(solution)/shard_map/pallas_call | solution.py:203
  8.0 0.2 collective-permute-start.6
  8.2 0.4 collective-permute-start.2
  8.6 0.1 collective-permute-start.7
  8.7 2.9 %shard_map.88 = (bf16[2,10,4,16,512]{4,3,2,1,0:T(8,128)(2,1)S(1)}, bf16[2,10,4,16,512]{4,3,2,1,0:T(8,128)(2,1)S(1)}) custom-call(s32[3]{0:T(128)S(1)} %pad_add_fusion.pos, bf16[28,4,4,2,16,512]{5,4,3,2,1,0:T(8,128)(2,1)} %bitcast.68, bf16[28,4,4,2,16,512]{5,4,3,2,1,0:T(8,128)(2,1)} %bitcast.66, bf16[28,4,4,2,16,512]{5,4,3,2,1,0:T(8,128)(2,1)} %bitcast.67, ...), custom_call_target="tpu_custom_call" | custom-call | flops 5242880 | bytes 10485760 | tf_op jit(solution)/shard_map/pallas_call | solution.py:203
  11.7 1.7 %collective-permute-start.8 = (bf16[2,10,4,16,512]{4,3,2,1,0:T(8,128)(2,1)S(1)}, bf16[2,10,4,16,512]{4,3,2,1,0:T(8,128)(2,1)S(1)}, u32[]{:S(2)}, u32[]{:S(2)}) collective-permute-start(bf16[2,10,4,16,512]{4,3,2,1,0:T(8,128)(2,1)S(1)} %get-tuple-element.86), channel_id=1, source_target_pairs={{0,8},{4,28},{8,0},{12,20},{16,24},{20,12},{24,16},{28,4},{32,40},... | collective-permute-start | bytes 3932168 | tf_op jit(solution)/shard_map/ppermute | solution.py:174
  13.4 1.9 %collective-permute-start.9 = (bf16[2,10,4,16,512]{4,3,2,1,0:T(8,128)(2,1)S(1)}, bf16[2,10,4,16,512]{4,3,2,1,0:T(8,128)(2,1)S(1)}, u32[]{:S(2)}, u32[]{:S(2)}) collective-permute-start(bf16[2,10,4,16,512]{4,3,2,1,0:T(8,128)(2,1)S(1)} %get-tuple-element.87), channel_id=1, source_target_pairs={{0,32},{4,100},{8,40},{12,108},{16,48},{20,116},{24,56},{28,124},{... | collective-permute-start | bytes 3932168 | tf_op jit(solution)/shard_map/ppermute | solution.py:174
  15.3 3.4 %collective-permute-start.3 = (bf16[2,4,4,16,512]{4,3,2,1,0:T(8,128)(2,1)S(1)}, bf16[2,4,4,16,512]{4,3,2,1,0:T(8,128)(2,1)S(1)}, u32[]{:S(2)}, u32[]{:S(2)}) collective-permute-start(bf16[2,4,4,16,512]{4,3,2,1,0:T(8,128)(2,1)S(1)} %get-tuple-element.75), channel_id=1, source_target_pairs={{0,4},{4,0},{8,12},{12,8},{16,20},{20,16},{24,28},{28,24},{32,36},... | collective-permute-start | bytes 1572872 | tf_op jit(solution)/shard_map/ppermute | solution.py:178
  18.7 1.5 collective-permute-done.3.refs_5_
  20.3 2.0 %shard_map.89 = (bf16[2,4,4,16,512]{4,3,2,1,0:T(8,128)(2,1)S(1)}, bf16[2,4,4,16,512]{4,3,2,1,0:T(8,128)(2,1)S(1)}) custom-call(s32[3]{0:T(128)S(1)} %pad_add_fusion.pos, bf16[28,4,4,2,16,512]{5,4,3,2,1,0:T(8,128)(2,1)} %bitcast.69, bf16[28,4,4,2,16,512]{5,4,3,2,1,0:T(8,128)(2,1)} %bitcast.70, bf16[28,4,4,2,16,512]{5,4,3,2,1,0:T(8,128)(2,1)} %bitcast.71, ...), custom_call_target="tpu_custom_call" | custom-call | flops 2097152 | bytes 4194304 | tf_op jit(solution)/shard_map/pallas_call | solution.py:203
  22.3 0.2 collective-permute-start.10
  22.5 1.8 %shard_map.90 = (bf16[2,4,4,16,512]{4,3,2,1,0:T(8,128)(2,1)S(1)}, bf16[2,4,4,16,512]{4,3,2,1,0:T(8,128)(2,1)S(1)}) custom-call(s32[3]{0:T(128)S(1)} %pad_add_fusion.pos, bf16[28,4,4,2,16,512]{5,4,3,2,1,0:T(8,128)(2,1)} %bitcast.73, bf16[28,4,4,2,16,512]{5,4,3,2,1,0:T(8,128)(2,1)} %bitcast.74, bf16[28,4,4,2,16,512]{5,4,3,2,1,0:T(8,128)(2,1)} %bitcast.75, ...), custom_call_target="tpu_custom_call" | custom-call | flops 2097152 | bytes 4194304 | tf_op jit(solution)/shard_map/pallas_call | solution.py:203
  24.4 1.2 collective-permute-start.4
  25.5 3.8 %collective-permute-done.8.refs_4_ = bf16[2,10,4,16,512]{4,3,2,1,0:T(8,128)(2,1)S(1)} collective-permute-done((bf16[2,10,4,16,512]{4,3,2,1,0:T(8,128)(2,1)S(1)}, bf16[2,10,4,16,512]{4,3,2,1,0:T(8,128)(2,1)S(1)}, u32[]{:S(2)}, u32[]{:S(2)}) %collective-permute-start.8) | collective-permute-done | bytes 1310752 | tf_op jit(solution)/shard_map/ppermute | solution.py:174
  29.3 0.6 collective-permute-start.5
  30.0 1.0 collective-permute-done.9.refs_5_
  31.0 2.4 %shard_map.91 = (bf16[10,4,16,512]{3,2,1,0:T(8,128)(2,1)S(1)}, bf16[10,4,16,512]{3,2,1,0:T(8,128)(2,1)S(1)}) custom-call(s32[3]{0:T(128)S(1)} %pad_add_fusion.pos, bf16[28,4,4,2,16,512]{5,4,3,2,1,0:T(8,128)(2,1)} %bitcast.77, bf16[28,4,4,2,16,512]{5,4,3,2,1,0:T(8,128)(2,1)} %bitcast.78, bf16[2,10,4,16,512]{4,3,2,1,0:T(8,128)(2,1)S(1)} %collective-permute-done.6.refs_2_, ...), custom_call_target="tpu_custom_call" | custom-call | flops 2621440 | bytes 5242880 | tf_op jit(solution)/shard_map/pallas_call | solution.py:203
  33.4 1.6 %collective-permute-done.10.refs_4_ = bf16[2,4,4,16,512]{4,3,2,1,0:T(8,128)(2,1)S(1)} collective-permute-done((bf16[2,4,4,16,512]{4,3,2,1,0:T(8,128)(2,1)S(1)}, bf16[2,4,4,16,512]{4,3,2,1,0:T(8,128)(2,1)S(1)}, u32[]{:S(2)}, u32[]{:S(2)}) %collective-permute-start.10) | collective-permute-done | bytes 524320 | tf_op jit(solution)/shard_map/ppermute | solution.py:174
  35.0 1.7 %collective-permute-done.11.refs_5_ = bf16[2,4,4,16,512]{4,3,2,1,0:T(8,128)(2,1)S(1)} collective-permute-done((bf16[2,4,4,16,512]{4,3,2,1,0:T(8,128)(2,1)S(1)}, bf16[2,4,4,16,512]{4,3,2,1,0:T(8,128)(2,1)S(1)}, u32[]{:S(2)}, u32[]{:S(2)}) %collective-permute-start.11) | collective-permute-done | bytes 524320 | tf_op jit(solution)/shard_map/ppermute | solution.py:174
  36.6 2.2 %collective-permute-start.14 = (bf16[10,4,16,512]{3,2,1,0:T(8,128)(2,1)S(1)}, bf16[10,4,16,512]{3,2,1,0:T(8,128)(2,1)S(1)}, u32[]{:S(2)}, u32[]{:S(2)}) collective-permute-start(bf16[10,4,16,512]{3,2,1,0:T(8,128)(2,1)S(1)} %get-tuple-element.100), channel_id=1, source_target_pairs={{0,24},{4,12},{8,16},{12,4},{16,8},{20,28},{24,0},{28,20},{32,56},... | collective-permute-start | bytes 1966088 | tf_op jit(solution)/shard_map/ppermute | solution.py:174
  38.8 4.0 %collective-permute-start.15 = (bf16[10,4,16,512]{3,2,1,0:T(8,128)(2,1)S(1)}, bf16[10,4,16,512]{3,2,1,0:T(8,128)(2,1)S(1)}, u32[]{:S(2)}, u32[]{:S(2)}) collective-permute-start(bf16[10,4,16,512]{3,2,1,0:T(8,128)(2,1)S(1)} %get-tuple-element.101), channel_id=1, source_target_pairs={{0,96},{4,36},{8,104},{12,44},{16,112},{20,52},{24,120},{28,60},{3... | collective-permute-start | bytes 1966088 | tf_op jit(solution)/shard_map/ppermute | solution.py:174
  42.8 1.8 %shard_map.93 = (bf16[4,4,16,512]{3,2,1,0:T(8,128)(2,1)S(1)}, bf16[4,4,16,512]{3,2,1,0:T(8,128)(2,1)S(1)}) custom-call(s32[3]{0:T(128)S(1)} %pad_add_fusion.pos, bf16[28,4,4,2,16,512]{5,4,3,2,1,0:T(8,128)(2,1)} %bitcast.79, bf16[28,4,4,2,16,512]{5,4,3,2,1,0:T(8,128)(2,1)} %bitcast.80, bf16[2,4,4,16,512]{4,3,2,1,0:T(8,128)(2,1)S(1)} %collective-permute-done.4.refs_2_, ...), custom_call_target="tpu_custom_call" | custom-call | flops 1048576 | bytes 2097152 | tf_op jit(solution)/shard_map/pallas_call | solution.py:203
  44.6 1.1 collective-permute-start.12
  45.8 1.8 %shard_map.92 = (f32[4,4,16,512]{3,2,1,0:T(8,128)S(1)}, f32[4,4,16,512]{3,2,1,0:T(8,128)S(1)}) custom-call(s32[3]{0:T(128)S(1)} %pad_add_fusion.pos, bf16[28,4,4,2,16,512]{5,4,3,2,1,0:T(8,128)(2,1)} %bitcast.81, bf16[28,4,4,2,16,512]{5,4,3,2,1,0:T(8,128)(2,1)} %bitcast.82, bf16[2,4,4,16,512]{4,3,2,1,0:T(8,128)(2,1)S(1)} %collective-permute-done.4.refs_2_, ...), custom_call_target="tpu_custom_call" | custom-call | flops 1048576 | bytes 2097152 | tf_op jit(solution)/shard_map/pallas_call | solution.py:203
  47.5 2.5 %shard_map.94 = (f32[10,4,16,512]{3,2,1,0:T(8,128)S(1)}, f32[10,4,16,512]{3,2,1,0:T(8,128)S(1)}) custom-call(s32[3]{0:T(128)S(1)} %pad_add_fusion.pos, bf16[28,4,4,2,16,512]{5,4,3,2,1,0:T(8,128)(2,1)} %bitcast.83, bf16[28,4,4,2,16,512]{5,4,3,2,1,0:T(8,128)(2,1)} %bitcast.84, bf16[2,10,4,16,512]{4,3,2,1,0:T(8,128)(2,1)S(1)} %collective-permute-done.6.refs_2_, ...), custom_call_target="tpu_custom_call" | custom-call | flops 2621440 | bytes 5242880 | tf_op jit(solution)/shard_map/pallas_call | solution.py:203
  50.0 1.4 collective-permute-done.15.refs_3_
  51.4 1.0 shard_map.95
  52.4 1.8 %collective-permute-done.13.refs_3_ = bf16[4,4,16,512]{3,2,1,0:T(8,128)(2,1)S(1)} collective-permute-done((bf16[4,4,16,512]{3,2,1,0:T(8,128)(2,1)S(1)}, bf16[4,4,16,512]{3,2,1,0:T(8,128)(2,1)S(1)}, u32[]{:S(2)}, u32[]{:S(2)}) %collective-permute-start.13) | collective-permute-done | bytes 262176 | tf_op jit(solution)/shard_map/ppermute | solution.py:174
  54.2 1.5 shard_map.96
  55.8 0.7 collective-permute-start.18
  56.4 8.0 %collective-permute-done.16.refs_1_ = bf16[2,14,16,512]{3,2,1,0:T(8,128)(2,1)S(1)} collective-permute-done((bf16[2,14,16,512]{3,2,1,0:T(8,128)(2,1)}, bf16[2,14,16,512]{3,2,1,0:T(8,128)(2,1)S(1)}, u32[]{:S(2)}, u32[]{:S(2)}) %collective-permute-start.16) | collective-permute-done | bytes 458784 | tf_op jit(solution)/shard_map/ppermute | solution.py:174
  64.4 0.1 fusion.1
  64.5 3.3 %collective-permute-start.17 = (bf16[14,16,512]{2,1,0:T(8,128)(2,1)S(1)}, bf16[14,16,512]{2,1,0:T(8,128)(2,1)S(1)}, u32[]{:S(2)}, u32[]{:S(2)}) collective-permute-start(bf16[14,16,512]{2,1,0:T(8,128)(2,1)S(1)} %fusion.1), channel_id=1, source_target_pairs={{0,96},{4,36},{8,104},{12,44},{16,112},{20,52},{24,120},{28,60},{3... | collective-permute-start | bytes 688136 | tf_op jit(solution)/shard_map/ppermute | solution.py:174
  67.8 0.1 fusion
  67.9 1.1 collective-permute-start.19
  69.0 0.1 add_minimum_fusion
  69.1 0.1 min.12.wanted
  69.2 2.6 %collective-permute-done.17.refs_2_ = bf16[14,16,512]{2,1,0:T(8,128)(2,1)S(1)} collective-permute-done((bf16[14,16,512]{2,1,0:T(8,128)(2,1)S(1)}, bf16[14,16,512]{2,1,0:T(8,128)(2,1)S(1)}, u32[]{:S(2)}, u32[]{:S(2)}) %collective-permute-start.17) | collective-permute-done | bytes 229408 | tf_op jit(solution)/shard_map/ppermute | solution.py:174
  71.8 3.4 %collective-permute-done.19.refs_5_ = bf16[14,16,512]{2,1,0:T(8,128)(2,1)S(1)} collective-permute-done((bf16[14,16,512]{2,1,0:T(8,128)(2,1)S(1)}, bf16[14,16,512]{2,1,0:T(8,128)(2,1)S(1)}, u32[]{:S(2)}, u32[]{:S(2)}) %collective-permute-start.19) | collective-permute-done | bytes 229408 | tf_op jit(solution)/shard_map/ppermute | solution.py:174
  75.2 2.0 %shard_map.97 = bf16[64,16,512]{2,1,0:T(8,128)(2,1)} custom-call(s32[64]{0:T(128)S(1)} %min.12.wanted, f32[14,16,512]{2,1,0:T(8,128)S(1)} %get-tuple-element.108.refs_0_, bf16[2,14,16,512]{3,2,1,0:T(8,128)(2,1)S(1)} %collective-permute-done.16.refs_1_, bf16[14,16,512]{2,1,0:T(8,128)(2,1)S(1)} %collective-permute-done.17.refs_2_, ...), custom_call_target="tpu_custom_call" | custom-call | flops 2097152 | bytes 4194304 | tf_op jit(solution)/shard_map/pallas_call | solution.py:203
  77.2 4.2 %all-to-all-start = ((bf16[32,2,16,512]{3,2,1,0:T(8,128)(2,1)}), bf16[32,2,16,512]{3,2,1,0:T(8,128)(2,1)S(1)}, u32[]{:S(2)}, u32[]{:S(2)}) async-start(bf16[32,2,16,512]{3,2,1,0:T(8,128)(2,1)} %bitcast.8), calls=%async_computation | async-start | bytes 2097152 | tf_op jit(solution)/shard_map/all_to_all | solution.py:458
  81.5 1.3 dynamic_slice.14
  82.8 15.8 %all-to-all-done.block_ref = bf16[32,2,16,512]{3,2,1,0:T(8,128)(2,1)S(1)} async-done(((bf16[32,2,16,512]{3,2,1,0:T(8,128)(2,1)}), bf16[32,2,16,512]{3,2,1,0:T(8,128)(2,1)S(1)}, u32[]{:S(2)}, u32[]{:S(2)}) %all-to-all-start) | async-done | bytes 1048608 | tf_op jit(solution)/shard_map/all_to_all | solution.py:458
  98.7 1.6 %copy-done.3 = f32[1,2,512,512]{3,2,1,0:T(8,128)S(1)} copy-done((f32[1,2,512,512]{3,2,1,0:T(8,128)S(1)}, f32[1,2,512,512]{3,2,1,0:T(8,128)}, u32[]{:S(2)}) %copy-start.3) | copy-done | bytes 2097176
  100.3 4.5 %shard_map.98 = (f32[2,512,512]{2,1,0:T(8,128)}, f32[2,512,512]{2,1,0:T(8,128)}, bf16[32,2,16,512]{3,2,1,0:T(8,128)(2,1)}) custom-call(s32[1]{0:T(128)} %bitcast.count_ref, bf16[32,2,16,512]{3,2,1,0:T(8,128)(2,1)S(1)} %all-to-all-done.block_ref, f32[2,512,512]{2,1,0:T(8,128)S(1)} %bitcast.51, f32[2,512,512]{2,1,0:T(8,128)S(1)} %bitcast.52), custom_call_target="tpu_custom_call" | custom-call | flops 9663676416 | bytes 10485760 | tf_op jit(solution)/shard_map/pallas_call | solution.py:122
  104.8 9.8 %all-to-all-start.1 = ((bf16[32,2,16,512]{3,2,1,0:T(8,128)(2,1)}), bf16[32,2,16,512]{3,2,1,0:T(8,128)(2,1)S(1)}, u32[]{:S(2)}, u32[]{:S(2)}) async-start(bf16[32,2,16,512]{3,2,1,0:T(8,128)(2,1)} %get-tuple-element.116), calls=%async_computation.1 | async-start | bytes 2097152 | tf_op jit(solution)/shard_map/all_to_all | solution.py:461
  114.8 0.7 gather_fusion
  115.5 16.5 %all-to-all-done.1 = bf16[32,2,16,512]{3,2,1,0:T(8,128)(2,1)S(1)} async-done(((bf16[32,2,16,512]{3,2,1,0:T(8,128)(2,1)}), bf16[32,2,16,512]{3,2,1,0:T(8,128)(2,1)S(1)}, u32[]{:S(2)}, u32[]{:S(2)}) %all-to-all-start.1) | async-done | bytes 1048608 | tf_op jit(solution)/shard_map/all_to_all | solution.py:461
  132.0 0.6 gather_fusion.1
  132.6 1.7 %collective-permute-start.24 = (bf16[28,16,512]{2,1,0:T(8,128)(2,1)S(1)}, bf16[28,16,512]{2,1,0:T(8,128)(2,1)S(1)}, u32[]{:S(2)}, u32[]{:S(2)}) collective-permute-start(bf16[28,16,512]{2,1,0:T(8,128)(2,1)S(1)} %gather_fusion.1), channel_id=1, source_target_pairs={{0,3},{1,0},{2,1},{3,2},{4,5},{5,6},{6,7},{7,4},{8,11},{9,8},{10,9... | collective-permute-start | bytes 1376264 | tf_op jit(solution)/shard_map/ppermute | solution.py:423
  134.3 1.0 collective-permute-start.20
  135.3 1.9 %collective-permute-start.21 = (bf16[14,16,512]{2,1,0:T(8,128)(2,1)S(1)}, bf16[14,16,512]{2,1,0:T(8,128)(2,1)S(1)}, u32[]{:S(2)}, u32[]{:S(2)}) collective-permute-start(bf16[14,16,512]{2,1,0:T(8,128)(2,1)S(1)} %get-tuple-element.117), channel_id=1, source_target_pairs={{0,1},{1,2},{2,3},{3,0},{4,7},{5,4},{6,5},{7,6},{8,9},{9,10},{10,1... | collective-permute-start | bytes 688136 | tf_op jit(solution)/shard_map/ppermute | solution.py:423
  137.2 0.2 broadcast_in_dim.33
  137.5 6.5 %collective-permute-done.20 = bf16[14,16,512]{2,1,0:T(8,128)(2,1)S(1)} collective-permute-done((bf16[14,16,512]{2,1,0:T(8,128)(2,1)S(1)}, bf16[14,16,512]{2,1,0:T(8,128)(2,1)S(1)}, u32[]{:S(2)}, u32[]{:S(2)}) %collective-permute-start.20) | collective-permute-done | bytes 229408 | tf_op jit(solution)/shard_map/ppermute | solution.py:423
  144.0 2.5 %collective-permute-done.21 = bf16[14,16,512]{2,1,0:T(8,128)(2,1)S(1)} collective-permute-done((bf16[14,16,512]{2,1,0:T(8,128)(2,1)S(1)}, bf16[14,16,512]{2,1,0:T(8,128)(2,1)S(1)}, u32[]{:S(2)}, u32[]{:S(2)}) %collective-permute-start.21) | collective-permute-done | bytes 229408 | tf_op jit(solution)/shard_map/ppermute | solution.py:423
  146.4 1.3 collective-permute-start.23
  147.8 3.4 %collective-permute-done.22 = bf16[14,16,512]{2,1,0:T(8,128)(2,1)S(1)} collective-permute-done((bf16[14,16,512]{2,1,0:T(8,128)(2,1)S(1)}, bf16[14,16,512]{2,1,0:T(8,128)(2,1)S(1)}, u32[]{:S(2)}, u32[]{:S(2)}) %collective-permute-start.22) | collective-permute-done | bytes 229408 | tf_op jit(solution)/shard_map/ppermute | solution.py:423
  151.2 2.4 %collective-permute-done.23 = bf16[14,16,512]{2,1,0:T(8,128)(2,1)S(1)} collective-permute-done((bf16[14,16,512]{2,1,0:T(8,128)(2,1)S(1)}, bf16[14,16,512]{2,1,0:T(8,128)(2,1)S(1)}, u32[]{:S(2)}, u32[]{:S(2)}) %collective-permute-start.23) | collective-permute-done | bytes 229408 | tf_op jit(solution)/shard_map/ppermute | solution.py:423
  153.8 1.2 copy-done.4
  (37 shorter events, 0.3 us)
Async XLA Ops:
  0.6 68.4 %copy-start = (s32[4,32]{1,0:T(4,128)S(1)}, s32[4,32]{1,0:T(4,128)}, u32[]{:S(2)}) copy-start(s32[4,32]{1,0:T(4,128)} %param.11) | copy-start | bytes 1540
  3.2 5.5 %collective-permute-start = (bf16[2,10,4,16,512]{4,3,2,1,0:T(8,128)(2,1)S(1)}, bf16[2,10,4,16,512]{4,3,2,1,0:T(8,128)(2,1)S(1)}, u32[]{:S(2)}, u32[]{:S(2)}) collective-permute-start(bf16[2,10,4,16,512]{4,3,2,1,0:T(8,128)(2,1)S(1)} %get-tuple-element.69), channel_id=1, source_target_pairs={{0,4},{4,0},{8,12},{12,8},{16,20},{20,16},{24,28},{28,24},{32,36},... | collective-permute-start | bytes 3932168 | tf_op jit(solution)/shard_map/ppermute | solution.py:178
  3.3 5.4 %collective-permute-start.1 = (bf16[2,10,4,16,512]{4,3,2,1,0:T(8,128)(2,1)S(1)}, bf16[2,10,4,16,512]{4,3,2,1,0:T(8,128)(2,1)S(1)}, u32[]{:S(2)}, u32[]{:S(2)}) collective-permute-start(bf16[2,10,4,16,512]{4,3,2,1,0:T(8,128)(2,1)S(1)} %get-tuple-element.70), channel_id=1, source_target_pairs={{0,4},{4,0},{8,12},{12,8},{16,20},{20,16},{24,28},{28,24},{32,36},... | collective-permute-start | bytes 3932168 | tf_op jit(solution)/shard_map/ppermute | solution.py:178
  8.0 14.5 %collective-permute-start.6 = (bf16[2,10,4,16,512]{4,3,2,1,0:T(8,128)(2,1)S(1)}, bf16[2,10,4,16,512]{4,3,2,1,0:T(8,128)(2,1)S(1)}, u32[]{:S(2)}, u32[]{:S(2)}) collective-permute-start(bf16[2,10,4,16,512]{4,3,2,1,0:T(8,128)(2,1)S(1)} %get-tuple-element.84), channel_id=1, source_target_pairs={{0,4},{4,0},{8,12},{12,8},{16,20},{20,16},{24,28},{28,24},{32,36},... | collective-permute-start | bytes 3932168 | tf_op jit(solution)/shard_map/ppermute | solution.py:178
  8.2 7.1 %collective-permute-start.2 = (bf16[2,4,4,16,512]{4,3,2,1,0:T(8,128)(2,1)S(1)}, bf16[2,4,4,16,512]{4,3,2,1,0:T(8,128)(2,1)S(1)}, u32[]{:S(2)}, u32[]{:S(2)}) collective-permute-start(bf16[2,4,4,16,512]{4,3,2,1,0:T(8,128)(2,1)S(1)} %get-tuple-element.74), channel_id=1, source_target_pairs={{0,4},{4,0},{8,12},{12,8},{16,20},{20,16},{24,28},{28,24},{32,36},... | collective-permute-start | bytes 1572872 | tf_op jit(solution)/shard_map/ppermute | solution.py:178
  8.6 15.7 %collective-permute-start.7 = (bf16[2,10,4,16,512]{4,3,2,1,0:T(8,128)(2,1)S(1)}, bf16[2,10,4,16,512]{4,3,2,1,0:T(8,128)(2,1)S(1)}, u32[]{:S(2)}, u32[]{:S(2)}) collective-permute-start(bf16[2,10,4,16,512]{4,3,2,1,0:T(8,128)(2,1)S(1)} %get-tuple-element.85), channel_id=1, source_target_pairs={{0,4},{4,0},{8,12},{12,8},{16,20},{20,16},{24,28},{28,24},{32,36},... | collective-permute-start | bytes 3932168 | tf_op jit(solution)/shard_map/ppermute | solution.py:178
  11.7 17.7 %collective-permute-start.8 = (bf16[2,10,4,16,512]{4,3,2,1,0:T(8,128)(2,1)S(1)}, bf16[2,10,4,16,512]{4,3,2,1,0:T(8,128)(2,1)S(1)}, u32[]{:S(2)}, u32[]{:S(2)}) collective-permute-start(bf16[2,10,4,16,512]{4,3,2,1,0:T(8,128)(2,1)S(1)} %get-tuple-element.86), channel_id=1, source_target_pairs={{0,8},{4,28},{8,0},{12,20},{16,24},{20,12},{24,16},{28,4},{32,40},... | collective-permute-start | bytes 3932168 | tf_op jit(solution)/shard_map/ppermute | solution.py:174
  13.4 17.6 %collective-permute-start.9 = (bf16[2,10,4,16,512]{4,3,2,1,0:T(8,128)(2,1)S(1)}, bf16[2,10,4,16,512]{4,3,2,1,0:T(8,128)(2,1)S(1)}, u32[]{:S(2)}, u32[]{:S(2)}) collective-permute-start(bf16[2,10,4,16,512]{4,3,2,1,0:T(8,128)(2,1)S(1)} %get-tuple-element.87), channel_id=1, source_target_pairs={{0,32},{4,100},{8,40},{12,108},{16,48},{20,116},{24,56},{28,124},{... | collective-permute-start | bytes 3932168 | tf_op jit(solution)/shard_map/ppermute | solution.py:174
  15.3 5.0 %collective-permute-start.3 = (bf16[2,4,4,16,512]{4,3,2,1,0:T(8,128)(2,1)S(1)}, bf16[2,4,4,16,512]{4,3,2,1,0:T(8,128)(2,1)S(1)}, u32[]{:S(2)}, u32[]{:S(2)}) collective-permute-start(bf16[2,4,4,16,512]{4,3,2,1,0:T(8,128)(2,1)S(1)} %get-tuple-element.75), channel_id=1, source_target_pairs={{0,4},{4,0},{8,12},{12,8},{16,20},{20,16},{24,28},{28,24},{32,36},... | collective-permute-start | bytes 1572872 | tf_op jit(solution)/shard_map/ppermute | solution.py:178
  22.3 12.7 %collective-permute-start.10 = (bf16[2,4,4,16,512]{4,3,2,1,0:T(8,128)(2,1)S(1)}, bf16[2,4,4,16,512]{4,3,2,1,0:T(8,128)(2,1)S(1)}, u32[]{:S(2)}, u32[]{:S(2)}) collective-permute-start(bf16[2,4,4,16,512]{4,3,2,1,0:T(8,128)(2,1)S(1)} %get-tuple-element.90), channel_id=1, source_target_pairs={{0,8},{4,28},{8,0},{12,20},{16,24},{20,12},{24,16},{28,4},{32,40},... | collective-permute-start | bytes 1572872 | tf_op jit(solution)/shard_map/ppermute | solution.py:174
  22.5 14.1 %collective-permute-start.11 = (bf16[2,4,4,16,512]{4,3,2,1,0:T(8,128)(2,1)S(1)}, bf16[2,4,4,16,512]{4,3,2,1,0:T(8,128)(2,1)S(1)}, u32[]{:S(2)}, u32[]{:S(2)}) collective-permute-start(bf16[2,4,4,16,512]{4,3,2,1,0:T(8,128)(2,1)S(1)} %get-tuple-element.91), channel_id=1, source_target_pairs={{0,32},{4,100},{8,40},{12,108},{16,48},{20,116},{24,56},{28,124},{... | collective-permute-start | bytes 1572872 | tf_op jit(solution)/shard_map/ppermute | solution.py:174
  24.4 18.5 %collective-permute-start.4 = (bf16[2,4,4,16,512]{4,3,2,1,0:T(8,128)(2,1)S(1)}, bf16[2,4,4,16,512]{4,3,2,1,0:T(8,128)(2,1)S(1)}, u32[]{:S(2)}, u32[]{:S(2)}) collective-permute-start(bf16[2,4,4,16,512]{4,3,2,1,0:T(8,128)(2,1)S(1)} %get-tuple-element.82), channel_id=1, source_target_pairs={{0,4},{4,0},{8,12},{12,8},{16,20},{20,16},{24,28},{28,24},{32,36},... | collective-permute-start | bytes 1572872 | tf_op jit(solution)/shard_map/ppermute | solution.py:178
  29.3 13.5 %collective-permute-start.5 = (bf16[2,4,4,16,512]{4,3,2,1,0:T(8,128)(2,1)S(1)}, bf16[2,4,4,16,512]{4,3,2,1,0:T(8,128)(2,1)S(1)}, u32[]{:S(2)}, u32[]{:S(2)}) collective-permute-start(bf16[2,4,4,16,512]{4,3,2,1,0:T(8,128)(2,1)S(1)} %get-tuple-element.83), channel_id=1, source_target_pairs={{0,4},{4,0},{8,12},{12,8},{16,20},{20,16},{24,28},{28,24},{32,36},... | collective-permute-start | bytes 1572872 | tf_op jit(solution)/shard_map/ppermute | solution.py:178
  31.0 2.4 %copy-start.1 = (bf16[2,10,4,16,512]{4,3,2,1,0:T(8,128)(2,1)}, bf16[2,10,4,16,512]{4,3,2,1,0:T(8,128)(2,1)S(1)}, u32[]{:S(2)}) copy-start(bf16[2,10,4,16,512]{4,3,2,1,0:T(8,128)(2,1)S(1)} %collective-permute-done.9.refs_5_) | copy-start | bytes 3932164
  36.6 13.4 %collective-permute-start.14 = (bf16[10,4,16,512]{3,2,1,0:T(8,128)(2,1)S(1)}, bf16[10,4,16,512]{3,2,1,0:T(8,128)(2,1)S(1)}, u32[]{:S(2)}, u32[]{:S(2)}) collective-permute-start(bf16[10,4,16,512]{3,2,1,0:T(8,128)(2,1)S(1)} %get-tuple-element.100), channel_id=1, source_target_pairs={{0,24},{4,12},{8,16},{12,4},{16,8},{20,28},{24,0},{28,20},{32,56},... | collective-permute-start | bytes 1966088 | tf_op jit(solution)/shard_map/ppermute | solution.py:174
  38.8 12.6 %collective-permute-start.15 = (bf16[10,4,16,512]{3,2,1,0:T(8,128)(2,1)S(1)}, bf16[10,4,16,512]{3,2,1,0:T(8,128)(2,1)S(1)}, u32[]{:S(2)}, u32[]{:S(2)}) collective-permute-start(bf16[10,4,16,512]{3,2,1,0:T(8,128)(2,1)S(1)} %get-tuple-element.101), channel_id=1, source_target_pairs={{0,96},{4,36},{8,104},{12,44},{16,112},{20,52},{24,120},{28,60},{3... | collective-permute-start | bytes 1966088 | tf_op jit(solution)/shard_map/ppermute | solution.py:174
  44.6 7.8 %collective-permute-start.12 = (bf16[4,4,16,512]{3,2,1,0:T(8,128)(2,1)S(1)}, bf16[4,4,16,512]{3,2,1,0:T(8,128)(2,1)S(1)}, u32[]{:S(2)}, u32[]{:S(2)}) collective-permute-start(bf16[4,4,16,512]{3,2,1,0:T(8,128)(2,1)S(1)} %get-tuple-element.96), channel_id=1, source_target_pairs={{0,24},{4,12},{8,16},{12,4},{16,8},{20,28},{24,0},{28,20},{32,56},... | collective-permute-start | bytes 786440 | tf_op jit(solution)/shard_map/ppermute | solution.py:174
  45.8 8.4 %collective-permute-start.13 = (bf16[4,4,16,512]{3,2,1,0:T(8,128)(2,1)S(1)}, bf16[4,4,16,512]{3,2,1,0:T(8,128)(2,1)S(1)}, u32[]{:S(2)}, u32[]{:S(2)}) collective-permute-start(bf16[4,4,16,512]{3,2,1,0:T(8,128)(2,1)S(1)} %get-tuple-element.97), channel_id=1, source_target_pairs={{0,96},{4,36},{8,104},{12,44},{16,112},{20,52},{24,120},{28,60},{3... | collective-permute-start | bytes 786440 | tf_op jit(solution)/shard_map/ppermute | solution.py:174
  55.8 8.7 %collective-permute-start.16 = (bf16[2,14,16,512]{3,2,1,0:T(8,128)(2,1)}, bf16[2,14,16,512]{3,2,1,0:T(8,128)(2,1)S(1)}, u32[]{:S(2)}, u32[]{:S(2)}) collective-permute-start(bf16[2,14,16,512]{3,2,1,0:T(8,128)(2,1)} %get-tuple-element.109), channel_id=1, source_target_pairs={{0,32},{4,100},{8,40},{12,108},{16,48},{20,116},{24,56},{28,124},{... | collective-permute-start | bytes 1376264 | tf_op jit(solution)/shard_map/ppermute | solution.py:174
  55.8 12.1 %collective-permute-start.18 = (bf16[2,14,16,512]{3,2,1,0:T(8,128)(2,1)S(1)}, bf16[2,14,16,512]{3,2,1,0:T(8,128)(2,1)S(1)}, u32[]{:S(2)}, u32[]{:S(2)}) collective-permute-start(bf16[2,14,16,512]{3,2,1,0:T(8,128)(2,1)S(1)} %get-tuple-element.112), channel_id=1, source_target_pairs={{0,8},{4,28},{8,0},{12,20},{16,24},{20,12},{24,16},{28,4},{32,40},... | collective-permute-start | bytes 1376264 | tf_op jit(solution)/shard_map/ppermute | solution.py:174
  64.5 7.3 %collective-permute-start.17 = (bf16[14,16,512]{2,1,0:T(8,128)(2,1)S(1)}, bf16[14,16,512]{2,1,0:T(8,128)(2,1)S(1)}, u32[]{:S(2)}, u32[]{:S(2)}) collective-permute-start(bf16[14,16,512]{2,1,0:T(8,128)(2,1)S(1)} %fusion.1), channel_id=1, source_target_pairs={{0,96},{4,36},{8,104},{12,44},{16,112},{20,52},{24,120},{28,60},{3... | collective-permute-start | bytes 688136 | tf_op jit(solution)/shard_map/ppermute | solution.py:174
  67.9 7.3 %collective-permute-start.19 = (bf16[14,16,512]{2,1,0:T(8,128)(2,1)S(1)}, bf16[14,16,512]{2,1,0:T(8,128)(2,1)S(1)}, u32[]{:S(2)}, u32[]{:S(2)}) collective-permute-start(bf16[14,16,512]{2,1,0:T(8,128)(2,1)S(1)} %fusion), channel_id=1, source_target_pairs={{0,24},{4,12},{8,16},{12,4},{16,8},{20,28},{24,0},{28,20},{32,56},... | collective-permute-start | bytes 688136 | tf_op jit(solution)/shard_map/ppermute | solution.py:174
  77.2 21.4 %copy-start.2 = (f32[1,2,512,512]{3,2,1,0:T(8,128)S(1)}, f32[1,2,512,512]{3,2,1,0:T(8,128)}, u32[]{:S(2)}) copy-start(f32[1,2,512,512]{3,2,1,0:T(8,128)} %param.7) | copy-start | bytes 6291460
  77.2 21.4 %all-to-all-start = ((bf16[32,2,16,512]{3,2,1,0:T(8,128)(2,1)}), bf16[32,2,16,512]{3,2,1,0:T(8,128)(2,1)S(1)}, u32[]{:S(2)}, u32[]{:S(2)}) async-start(bf16[32,2,16,512]{3,2,1,0:T(8,128)(2,1)} %bitcast.8), calls=%async_computation | async-start | bytes 2097152 | tf_op jit(solution)/shard_map/all_to_all | solution.py:458
  98.7 1.6 %copy-start.3 = (f32[1,2,512,512]{3,2,1,0:T(8,128)S(1)}, f32[1,2,512,512]{3,2,1,0:T(8,128)}, u32[]{:S(2)}) copy-start(f32[1,2,512,512]{3,2,1,0:T(8,128)} %param.8) | copy-start | bytes 6291460
  104.8 9.9 %copy-start.5 = (s32[4,28]{1,0:T(4,128)S(1)}, s32[4,28]{1,0:T(4,128)}, u32[]{:S(2)}) copy-start(s32[4,28]{1,0:T(4,128)} %param.9) | copy-start | bytes 1348
  104.8 27.2 %all-to-all-start.1 = ((bf16[32,2,16,512]{3,2,1,0:T(8,128)(2,1)}), bf16[32,2,16,512]{3,2,1,0:T(8,128)(2,1)S(1)}, u32[]{:S(2)}, u32[]{:S(2)}) async-start(bf16[32,2,16,512]{3,2,1,0:T(8,128)(2,1)} %get-tuple-element.116), calls=%async_computation.1 | async-start | bytes 2097152 | tf_op jit(solution)/shard_map/all_to_all | solution.py:461
  132.6 21.1 %collective-permute-start.24 = (bf16[28,16,512]{2,1,0:T(8,128)(2,1)S(1)}, bf16[28,16,512]{2,1,0:T(8,128)(2,1)S(1)}, u32[]{:S(2)}, u32[]{:S(2)}) collective-permute-start(bf16[28,16,512]{2,1,0:T(8,128)(2,1)S(1)} %gather_fusion.1), channel_id=1, source_target_pairs={{0,3},{1,0},{2,1},{3,2},{4,5},{5,6},{6,7},{7,4},{8,11},{9,8},{10,9... | collective-permute-start | bytes 1376264 | tf_op jit(solution)/shard_map/ppermute | solution.py:423
  134.3 9.7 %collective-permute-start.20 = (bf16[14,16,512]{2,1,0:T(8,128)(2,1)S(1)}, bf16[14,16,512]{2,1,0:T(8,128)(2,1)S(1)}, u32[]{:S(2)}, u32[]{:S(2)}) collective-permute-start(bf16[14,16,512]{2,1,0:T(8,128)(2,1)S(1)} %get-tuple-element.118), channel_id=1, source_target_pairs={{0,1},{1,2},{2,3},{3,0},{4,7},{5,4},{6,5},{7,6},{8,9},{9,10},{10,1... | collective-permute-start | bytes 688136 | tf_op jit(solution)/shard_map/ppermute | solution.py:423
  135.3 11.2 %collective-permute-start.21 = (bf16[14,16,512]{2,1,0:T(8,128)(2,1)S(1)}, bf16[14,16,512]{2,1,0:T(8,128)(2,1)S(1)}, u32[]{:S(2)}, u32[]{:S(2)}) collective-permute-start(bf16[14,16,512]{2,1,0:T(8,128)(2,1)S(1)} %get-tuple-element.117), channel_id=1, source_target_pairs={{0,1},{1,2},{2,3},{3,0},{4,7},{5,4},{6,5},{7,6},{8,9},{9,10},{10,1... | collective-permute-start | bytes 688136 | tf_op jit(solution)/shard_map/ppermute | solution.py:423
  144.0 7.2 %collective-permute-start.22 = (bf16[14,16,512]{2,1,0:T(8,128)(2,1)S(1)}, bf16[14,16,512]{2,1,0:T(8,128)(2,1)S(1)}, u32[]{:S(2)}, u32[]{:S(2)}) collective-permute-start(bf16[14,16,512]{2,1,0:T(8,128)(2,1)S(1)} %collective-permute-done.20), channel_id=1, source_target_pairs={{0,1},{1,2},{2,3},{3,0},{4,7},{5,4},{6,5},{7,6},{8,9},{9,10},{10,1... | collective-permute-start | bytes 688136 | tf_op jit(solution)/shard_map/ppermute | solution.py:423
  146.4 7.2 %collective-permute-start.23 = (bf16[14,16,512]{2,1,0:T(8,128)(2,1)S(1)}, bf16[14,16,512]{2,1,0:T(8,128)(2,1)S(1)}, u32[]{:S(2)}, u32[]{:S(2)}) collective-permute-start(bf16[14,16,512]{2,1,0:T(8,128)(2,1)S(1)} %collective-permute-done.21), channel_id=1, source_target_pairs={{0,1},{1,2},{2,3},{3,0},{4,7},{5,4},{6,5},{7,6},{8,9},{9,10},{10,1... | collective-permute-start | bytes 688136 | tf_op jit(solution)/shard_map/ppermute | solution.py:423
  153.7 1.2 copy-start.4

commit v4 on v3

--- a/solution.py
+++ b/solution.py
@@ -133,7 +133,7 @@
             jax.ShapeDtypeStruct(right.shape, jnp.float32),
             jax.ShapeDtypeStruct(received.shape, jnp.bfloat16),
         ],
-        compiler_params=pltpu.CompilerParams(vmem_limit_bytes=47 * 1024 * 1024),
+        compiler_params=pltpu.CompilerParams(vmem_limit_bytes=49 * 1024 * 1024),
         cost_estimate=pl.CostEstimate(
             flops=slots * 18 * 2 * extent**3,
             bytes_accessed=4 * left.size * 4 + 2 * received.size * 2,

time: 156 us -> 156 us (level)
  Pallas kernels: 30.9 us -> 35.5 us
  starting transfers between devices: 42.8 us -> 38.8 us
  local copies, waits for them, and re-layouts: 5.94 us -> 4.3 us
    pallas_call x1, Pallas kernels: 4.52 us -> 9.08 us  [slot_step(): pl.pallas_call(slot_kernel, grid_spec=pltpu.PrefetchScalarGridSpec(num_sc...]
    all_to_all x1, starting transfers between devices: 9.84 us -> 6.94 us  [per_device(): lax.all_to_all(updates, 'dp', split_axis=0, concat_axis=0, tiled=True)]
    unnamed x12 -> x10, local copies, waits for them, and re-layouts: 2.84 us -> 1.25 us
where the time goes in v4:
time: 156 us; the launch traced here: 155 us
  waiting for transfers between devices  75.4 us (48%)
  starting transfers between devices  38.8 us (25%)
  Pallas kernels  35.5 us (23%)
  local copies, waits for them, and re-layouts  4.3 us (3%)
    pallas_call x13, Pallas kernels, local_call(): pl.pallas_call(body, grid_spec=pltpu.PrefetchScalarGridSpec(num_scalar_pr...  26.4 us
    ppermute x12, waiting for transfers between devices, exchange(): return lax.ppermute(value, 'dp', pairs)  25.2 us
    all_to_all x1, waiting for transfers between devices, per_device(): lax.all_to_all(updates, 'dp', split_axis=0, concat_axis=0, tiled=True)  16.5 us
    ppermute x12, starting transfers between devices, exchange(): return lax.ppermute(value, 'dp', pairs)  16.4 us
    ppermute x5, waiting for transfers between devices, send_group(): return lax.ppermute(value, ('dp', 'mp'), pairs)  16.2 us
    all_to_all x1, waiting for transfers between devices, per_device(): lax.all_to_all(outgoing, 'dp', split_axis=0, concat_axis=0, tiled=True)  15.9 us
    pallas_call x1, Pallas kernels, slot_step(): pl.pallas_call(slot_kernel, grid_spec=pltpu.PrefetchScalarGridSpec(num_sc...  9.08 us
    all_to_all x1, starting transfers between devices, per_device(): lax.all_to_all(updates, 'dp', split_axis=0, concat_axis=0, tiled=True)  6.94 us
  transfers between devices with their start and end apart: 27, of which 16 were waited for; matrix products, arithmetic and copies ran while one was open for 2% of the time, Pallas kernels for 13%

profile of v4, /device:TPU:0, one launch (start us, length us, event | category | flops | bytes accessed | tf_op | source)
XLA Modules:
  0.0 155.3 jit_solution(7926940316126533289)
XLA Ops:
  0.7 0.1 pad_add_fusion.pos
  0.8 2.4 %shard_map.85 = (bf16[2,10,4,16,512]{4,3,2,1,0:T(8,128)(2,1)S(1)}, bf16[2,10,4,16,512]{4,3,2,1,0:T(8,128)(2,1)S(1)}) custom-call(s32[3]{0:T(128)S(1)} %pad_add_fusion.pos, bf16[28,4,4,2,16,512]{5,4,3,2,1,0:T(8,128)(2,1)} %bitcast.52, bf16[28,4,4,2,16,512]{5,4,3,2,1,0:T(8,128)(2,1)} %bitcast.53, bf16[28,4,4,2,16,512]{5,4,3,2,1,0:T(8,128)(2,1)} %bitcast.54, ...), custom_call_target="tpu_custom_call" | custom-call | flops 5242880 | bytes 10485760 | tf_op jit(solution)/shard_map/pallas_call | solution.py:203
  3.2 0.1 collective-permute-start
  3.3 0.5 collective-permute-start.1
  3.8 1.8 %shard_map.86 = (bf16[2,4,4,16,512]{4,3,2,1,0:T(8,128)(2,1)S(1)}, bf16[2,4,4,16,512]{4,3,2,1,0:T(8,128)(2,1)S(1)}) custom-call(s32[3]{0:T(128)S(1)} %pad_add_fusion.pos, bf16[28,4,4,2,16,512]{5,4,3,2,1,0:T(8,128)(2,1)} %bitcast.56, bf16[28,4,4,2,16,512]{5,4,3,2,1,0:T(8,128)(2,1)} %bitcast.57, bf16[28,4,4,2,16,512]{5,4,3,2,1,0:T(8,128)(2,1)} %bitcast.58, ...), custom_call_target="tpu_custom_call" | custom-call | flops 2097152 | bytes 4194304 | tf_op jit(solution)/shard_map/pallas_call | solution.py:203
  5.6 2.4 %shard_map.87 = (bf16[2,10,4,16,512]{4,3,2,1,0:T(8,128)(2,1)S(1)}, bf16[2,10,4,16,512]{4,3,2,1,0:T(8,128)(2,1)S(1)}) custom-call(s32[3]{0:T(128)S(1)} %pad_add_fusion.pos, bf16[28,4,4,2,16,512]{5,4,3,2,1,0:T(8,128)(2,1)} %bitcast.60, bf16[28,4,4,2,16,512]{5,4,3,2,1,0:T(8,128)(2,1)} %bitcast.61, bf16[28,4,4,2,16,512]{5,4,3,2,1,0:T(8,128)(2,1)} %bitcast.62, ...), custom_call_target="tpu_custom_call" | custom-call | flops 5242880 | bytes 10485760 | tf_op jit(solution)/shard_map/pallas_call | solution.py:203
  8.0 0.2 collective-permute-start.6
  8.2 0.4 collective-permute-start.2
  8.6 0.1 collective-permute-start.7
  8.7 2.9 %shard_map.88 = (bf16[2,10,4,16,512]{4,3,2,1,0:T(8,128)(2,1)S(1)}, bf16[2,10,4,16,512]{4,3,2,1,0:T(8,128)(2,1)S(1)}) custom-call(s32[3]{0:T(128)S(1)} %pad_add_fusion.pos, bf16[28,4,4,2,16,512]{5,4,3,2,1,0:T(8,128)(2,1)} %bitcast.67, bf16[28,4,4,2,16,512]{5,4,3,2,1,0:T(8,128)(2,1)} %bitcast.65, bf16[28,4,4,2,16,512]{5,4,3,2,1,0:T(8,128)(2,1)} %bitcast.66, ...), custom_call_target="tpu_custom_call" | custom-call | flops 5242880 | bytes 10485760 | tf_op jit(solution)/shard_map/pallas_call | solution.py:203
  11.7 1.7 %collective-permute-start.8 = (bf16[2,10,4,16,512]{4,3,2,1,0:T(8,128)(2,1)S(1)}, bf16[2,10,4,16,512]{4,3,2,1,0:T(8,128)(2,1)S(1)}, u32[]{:S(2)}, u32[]{:S(2)}) collective-permute-start(bf16[2,10,4,16,512]{4,3,2,1,0:T(8,128)(2,1)S(1)} %get-tuple-element.86), channel_id=1, source_target_pairs={{0,8},{4,28},{8,0},{12,20},{16,24},{20,12},{24,16},{28,4},{32,40},... | collective-permute-start | bytes 3932168 | tf_op jit(solution)/shard_map/ppermute | solution.py:174
  13.4 1.9 %collective-permute-start.9 = (bf16[2,10,4,16,512]{4,3,2,1,0:T(8,128)(2,1)S(1)}, bf16[2,10,4,16,512]{4,3,2,1,0:T(8,128)(2,1)S(1)}, u32[]{:S(2)}, u32[]{:S(2)}) collective-permute-start(bf16[2,10,4,16,512]{4,3,2,1,0:T(8,128)(2,1)S(1)} %get-tuple-element.87), channel_id=1, source_target_pairs={{0,32},{4,100},{8,40},{12,108},{16,48},{20,116},{24,56},{28,124},{... | collective-permute-start | bytes 3932168 | tf_op jit(solution)/shard_map/ppermute | solution.py:174
  15.3 3.4 %collective-permute-start.3 = (bf16[2,4,4,16,512]{4,3,2,1,0:T(8,128)(2,1)S(1)}, bf16[2,4,4,16,512]{4,3,2,1,0:T(8,128)(2,1)S(1)}, u32[]{:S(2)}, u32[]{:S(2)}) collective-permute-start(bf16[2,4,4,16,512]{4,3,2,1,0:T(8,128)(2,1)S(1)} %get-tuple-element.75), channel_id=1, source_target_pairs={{0,4},{4,0},{8,12},{12,8},{16,20},{20,16},{24,28},{28,24},{32,36},... | collective-permute-start | bytes 1572872 | tf_op jit(solution)/shard_map/ppermute | solution.py:178
  18.7 1.5 collective-permute-done.3.refs_5_
  20.3 2.0 %shard_map.89 = (bf16[2,4,4,16,512]{4,3,2,1,0:T(8,128)(2,1)S(1)}, bf16[2,4,4,16,512]{4,3,2,1,0:T(8,128)(2,1)S(1)}) custom-call(s32[3]{0:T(128)S(1)} %pad_add_fusion.pos, bf16[28,4,4,2,16,512]{5,4,3,2,1,0:T(8,128)(2,1)} %bitcast.68, bf16[28,4,4,2,16,512]{5,4,3,2,1,0:T(8,128)(2,1)} %bitcast.69, bf16[28,4,4,2,16,512]{5,4,3,2,1,0:T(8,128)(2,1)} %bitcast.70, ...), custom_call_target="tpu_custom_call" | custom-call | flops 2097152 | bytes 4194304 | tf_op jit(solution)/shard_map/pallas_call | solution.py:203
  22.3 0.2 collective-permute-start.10
  22.5 1.8 %shard_map.90 = (bf16[2,4,4,16,512]{4,3,2,1,0:T(8,128)(2,1)S(1)}, bf16[2,4,4,16,512]{4,3,2,1,0:T(8,128)(2,1)S(1)}) custom-call(s32[3]{0:T(128)S(1)} %pad_add_fusion.pos, bf16[28,4,4,2,16,512]{5,4,3,2,1,0:T(8,128)(2,1)} %bitcast.72, bf16[28,4,4,2,16,512]{5,4,3,2,1,0:T(8,128)(2,1)} %bitcast.73, bf16[28,4,4,2,16,512]{5,4,3,2,1,0:T(8,128)(2,1)} %bitcast.74, ...), custom_call_target="tpu_custom_call" | custom-call | flops 2097152 | bytes 4194304 | tf_op jit(solution)/shard_map/pallas_call | solution.py:203
  24.4 1.2 collective-permute-start.4
  25.5 3.8 %collective-permute-done.8.refs_4_ = bf16[2,10,4,16,512]{4,3,2,1,0:T(8,128)(2,1)S(1)} collective-permute-done((bf16[2,10,4,16,512]{4,3,2,1,0:T(8,128)(2,1)S(1)}, bf16[2,10,4,16,512]{4,3,2,1,0:T(8,128)(2,1)S(1)}, u32[]{:S(2)}, u32[]{:S(2)}) %collective-permute-start.8) | collective-permute-done | bytes 1310752 | tf_op jit(solution)/shard_map/ppermute | solution.py:174
  29.3 0.6 collective-permute-start.5
  30.0 1.0 collective-permute-done.9.refs_5_
  31.0 2.4 %shard_map.91 = (bf16[10,4,16,512]{3,2,1,0:T(8,128)(2,1)S(1)}, bf16[10,4,16,512]{3,2,1,0:T(8,128)(2,1)S(1)}) custom-call(s32[3]{0:T(128)S(1)} %pad_add_fusion.pos, bf16[28,4,4,2,16,512]{5,4,3,2,1,0:T(8,128)(2,1)} %bitcast.76, bf16[28,4,4,2,16,512]{5,4,3,2,1,0:T(8,128)(2,1)} %bitcast.77, bf16[2,10,4,16,512]{4,3,2,1,0:T(8,128)(2,1)S(1)} %collective-permute-done.6.refs_2_, ...), custom_call_target="tpu_custom_call" | custom-call | flops 2621440 | bytes 5242880 | tf_op jit(solution)/shard_map/pallas_call | solution.py:203
  33.4 1.6 %collective-permute-done.10.refs_4_ = bf16[2,4,4,16,512]{4,3,2,1,0:T(8,128)(2,1)S(1)} collective-permute-done((bf16[2,4,4,16,512]{4,3,2,1,0:T(8,128)(2,1)S(1)}, bf16[2,4,4,16,512]{4,3,2,1,0:T(8,128)(2,1)S(1)}, u32[]{:S(2)}, u32[]{:S(2)}) %collective-permute-start.10) | collective-permute-done | bytes 524320 | tf_op jit(solution)/shard_map/ppermute | solution.py:174
  35.0 1.7 %collective-permute-done.11.refs_5_ = bf16[2,4,4,16,512]{4,3,2,1,0:T(8,128)(2,1)S(1)} collective-permute-done((bf16[2,4,4,16,512]{4,3,2,1,0:T(8,128)(2,1)S(1)}, bf16[2,4,4,16,512]{4,3,2,1,0:T(8,128)(2,1)S(1)}, u32[]{:S(2)}, u32[]{:S(2)}) %collective-permute-start.11) | collective-permute-done | bytes 524320 | tf_op jit(solution)/shard_map/ppermute | solution.py:174
  36.6 2.2 %collective-permute-start.14 = (bf16[10,4,16,512]{3,2,1,0:T(8,128)(2,1)S(1)}, bf16[10,4,16,512]{3,2,1,0:T(8,128)(2,1)S(1)}, u32[]{:S(2)}, u32[]{:S(2)}) collective-permute-start(bf16[10,4,16,512]{3,2,1,0:T(8,128)(2,1)S(1)} %get-tuple-element.100), channel_id=1, source_target_pairs={{0,24},{4,12},{8,16},{12,4},{16,8},{20,28},{24,0},{28,20},{32,56},... | collective-permute-start | bytes 1966088 | tf_op jit(solution)/shard_map/ppermute | solution.py:174
  38.8 4.0 %collective-permute-start.15 = (bf16[10,4,16,512]{3,2,1,0:T(8,128)(2,1)S(1)}, bf16[10,4,16,512]{3,2,1,0:T(8,128)(2,1)S(1)}, u32[]{:S(2)}, u32[]{:S(2)}) collective-permute-start(bf16[10,4,16,512]{3,2,1,0:T(8,128)(2,1)S(1)} %get-tuple-element.101), channel_id=1, source_target_pairs={{0,96},{4,36},{8,104},{12,44},{16,112},{20,52},{24,120},{28,60},{3... | collective-permute-start | bytes 1966088 | tf_op jit(solution)/shard_map/ppermute | solution.py:174
  42.8 1.8 %shard_map.93 = (bf16[4,4,16,512]{3,2,1,0:T(8,128)(2,1)S(1)}, bf16[4,4,16,512]{3,2,1,0:T(8,128)(2,1)S(1)}) custom-call(s32[3]{0:T(128)S(1)} %pad_add_fusion.pos, bf16[28,4,4,2,16,512]{5,4,3,2,1,0:T(8,128)(2,1)} %bitcast.78, bf16[28,4,4,2,16,512]{5,4,3,2,1,0:T(8,128)(2,1)} %bitcast.79, bf16[2,4,4,16,512]{4,3,2,1,0:T(8,128)(2,1)S(1)} %collective-permute-done.4.refs_2_, ...), custom_call_target="tpu_custom_call" | custom-call | flops 1048576 | bytes 2097152 | tf_op jit(solution)/shard_map/pallas_call | solution.py:203
  44.6 1.1 collective-permute-start.12
  45.8 0.0 collective-permute-start.13
  45.8 1.8 %shard_map.92 = (f32[4,4,16,512]{3,2,1,0:T(8,128)S(1)}, f32[4,4,16,512]{3,2,1,0:T(8,128)S(1)}) custom-call(s32[3]{0:T(128)S(1)} %pad_add_fusion.pos, bf16[28,4,4,2,16,512]{5,4,3,2,1,0:T(8,128)(2,1)} %bitcast.80, bf16[28,4,4,2,16,512]{5,4,3,2,1,0:T(8,128)(2,1)} %bitcast.81, bf16[2,4,4,16,512]{4,3,2,1,0:T(8,128)(2,1)S(1)} %collective-permute-done.4.refs_2_, ...), custom_call_target="tpu_custom_call" | custom-call | flops 1048576 | bytes 2097152 | tf_op jit(solution)/shard_map/pallas_call | solution.py:203
  47.5 2.5 %shard_map.94 = (f32[10,4,16,512]{3,2,1,0:T(8,128)S(1)}, f32[10,4,16,512]{3,2,1,0:T(8,128)S(1)}) custom-call(s32[3]{0:T(128)S(1)} %pad_add_fusion.pos, bf16[28,4,4,2,16,512]{5,4,3,2,1,0:T(8,128)(2,1)} %bitcast.82, bf16[28,4,4,2,16,512]{5,4,3,2,1,0:T(8,128)(2,1)} %bitcast.83, bf16[2,10,4,16,512]{4,3,2,1,0:T(8,128)(2,1)S(1)} %collective-permute-done.6.refs_2_, ...), custom_call_target="tpu_custom_call" | custom-call | flops 2621440 | bytes 5242880 | tf_op jit(solution)/shard_map/pallas_call | solution.py:203
  50.0 1.4 collective-permute-done.15.refs_3_
  51.4 1.0 shard_map.95
  52.4 1.8 %collective-permute-done.13.refs_3_ = bf16[4,4,16,512]{3,2,1,0:T(8,128)(2,1)S(1)} collective-permute-done((bf16[4,4,16,512]{3,2,1,0:T(8,128)(2,1)S(1)}, bf16[4,4,16,512]{3,2,1,0:T(8,128)(2,1)S(1)}, u32[]{:S(2)}, u32[]{:S(2)}) %collective-permute-start.13) | collective-permute-done | bytes 262176 | tf_op jit(solution)/shard_map/ppermute | solution.py:174
  54.2 1.5 shard_map.96
  55.8 0.7 collective-permute-start.18
  56.4 8.0 %collective-permute-done.16.refs_1_ = bf16[2,14,16,512]{3,2,1,0:T(8,128)(2,1)S(1)} collective-permute-done((bf16[2,14,16,512]{3,2,1,0:T(8,128)(2,1)}, bf16[2,14,16,512]{3,2,1,0:T(8,128)(2,1)S(1)}, u32[]{:S(2)}, u32[]{:S(2)}) %collective-permute-start.16) | collective-permute-done | bytes 458784 | tf_op jit(solution)/shard_map/ppermute | solution.py:174
  64.4 0.1 fusion.1
  64.5 3.3 %collective-permute-start.17 = (bf16[14,16,512]{2,1,0:T(8,128)(2,1)S(1)}, bf16[14,16,512]{2,1,0:T(8,128)(2,1)S(1)}, u32[]{:S(2)}, u32[]{:S(2)}) collective-permute-start(bf16[14,16,512]{2,1,0:T(8,128)(2,1)S(1)} %fusion.1), channel_id=1, source_target_pairs={{0,96},{4,36},{8,104},{12,44},{16,112},{20,52},{24,120},{28,60},{3... | collective-permute-start | bytes 688136 | tf_op jit(solution)/shard_map/ppermute | solution.py:174
  67.8 0.1 fusion
  67.9 1.1 collective-permute-start.19
  69.0 0.1 add_minimum_fusion
  69.1 0.1 min.12.wanted
  69.2 2.6 %collective-permute-done.17.refs_2_ = bf16[14,16,512]{2,1,0:T(8,128)(2,1)S(1)} collective-permute-done((bf16[14,16,512]{2,1,0:T(8,128)(2,1)S(1)}, bf16[14,16,512]{2,1,0:T(8,128)(2,1)S(1)}, u32[]{:S(2)}, u32[]{:S(2)}) %collective-permute-start.17) | collective-permute-done | bytes 229408 | tf_op jit(solution)/shard_map/ppermute | solution.py:174
  71.8 3.4 %collective-permute-done.19.refs_5_ = bf16[14,16,512]{2,1,0:T(8,128)(2,1)S(1)} collective-permute-done((bf16[14,16,512]{2,1,0:T(8,128)(2,1)S(1)}, bf16[14,16,512]{2,1,0:T(8,128)(2,1)S(1)}, u32[]{:S(2)}, u32[]{:S(2)}) %collective-permute-start.19) | collective-permute-done | bytes 229408 | tf_op jit(solution)/shard_map/ppermute | solution.py:174
  75.2 2.0 %shard_map.97 = bf16[64,16,512]{2,1,0:T(8,128)(2,1)} custom-call(s32[64]{0:T(128)S(1)} %min.12.wanted, f32[14,16,512]{2,1,0:T(8,128)S(1)} %get-tuple-element.108.refs_0_, bf16[2,14,16,512]{3,2,1,0:T(8,128)(2,1)S(1)} %collective-permute-done.16.refs_1_, bf16[14,16,512]{2,1,0:T(8,128)(2,1)S(1)} %collective-permute-done.17.refs_2_, ...), custom_call_target="tpu_custom_call" | custom-call | flops 2097152 | bytes 4194304 | tf_op jit(solution)/shard_map/pallas_call | solution.py:203
  77.2 4.2 %all-to-all-start = ((bf16[32,2,16,512]{3,2,1,0:T(8,128)(2,1)}), bf16[32,2,16,512]{3,2,1,0:T(8,128)(2,1)S(1)}, u32[]{:S(2)}, u32[]{:S(2)}) async-start(bf16[32,2,16,512]{3,2,1,0:T(8,128)(2,1)} %bitcast.8), calls=%async_computation | async-start | bytes 2097152 | tf_op jit(solution)/shard_map/all_to_all | solution.py:458
  81.5 1.2 dynamic_slice.14
  82.8 15.9 %all-to-all-done.block_ref = bf16[32,2,16,512]{3,2,1,0:T(8,128)(2,1)S(1)} async-done(((bf16[32,2,16,512]{3,2,1,0:T(8,128)(2,1)}), bf16[32,2,16,512]{3,2,1,0:T(8,128)(2,1)S(1)}, u32[]{:S(2)}, u32[]{:S(2)}) %all-to-all-start) | async-done | bytes 1048608 | tf_op jit(solution)/shard_map/all_to_all | solution.py:458
  98.7 9.1 %shard_map.98 = (f32[2,512,512]{2,1,0:T(8,128)}, f32[2,512,512]{2,1,0:T(8,128)}, bf16[32,2,16,512]{3,2,1,0:T(8,128)(2,1)}) custom-call(s32[1]{0:T(128)} %bitcast.count_ref, bf16[32,2,16,512]{3,2,1,0:T(8,128)(2,1)S(1)} %all-to-all-done.block_ref, f32[2,512,512]{2,1,0:T(8,128)S(1)} %bitcast.51, f32[2,512,512]{2,1,0:T(8,128)} %bitcast.85), custom_call_target="tpu_custom_call" | custom-call | flops 9663676416 | bytes 10485760 | tf_op jit(solution)/shard_map/pallas_call | solution.py:122
  107.8 6.9 %all-to-all-start.1 = ((bf16[32,2,16,512]{3,2,1,0:T(8,128)(2,1)}), bf16[32,2,16,512]{3,2,1,0:T(8,128)(2,1)S(1)}, u32[]{:S(2)}, u32[]{:S(2)}) async-start(bf16[32,2,16,512]{3,2,1,0:T(8,128)(2,1)} %get-tuple-element.116), calls=%async_computation.1 | async-start | bytes 2097152 | tf_op jit(solution)/shard_map/all_to_all | solution.py:461
  114.8 0.7 gather_fusion
  115.6 16.5 %all-to-all-done.1 = bf16[32,2,16,512]{3,2,1,0:T(8,128)(2,1)S(1)} async-done(((bf16[32,2,16,512]{3,2,1,0:T(8,128)(2,1)}), bf16[32,2,16,512]{3,2,1,0:T(8,128)(2,1)S(1)}, u32[]{:S(2)}, u32[]{:S(2)}) %all-to-all-start.1) | async-done | bytes 1048608 | tf_op jit(solution)/shard_map/all_to_all | solution.py:461
  132.0 0.6 gather_fusion.1
  132.7 3.3 %collective-permute-start.24 = (bf16[28,16,512]{2,1,0:T(8,128)(2,1)S(1)}, bf16[28,16,512]{2,1,0:T(8,128)(2,1)S(1)}, u32[]{:S(2)}, u32[]{:S(2)}) collective-permute-start(bf16[28,16,512]{2,1,0:T(8,128)(2,1)S(1)} %gather_fusion.1), channel_id=1, source_target_pairs={{0,3},{1,0},{2,1},{3,2},{4,5},{5,6},{6,7},{7,4},{8,11},{9,8},{10,9... | collective-permute-start | bytes 1376264 | tf_op jit(solution)/shard_map/ppermute | solution.py:423
  135.9 0.8 collective-permute-start.21
  136.7 0.2 broadcast_in_dim.33
  137.0 7.3 %collective-permute-done.20 = bf16[14,16,512]{2,1,0:T(8,128)(2,1)S(1)} collective-permute-done((bf16[14,16,512]{2,1,0:T(8,128)(2,1)S(1)}, bf16[14,16,512]{2,1,0:T(8,128)(2,1)S(1)}, u32[]{:S(2)}, u32[]{:S(2)}) %collective-permute-start.20) | collective-permute-done | bytes 229408 | tf_op jit(solution)/shard_map/ppermute | solution.py:423
  144.3 0.2 collective-permute-start.22
  144.5 2.3 %collective-permute-done.21 = bf16[14,16,512]{2,1,0:T(8,128)(2,1)S(1)} collective-permute-done((bf16[14,16,512]{2,1,0:T(8,128)(2,1)S(1)}, bf16[14,16,512]{2,1,0:T(8,128)(2,1)S(1)}, u32[]{:S(2)}, u32[]{:S(2)}) %collective-permute-start.21) | collective-permute-done | bytes 229408 | tf_op jit(solution)/shard_map/ppermute | solution.py:423
  146.7 0.5 collective-permute-start.23
  147.3 4.2 %collective-permute-done.22 = bf16[14,16,512]{2,1,0:T(8,128)(2,1)S(1)} collective-permute-done((bf16[14,16,512]{2,1,0:T(8,128)(2,1)S(1)}, bf16[14,16,512]{2,1,0:T(8,128)(2,1)S(1)}, u32[]{:S(2)}, u32[]{:S(2)}) %collective-permute-start.22) | collective-permute-done | bytes 229408 | tf_op jit(solution)/shard_map/ppermute | solution.py:423
  151.5 2.4 %collective-permute-done.23 = bf16[14,16,512]{2,1,0:T(8,128)(2,1)S(1)} collective-permute-done((bf16[14,16,512]{2,1,0:T(8,128)(2,1)S(1)}, bf16[14,16,512]{2,1,0:T(8,128)(2,1)S(1)}, u32[]{:S(2)}, u32[]{:S(2)}) %collective-permute-start.23) | collective-permute-done | bytes 229408 | tf_op jit(solution)/shard_map/ppermute | solution.py:423
  154.1 1.2 copy-done.3
  (35 shorter events, 0.3 us)
Async XLA Ops:
  0.6 68.4 %copy-start = (s32[4,32]{1,0:T(4,128)S(1)}, s32[4,32]{1,0:T(4,128)}, u32[]{:S(2)}) copy-start(s32[4,32]{1,0:T(4,128)} %param.11) | copy-start | bytes 1540
  3.2 5.5 %collective-permute-start = (bf16[2,10,4,16,512]{4,3,2,1,0:T(8,128)(2,1)S(1)}, bf16[2,10,4,16,512]{4,3,2,1,0:T(8,128)(2,1)S(1)}, u32[]{:S(2)}, u32[]{:S(2)}) collective-permute-start(bf16[2,10,4,16,512]{4,3,2,1,0:T(8,128)(2,1)S(1)} %get-tuple-element.69), channel_id=1, source_target_pairs={{0,4},{4,0},{8,12},{12,8},{16,20},{20,16},{24,28},{28,24},{32,36},... | collective-permute-start | bytes 3932168 | tf_op jit(solution)/shard_map/ppermute | solution.py:178
  3.3 5.4 %collective-permute-start.1 = (bf16[2,10,4,16,512]{4,3,2,1,0:T(8,128)(2,1)S(1)}, bf16[2,10,4,16,512]{4,3,2,1,0:T(8,128)(2,1)S(1)}, u32[]{:S(2)}, u32[]{:S(2)}) collective-permute-start(bf16[2,10,4,16,512]{4,3,2,1,0:T(8,128)(2,1)S(1)} %get-tuple-element.70), channel_id=1, source_target_pairs={{0,4},{4,0},{8,12},{12,8},{16,20},{20,16},{24,28},{28,24},{32,36},... | collective-permute-start | bytes 3932168 | tf_op jit(solution)/shard_map/ppermute | solution.py:178
  8.0 14.5 %collective-permute-start.6 = (bf16[2,10,4,16,512]{4,3,2,1,0:T(8,128)(2,1)S(1)}, bf16[2,10,4,16,512]{4,3,2,1,0:T(8,128)(2,1)S(1)}, u32[]{:S(2)}, u32[]{:S(2)}) collective-permute-start(bf16[2,10,4,16,512]{4,3,2,1,0:T(8,128)(2,1)S(1)} %get-tuple-element.84), channel_id=1, source_target_pairs={{0,4},{4,0},{8,12},{12,8},{16,20},{20,16},{24,28},{28,24},{32,36},... | collective-permute-start | bytes 3932168 | tf_op jit(solution)/shard_map/ppermute | solution.py:178
  8.2 7.1 %collective-permute-start.2 = (bf16[2,4,4,16,512]{4,3,2,1,0:T(8,128)(2,1)S(1)}, bf16[2,4,4,16,512]{4,3,2,1,0:T(8,128)(2,1)S(1)}, u32[]{:S(2)}, u32[]{:S(2)}) collective-permute-start(bf16[2,4,4,16,512]{4,3,2,1,0:T(8,128)(2,1)S(1)} %get-tuple-element.74), channel_id=1, source_target_pairs={{0,4},{4,0},{8,12},{12,8},{16,20},{20,16},{24,28},{28,24},{32,36},... | collective-permute-start | bytes 1572872 | tf_op jit(solution)/shard_map/ppermute | solution.py:178
  8.6 15.7 %collective-permute-start.7 = (bf16[2,10,4,16,512]{4,3,2,1,0:T(8,128)(2,1)S(1)}, bf16[2,10,4,16,512]{4,3,2,1,0:T(8,128)(2,1)S(1)}, u32[]{:S(2)}, u32[]{:S(2)}) collective-permute-start(bf16[2,10,4,16,512]{4,3,2,1,0:T(8,128)(2,1)S(1)} %get-tuple-element.85), channel_id=1, source_target_pairs={{0,4},{4,0},{8,12},{12,8},{16,20},{20,16},{24,28},{28,24},{32,36},... | collective-permute-start | bytes 3932168 | tf_op jit(solution)/shard_map/ppermute | solution.py:178
  11.7 17.7 %collective-permute-start.8 = (bf16[2,10,4,16,512]{4,3,2,1,0:T(8,128)(2,1)S(1)}, bf16[2,10,4,16,512]{4,3,2,1,0:T(8,128)(2,1)S(1)}, u32[]{:S(2)}, u32[]{:S(2)}) collective-permute-start(bf16[2,10,4,16,512]{4,3,2,1,0:T(8,128)(2,1)S(1)} %get-tuple-element.86), channel_id=1, source_target_pairs={{0,8},{4,28},{8,0},{12,20},{16,24},{20,12},{24,16},{28,4},{32,40},... | collective-permute-start | bytes 3932168 | tf_op jit(solution)/shard_map/ppermute | solution.py:174
  13.4 17.6 %collective-permute-start.9 = (bf16[2,10,4,16,512]{4,3,2,1,0:T(8,128)(2,1)S(1)}, bf16[2,10,4,16,512]{4,3,2,1,0:T(8,128)(2,1)S(1)}, u32[]{:S(2)}, u32[]{:S(2)}) collective-permute-start(bf16[2,10,4,16,512]{4,3,2,1,0:T(8,128)(2,1)S(1)} %get-tuple-element.87), channel_id=1, source_target_pairs={{0,32},{4,100},{8,40},{12,108},{16,48},{20,116},{24,56},{28,124},{... | collective-permute-start | bytes 3932168 | tf_op jit(solution)/shard_map/ppermute | solution.py:174
  15.3 5.0 %collective-permute-start.3 = (bf16[2,4,4,16,512]{4,3,2,1,0:T(8,128)(2,1)S(1)}, bf16[2,4,4,16,512]{4,3,2,1,0:T(8,128)(2,1)S(1)}, u32[]{:S(2)}, u32[]{:S(2)}) collective-permute-start(bf16[2,4,4,16,512]{4,3,2,1,0:T(8,128)(2,1)S(1)} %get-tuple-element.75), channel_id=1, source_target_pairs={{0,4},{4,0},{8,12},{12,8},{16,20},{20,16},{24,28},{28,24},{32,36},... | collective-permute-start | bytes 1572872 | tf_op jit(solution)/shard_map/ppermute | solution.py:178
  22.3 12.7 %collective-permute-start.10 = (bf16[2,4,4,16,512]{4,3,2,1,0:T(8,128)(2,1)S(1)}, bf16[2,4,4,16,512]{4,3,2,1,0:T(8,128)(2,1)S(1)}, u32[]{:S(2)}, u32[]{:S(2)}) collective-permute-start(bf16[2,4,4,16,512]{4,3,2,1,0:T(8,128)(2,1)S(1)} %get-tuple-element.90), channel_id=1, source_target_pairs={{0,8},{4,28},{8,0},{12,20},{16,24},{20,12},{24,16},{28,4},{32,40},... | collective-permute-start | bytes 1572872 | tf_op jit(solution)/shard_map/ppermute | solution.py:174
  22.5 14.1 %collective-permute-start.11 = (bf16[2,4,4,16,512]{4,3,2,1,0:T(8,128)(2,1)S(1)}, bf16[2,4,4,16,512]{4,3,2,1,0:T(8,128)(2,1)S(1)}, u32[]{:S(2)}, u32[]{:S(2)}) collective-permute-start(bf16[2,4,4,16,512]{4,3,2,1,0:T(8,128)(2,1)S(1)} %get-tuple-element.91), channel_id=1, source_target_pairs={{0,32},{4,100},{8,40},{12,108},{16,48},{20,116},{24,56},{28,124},{... | collective-permute-start | bytes 1572872 | tf_op jit(solution)/shard_map/ppermute | solution.py:174
  24.4 18.5 %collective-permute-start.4 = (bf16[2,4,4,16,512]{4,3,2,1,0:T(8,128)(2,1)S(1)}, bf16[2,4,4,16,512]{4,3,2,1,0:T(8,128)(2,1)S(1)}, u32[]{:S(2)}, u32[]{:S(2)}) collective-permute-start(bf16[2,4,4,16,512]{4,3,2,1,0:T(8,128)(2,1)S(1)} %get-tuple-element.82), channel_id=1, source_target_pairs={{0,4},{4,0},{8,12},{12,8},{16,20},{20,16},{24,28},{28,24},{32,36},... | collective-permute-start | bytes 1572872 | tf_op jit(solution)/shard_map/ppermute | solution.py:178
  29.3 13.5 %collective-permute-start.5 = (bf16[2,4,4,16,512]{4,3,2,1,0:T(8,128)(2,1)S(1)}, bf16[2,4,4,16,512]{4,3,2,1,0:T(8,128)(2,1)S(1)}, u32[]{:S(2)}, u32[]{:S(2)}) collective-permute-start(bf16[2,4,4,16,512]{4,3,2,1,0:T(8,128)(2,1)S(1)} %get-tuple-element.83), channel_id=1, source_target_pairs={{0,4},{4,0},{8,12},{12,8},{16,20},{20,16},{24,28},{28,24},{32,36},... | collective-permute-start | bytes 1572872 | tf_op jit(solution)/shard_map/ppermute | solution.py:178
  31.0 2.4 %copy-start.1 = (bf16[2,10,4,16,512]{4,3,2,1,0:T(8,128)(2,1)}, bf16[2,10,4,16,512]{4,3,2,1,0:T(8,128)(2,1)S(1)}, u32[]{:S(2)}) copy-start(bf16[2,10,4,16,512]{4,3,2,1,0:T(8,128)(2,1)S(1)} %collective-permute-done.9.refs_5_) | copy-start | bytes 3932164
  36.6 13.4 %collective-permute-start.14 = (bf16[10,4,16,512]{3,2,1,0:T(8,128)(2,1)S(1)}, bf16[10,4,16,512]{3,2,1,0:T(8,128)(2,1)S(1)}, u32[]{:S(2)}, u32[]{:S(2)}) collective-permute-start(bf16[10,4,16,512]{3,2,1,0:T(8,128)(2,1)S(1)} %get-tuple-element.100), channel_id=1, source_target_pairs={{0,24},{4,12},{8,16},{12,4},{16,8},{20,28},{24,0},{28,20},{32,56},... | collective-permute-start | bytes 1966088 | tf_op jit(solution)/shard_map/ppermute | solution.py:174
  38.8 12.6 %collective-permute-start.15 = (bf16[10,4,16,512]{3,2,1,0:T(8,128)(2,1)S(1)}, bf16[10,4,16,512]{3,2,1,0:T(8,128)(2,1)S(1)}, u32[]{:S(2)}, u32[]{:S(2)}) collective-permute-start(bf16[10,4,16,512]{3,2,1,0:T(8,128)(2,1)S(1)} %get-tuple-element.101), channel_id=1, source_target_pairs={{0,96},{4,36},{8,104},{12,44},{16,112},{20,52},{24,120},{28,60},{3... | collective-permute-start | bytes 1966088 | tf_op jit(solution)/shard_map/ppermute | solution.py:174
  44.6 7.8 %collective-permute-start.12 = (bf16[4,4,16,512]{3,2,1,0:T(8,128)(2,1)S(1)}, bf16[4,4,16,512]{3,2,1,0:T(8,128)(2,1)S(1)}, u32[]{:S(2)}, u32[]{:S(2)}) collective-permute-start(bf16[4,4,16,512]{3,2,1,0:T(8,128)(2,1)S(1)} %get-tuple-element.96), channel_id=1, source_target_pairs={{0,24},{4,12},{8,16},{12,4},{16,8},{20,28},{24,0},{28,20},{32,56},... | collective-permute-start | bytes 786440 | tf_op jit(solution)/shard_map/ppermute | solution.py:174
  45.8 8.4 %collective-permute-start.13 = (bf16[4,4,16,512]{3,2,1,0:T(8,128)(2,1)S(1)}, bf16[4,4,16,512]{3,2,1,0:T(8,128)(2,1)S(1)}, u32[]{:S(2)}, u32[]{:S(2)}) collective-permute-start(bf16[4,4,16,512]{3,2,1,0:T(8,128)(2,1)S(1)} %get-tuple-element.97), channel_id=1, source_target_pairs={{0,96},{4,36},{8,104},{12,44},{16,112},{20,52},{24,120},{28,60},{3... | collective-permute-start | bytes 786440 | tf_op jit(solution)/shard_map/ppermute | solution.py:174
  55.8 8.7 %collective-permute-start.16 = (bf16[2,14,16,512]{3,2,1,0:T(8,128)(2,1)}, bf16[2,14,16,512]{3,2,1,0:T(8,128)(2,1)S(1)}, u32[]{:S(2)}, u32[]{:S(2)}) collective-permute-start(bf16[2,14,16,512]{3,2,1,0:T(8,128)(2,1)} %get-tuple-element.109), channel_id=1, source_target_pairs={{0,32},{4,100},{8,40},{12,108},{16,48},{20,116},{24,56},{28,124},{... | collective-permute-start | bytes 1376264 | tf_op jit(solution)/shard_map/ppermute | solution.py:174
  55.8 12.1 %collective-permute-start.18 = (bf16[2,14,16,512]{3,2,1,0:T(8,128)(2,1)S(1)}, bf16[2,14,16,512]{3,2,1,0:T(8,128)(2,1)S(1)}, u32[]{:S(2)}, u32[]{:S(2)}) collective-permute-start(bf16[2,14,16,512]{3,2,1,0:T(8,128)(2,1)S(1)} %get-tuple-element.112), channel_id=1, source_target_pairs={{0,8},{4,28},{8,0},{12,20},{16,24},{20,12},{24,16},{28,4},{32,40},... | collective-permute-start | bytes 1376264 | tf_op jit(solution)/shard_map/ppermute | solution.py:174
  64.5 7.3 %collective-permute-start.17 = (bf16[14,16,512]{2,1,0:T(8,128)(2,1)S(1)}, bf16[14,16,512]{2,1,0:T(8,128)(2,1)S(1)}, u32[]{:S(2)}, u32[]{:S(2)}) collective-permute-start(bf16[14,16,512]{2,1,0:T(8,128)(2,1)S(1)} %fusion.1), channel_id=1, source_target_pairs={{0,96},{4,36},{8,104},{12,44},{16,112},{20,52},{24,120},{28,60},{3... | collective-permute-start | bytes 688136 | tf_op jit(solution)/shard_map/ppermute | solution.py:174
  67.9 7.3 %collective-permute-start.19 = (bf16[14,16,512]{2,1,0:T(8,128)(2,1)S(1)}, bf16[14,16,512]{2,1,0:T(8,128)(2,1)S(1)}, u32[]{:S(2)}, u32[]{:S(2)}) collective-permute-start(bf16[14,16,512]{2,1,0:T(8,128)(2,1)S(1)} %fusion), channel_id=1, source_target_pairs={{0,24},{4,12},{8,16},{12,4},{16,8},{20,28},{24,0},{28,20},{32,56},... | collective-permute-start | bytes 688136 | tf_op jit(solution)/shard_map/ppermute | solution.py:174
  77.2 21.4 %copy-start.2 = (f32[1,2,512,512]{3,2,1,0:T(8,128)S(1)}, f32[1,2,512,512]{3,2,1,0:T(8,128)}, u32[]{:S(2)}) copy-start(f32[1,2,512,512]{3,2,1,0:T(8,128)} %param.7) | copy-start | bytes 6291460
  77.2 21.4 %all-to-all-start = ((bf16[32,2,16,512]{3,2,1,0:T(8,128)(2,1)}), bf16[32,2,16,512]{3,2,1,0:T(8,128)(2,1)S(1)}, u32[]{:S(2)}, u32[]{:S(2)}) async-start(bf16[32,2,16,512]{3,2,1,0:T(8,128)(2,1)} %bitcast.8), calls=%async_computation | async-start | bytes 2097152 | tf_op jit(solution)/shard_map/all_to_all | solution.py:458
  107.8 7.0 %copy-start.4 = (s32[4,28]{1,0:T(4,128)S(1)}, s32[4,28]{1,0:T(4,128)}, u32[]{:S(2)}) copy-start(s32[4,28]{1,0:T(4,128)} %param.9) | copy-start | bytes 1348
  107.8 24.3 %all-to-all-start.1 = ((bf16[32,2,16,512]{3,2,1,0:T(8,128)(2,1)}), bf16[32,2,16,512]{3,2,1,0:T(8,128)(2,1)S(1)}, u32[]{:S(2)}, u32[]{:S(2)}) async-start(bf16[32,2,16,512]{3,2,1,0:T(8,128)(2,1)} %get-tuple-element.116), calls=%async_computation.1 | async-start | bytes 2097152 | tf_op jit(solution)/shard_map/all_to_all | solution.py:461
  132.7 21.3 %collective-permute-start.24 = (bf16[28,16,512]{2,1,0:T(8,128)(2,1)S(1)}, bf16[28,16,512]{2,1,0:T(8,128)(2,1)S(1)}, u32[]{:S(2)}, u32[]{:S(2)}) collective-permute-start(bf16[28,16,512]{2,1,0:T(8,128)(2,1)S(1)} %gather_fusion.1), channel_id=1, source_target_pairs={{0,3},{1,0},{2,1},{3,2},{4,5},{5,6},{6,7},{7,4},{8,11},{9,8},{10,9... | collective-permute-start | bytes 1376264 | tf_op jit(solution)/shard_map/ppermute | solution.py:423
  135.9 8.3 %collective-permute-start.20 = (bf16[14,16,512]{2,1,0:T(8,128)(2,1)S(1)}, bf16[14,16,512]{2,1,0:T(8,128)(2,1)S(1)}, u32[]{:S(2)}, u32[]{:S(2)}) collective-permute-start(bf16[14,16,512]{2,1,0:T(8,128)(2,1)S(1)} %get-tuple-element.118), channel_id=1, source_target_pairs={{0,1},{1,2},{2,3},{3,0},{4,7},{5,4},{6,5},{7,6},{8,9},{9,10},{10,1... | collective-permute-start | bytes 688136 | tf_op jit(solution)/shard_map/ppermute | solution.py:423
  135.9 10.8 %collective-permute-start.21 = (bf16[14,16,512]{2,1,0:T(8,128)(2,1)S(1)}, bf16[14,16,512]{2,1,0:T(8,128)(2,1)S(1)}, u32[]{:S(2)}, u32[]{:S(2)}) collective-permute-start(bf16[14,16,512]{2,1,0:T(8,128)(2,1)S(1)} %get-tuple-element.117), channel_id=1, source_target_pairs={{0,1},{1,2},{2,3},{3,0},{4,7},{5,4},{6,5},{7,6},{8,9},{9,10},{10,1... | collective-permute-start | bytes 688136 | tf_op jit(solution)/shard_map/ppermute | solution.py:423
  144.3 7.2 %collective-permute-start.22 = (bf16[14,16,512]{2,1,0:T(8,128)(2,1)S(1)}, bf16[14,16,512]{2,1,0:T(8,128)(2,1)S(1)}, u32[]{:S(2)}, u32[]{:S(2)}) collective-permute-start(bf16[14,16,512]{2,1,0:T(8,128)(2,1)S(1)} %collective-permute-done.20), channel_id=1, source_target_pairs={{0,1},{1,2},{2,3},{3,0},{4,7},{5,4},{6,5},{7,6},{8,9},{9,10},{10,1... | collective-permute-start | bytes 688136 | tf_op jit(solution)/shard_map/ppermute | solution.py:423
  146.7 7.2 %collective-permute-start.23 = (bf16[14,16,512]{2,1,0:T(8,128)(2,1)S(1)}, bf16[14,16,512]{2,1,0:T(8,128)(2,1)S(1)}, u32[]{:S(2)}, u32[]{:S(2)}) collective-permute-start(bf16[14,16,512]{2,1,0:T(8,128)(2,1)S(1)} %collective-permute-done.21), channel_id=1, source_target_pairs={{0,1},{1,2},{2,3},{3,0},{4,7},{5,4},{6,5},{7,6},{8,9},{9,10},{10,1... | collective-permute-start | bytes 688136 | tf_op jit(solution)/shard_map/ppermute | solution.py:423
  154.0 1.2 copy-start.3

commit v5 on v4

--- a/solution.py
+++ b/solution.py
@@ -13,6 +13,7 @@
 START = 25.0 / 16.0
 VMEM = 47 * 1024 * 1024
 SETS = (10, 4)
+PLACES = 2
 
 
 def tail_coefficients():
@@ -198,13 +199,13 @@
     ]
 
 
-def local_call(body, pos, in_specs, args, out_specs, out_shape, scratch=()):
+def local_call(body, pos, in_specs, args, out_specs, out_shape, scratch=(), steps=1):
     moved = sum(4 * v.size for v in out_shape)
     return pl.pallas_call(
         body,
         grid_spec=pltpu.PrefetchScalarGridSpec(
             num_scalar_prefetch=1,
-            grid=(1,),
+            grid=(steps,),
             in_specs=in_specs,
             out_specs=out_specs,
             scratch_shapes=list(scratch),
@@ -379,15 +380,19 @@
 
 def place_kernel(wanted, *refs):
     *terms, out_ref, summed = refs
-    for part, (own, arrived, more) in enumerate(zip(terms[::3], terms[1::3], terms[2::3])):
-        value = own[...] + arrived[0].astype(jnp.float32) + more[...].astype(jnp.float32)
-        value = value.astype(jnp.bfloat16)
-        for half, size in enumerate(SETS):
-            start = sum(SETS[:half])
-            summed[pl.ds(2 * start + part * size, size)] = value[start : start + size]
+    @pl.when(pl.program_id(0) == 0)
+    def _():
+        for part, (own, arrived, more) in enumerate(zip(terms[::3], terms[1::3], terms[2::3])):
+            value = own[...] + arrived[0].astype(jnp.float32) + more[...].astype(jnp.float32)
+            value = value.astype(jnp.bfloat16)
+            for half, size in enumerate(SETS):
+                start = sum(SETS[:half])
+                summed[pl.ds(2 * start + part * size, size)] = value[start : start + size]
+
+    first = pl.program_id(0) * out_ref.shape[0]
 
     def copy(i, carry):
-        out_ref[i] = summed[wanted[i]]
+        out_ref[i] = summed[wanted[first + i]]
         return carry
 
     lax.fori_loop(0, out_ref.shape[0], copy, 0)
@@ -406,9 +411,10 @@
         wanted,
         specs,
         terms,
-        [pl.BlockSpec(shape, lambda i, wanted: (0, 0, 0))],
+        [pl.BlockSpec((shape[0] // PLACES, *shape[1:]), lambda i, wanted: (i, 0, 0))],
         [jax.ShapeDtypeStruct(shape, jnp.bfloat16)],
         [pltpu.VMEM((2 * sum(SETS), rows, extent), jnp.bfloat16)],
+        PLACES,
     )
     return out
 
@@ -423,19 +429,18 @@
     return lax.ppermute(value, ("dp", "mp"), pairs)
 
 
-def gather_groups(mine, group, core):
+def gather_groups(halves, group, core):
     groups = lax.axis_size("mp")
     sign = 1 - 2 * core
-    mid = mine.shape[0] // 2
-    behind = [send_group(mine[:mid], 1), send_group(mine[mid:], 1)]
-    before = send_group(mine, -1)
+    size = halves[0].shape[0]
+    behind = [send_group(v, 1) for v in halves]
+    before = [send_group(v, -1) for v in halves]
     opposite = [send_group(v, 1) for v in behind]
-    out = jnp.zeros((groups,) + mine.shape, mine.dtype)
-    for away, values in ((0, [mine]), (-1, behind), (2, opposite), (1, [before])):
-        start = 0
-        for value in values:
-            out = lax.dynamic_update_slice(out, value[None], ((group + sign * away + groups) % groups, start, 0, 0))
-            start += mid
+    out = jnp.zeros((groups, size * len(halves), *halves[0].shape[1:]), halves[0].dtype)
+    for away, values in ((0, halves), (-1, behind), (2, opposite), (1, before)):
+        for k, value in enumerate(values):
+            place = ((group + sign * away + groups) % groups, size * k, 0, 0)
+            out = lax.dynamic_update_slice(out, value[None], place)
     return out
 
 
@@ -461,7 +466,8 @@
     returned = lax.all_to_all(updates, "dp", split_axis=0, concat_axis=0, tiled=True)
     returned = returned.reshape(-1, *returned.shape[2:])
     slot_of_block = jnp.arange(blocks, dtype=jnp.int32) - offsets_row[owners_row]
-    placed = returned[owners_row * slots + slot_of_block]
+    position = owners_row * slots + slot_of_block
+    placed = [returned[position[: blocks // 2]], returned[position[blocks // 2 :]]]
     return new_left[None], new_right[None], gather_groups(placed, group, core)
 
 

time: 156 us -> 155 us (level)
  starting transfers between devices: 38.8 us -> 46.2 us
  waiting for transfers between devices: 75.4 us -> 70.1 us
  Pallas kernels: 35.5 us -> 32 us
    ppermute x5 -> x6, waiting for transfers between devices: 16.2 us -> 11.1 us  [send_group(): return lax.ppermute(value, ('dp', 'mp'), pairs)]
    ppermute x5 -> x6, starting transfers between devices: 4.72 us -> 8.92 us  [send_group(): return lax.ppermute(value, ('dp', 'mp'), pairs)]
    pallas_call x1, Pallas kernels: 9.08 us -> 5.69 us  [slot_step(): pl.pallas_call(slot_kernel, grid_spec=pltpu.PrefetchScalarGridSpec(num_sc...]
    all_to_all x1, starting transfers between devices: 6.94 us -> 10.2 us  [per_device(): lax.all_to_all(updates, 'dp', split_axis=0, concat_axis=0, tiled=True)]
  transfers between devices with their start and end apart: 27 -> 28, of which waited for: 16 -> 16; matrix products, arithmetic and copies ran while one was open for 2% -> 2% of each run, Pallas kernels for 13% -> 13%
where the time goes in v5:
time: 155 us
  waiting for transfers between devices  70.1 us (45%)
  starting transfers between devices  46.2 us (30%)
  Pallas kernels  32 us (21%)
  local copies, waits for them, and re-layouts  4.85 us (3%)
    pallas_call x13, Pallas kernels, local_call(): pl.pallas_call(body, grid_spec=pltpu.PrefetchScalarGridSpec(num_scalar_pr...  26.3 us
    ppermute x12, waiting for transfers between devices, exchange(): return lax.ppermute(value, 'dp', pairs)  25.2 us
    all_to_all x1, waiting for transfers between devices, per_device(): lax.all_to_all(updates, 'dp', split_axis=0, concat_axis=0, tiled=True)  16.4 us
    ppermute x12, starting transfers between devices, exchange(): return lax.ppermute(value, 'dp', pairs)  16.4 us
    all_to_all x1, waiting for transfers between devices, per_device(): lax.all_to_all(outgoing, 'dp', split_axis=0, concat_axis=0, tiled=True)  15.8 us
    ppermute x6, waiting for transfers between devices, send_group(): return lax.ppermute(value, ('dp', 'mp'), pairs)  11.1 us
    all_to_all x1, starting transfers between devices, per_device(): lax.all_to_all(updates, 'dp', split_axis=0, concat_axis=0, tiled=True)  10.2 us
    ppermute x6, starting transfers between devices, send_group(): return lax.ppermute(value, ('dp', 'mp'), pairs)  8.92 us
  transfers between devices with their start and end apart: 28, of which 16 were waited for; matrix products, arithmetic and copies ran while one was open for 2% of the time, Pallas kernels for 13%

profile of v5, /device:TPU:0, one launch (start us, length us, event | category | flops | bytes accessed | tf_op | source)
XLA Modules:
  0.0 154.7 jit_solution(5399207178025744178)
XLA Ops:
  0.7 0.1 pad_add_fusion.pos
  0.8 2.4 %shard_map.85 = (bf16[2,10,4,16,512]{4,3,2,1,0:T(8,128)(2,1)S(1)}, bf16[2,10,4,16,512]{4,3,2,1,0:T(8,128)(2,1)S(1)}) custom-call(s32[3]{0:T(128)S(1)} %pad_add_fusion.pos, bf16[28,4,4,2,16,512]{5,4,3,2,1,0:T(8,128)(2,1)} %bitcast.46, bf16[28,4,4,2,16,512]{5,4,3,2,1,0:T(8,128)(2,1)} %bitcast.47, bf16[28,4,4,2,16,512]{5,4,3,2,1,0:T(8,128)(2,1)} %bitcast.48, ...), custom_call_target="tpu_custom_call" | custom-call | flops 5242880 | bytes 10485760 | tf_op jit(solution)/shard_map/pallas_call | solution.py:204
  3.2 0.1 collective-permute-start
  3.3 0.5 collective-permute-start.1
  3.8 1.8 %shard_map.86 = (bf16[2,4,4,16,512]{4,3,2,1,0:T(8,128)(2,1)S(1)}, bf16[2,4,4,16,512]{4,3,2,1,0:T(8,128)(2,1)S(1)}) custom-call(s32[3]{0:T(128)S(1)} %pad_add_fusion.pos, bf16[28,4,4,2,16,512]{5,4,3,2,1,0:T(8,128)(2,1)} %bitcast.50, bf16[28,4,4,2,16,512]{5,4,3,2,1,0:T(8,128)(2,1)} %bitcast.51, bf16[28,4,4,2,16,512]{5,4,3,2,1,0:T(8,128)(2,1)} %bitcast.52, ...), custom_call_target="tpu_custom_call" | custom-call | flops 2097152 | bytes 4194304 | tf_op jit(solution)/shard_map/pallas_call | solution.py:204
  5.6 2.4 %shard_map.87 = (bf16[2,10,4,16,512]{4,3,2,1,0:T(8,128)(2,1)S(1)}, bf16[2,10,4,16,512]{4,3,2,1,0:T(8,128)(2,1)S(1)}) custom-call(s32[3]{0:T(128)S(1)} %pad_add_fusion.pos, bf16[28,4,4,2,16,512]{5,4,3,2,1,0:T(8,128)(2,1)} %bitcast.54, bf16[28,4,4,2,16,512]{5,4,3,2,1,0:T(8,128)(2,1)} %bitcast.55, bf16[28,4,4,2,16,512]{5,4,3,2,1,0:T(8,128)(2,1)} %bitcast.56, ...), custom_call_target="tpu_custom_call" | custom-call | flops 5242880 | bytes 10485760 | tf_op jit(solution)/shard_map/pallas_call | solution.py:204
  8.0 0.2 collective-permute-start.6
  8.2 0.4 collective-permute-start.2
  8.6 0.1 collective-permute-start.7
  8.7 2.9 %shard_map.88 = (bf16[2,10,4,16,512]{4,3,2,1,0:T(8,128)(2,1)S(1)}, bf16[2,10,4,16,512]{4,3,2,1,0:T(8,128)(2,1)S(1)}) custom-call(s32[3]{0:T(128)S(1)} %pad_add_fusion.pos, bf16[28,4,4,2,16,512]{5,4,3,2,1,0:T(8,128)(2,1)} %bitcast.61, bf16[28,4,4,2,16,512]{5,4,3,2,1,0:T(8,128)(2,1)} %bitcast.59, bf16[28,4,4,2,16,512]{5,4,3,2,1,0:T(8,128)(2,1)} %bitcast.60, ...), custom_call_target="tpu_custom_call" | custom-call | flops 5242880 | bytes 10485760 | tf_op jit(solution)/shard_map/pallas_call | solution.py:204
  11.7 1.7 %collective-permute-start.8 = (bf16[2,10,4,16,512]{4,3,2,1,0:T(8,128)(2,1)S(1)}, bf16[2,10,4,16,512]{4,3,2,1,0:T(8,128)(2,1)S(1)}, u32[]{:S(2)}, u32[]{:S(2)}) collective-permute-start(bf16[2,10,4,16,512]{4,3,2,1,0:T(8,128)(2,1)S(1)} %get-tuple-element.86), channel_id=1, source_target_pairs={{0,8},{4,28},{8,0},{12,20},{16,24},{20,12},{24,16},{28,4},{32,40},... | collective-permute-start | bytes 3932168 | tf_op jit(solution)/shard_map/ppermute | solution.py:175
  13.4 1.9 %collective-permute-start.9 = (bf16[2,10,4,16,512]{4,3,2,1,0:T(8,128)(2,1)S(1)}, bf16[2,10,4,16,512]{4,3,2,1,0:T(8,128)(2,1)S(1)}, u32[]{:S(2)}, u32[]{:S(2)}) collective-permute-start(bf16[2,10,4,16,512]{4,3,2,1,0:T(8,128)(2,1)S(1)} %get-tuple-element.87), channel_id=1, source_target_pairs={{0,32},{4,100},{8,40},{12,108},{16,48},{20,116},{24,56},{28,124},{... | collective-permute-start | bytes 3932168 | tf_op jit(solution)/shard_map/ppermute | solution.py:175
  15.3 3.4 %collective-permute-start.3 = (bf16[2,4,4,16,512]{4,3,2,1,0:T(8,128)(2,1)S(1)}, bf16[2,4,4,16,512]{4,3,2,1,0:T(8,128)(2,1)S(1)}, u32[]{:S(2)}, u32[]{:S(2)}) collective-permute-start(bf16[2,4,4,16,512]{4,3,2,1,0:T(8,128)(2,1)S(1)} %get-tuple-element.75), channel_id=1, source_target_pairs={{0,4},{4,0},{8,12},{12,8},{16,20},{20,16},{24,28},{28,24},{32,36},... | collective-permute-start | bytes 1572872 | tf_op jit(solution)/shard_map/ppermute | solution.py:179
  18.7 1.5 collective-permute-done.3.refs_5_
  20.3 2.0 %shard_map.89 = (bf16[2,4,4,16,512]{4,3,2,1,0:T(8,128)(2,1)S(1)}, bf16[2,4,4,16,512]{4,3,2,1,0:T(8,128)(2,1)S(1)}) custom-call(s32[3]{0:T(128)S(1)} %pad_add_fusion.pos, bf16[28,4,4,2,16,512]{5,4,3,2,1,0:T(8,128)(2,1)} %bitcast.62, bf16[28,4,4,2,16,512]{5,4,3,2,1,0:T(8,128)(2,1)} %bitcast.63, bf16[28,4,4,2,16,512]{5,4,3,2,1,0:T(8,128)(2,1)} %bitcast.64, ...), custom_call_target="tpu_custom_call" | custom-call | flops 2097152 | bytes 4194304 | tf_op jit(solution)/shard_map/pallas_call | solution.py:204
  22.3 0.2 collective-permute-start.10
  22.5 1.8 %shard_map.90 = (bf16[2,4,4,16,512]{4,3,2,1,0:T(8,128)(2,1)S(1)}, bf16[2,4,4,16,512]{4,3,2,1,0:T(8,128)(2,1)S(1)}) custom-call(s32[3]{0:T(128)S(1)} %pad_add_fusion.pos, bf16[28,4,4,2,16,512]{5,4,3,2,1,0:T(8,128)(2,1)} %bitcast.66, bf16[28,4,4,2,16,512]{5,4,3,2,1,0:T(8,128)(2,1)} %bitcast.67, bf16[28,4,4,2,16,512]{5,4,3,2,1,0:T(8,128)(2,1)} %bitcast.68, ...), custom_call_target="tpu_custom_call" | custom-call | flops 2097152 | bytes 4194304 | tf_op jit(solution)/shard_map/pallas_call | solution.py:204
  24.4 1.2 collective-permute-start.4
  25.5 3.8 %collective-permute-done.8.refs_4_ = bf16[2,10,4,16,512]{4,3,2,1,0:T(8,128)(2,1)S(1)} collective-permute-done((bf16[2,10,4,16,512]{4,3,2,1,0:T(8,128)(2,1)S(1)}, bf16[2,10,4,16,512]{4,3,2,1,0:T(8,128)(2,1)S(1)}, u32[]{:S(2)}, u32[]{:S(2)}) %collective-permute-start.8) | collective-permute-done | bytes 1310752 | tf_op jit(solution)/shard_map/ppermute | solution.py:175
  29.3 0.6 collective-permute-start.5
  30.0 1.0 collective-permute-done.9.refs_5_
  31.0 2.4 %shard_map.91 = (bf16[10,4,16,512]{3,2,1,0:T(8,128)(2,1)S(1)}, bf16[10,4,16,512]{3,2,1,0:T(8,128)(2,1)S(1)}) custom-call(s32[3]{0:T(128)S(1)} %pad_add_fusion.pos, bf16[28,4,4,2,16,512]{5,4,3,2,1,0:T(8,128)(2,1)} %bitcast.70, bf16[28,4,4,2,16,512]{5,4,3,2,1,0:T(8,128)(2,1)} %bitcast.71, bf16[2,10,4,16,512]{4,3,2,1,0:T(8,128)(2,1)S(1)} %collective-permute-done.6.refs_2_, ...), custom_call_target="tpu_custom_call" | custom-call | flops 2621440 | bytes 5242880 | tf_op jit(solution)/shard_map/pallas_call | solution.py:204
  33.4 1.6 %collective-permute-done.10.refs_4_ = bf16[2,4,4,16,512]{4,3,2,1,0:T(8,128)(2,1)S(1)} collective-permute-done((bf16[2,4,4,16,512]{4,3,2,1,0:T(8,128)(2,1)S(1)}, bf16[2,4,4,16,512]{4,3,2,1,0:T(8,128)(2,1)S(1)}, u32[]{:S(2)}, u32[]{:S(2)}) %collective-permute-start.10) | collective-permute-done | bytes 524320 | tf_op jit(solution)/shard_map/ppermute | solution.py:175
  35.0 1.7 %collective-permute-done.11.refs_5_ = bf16[2,4,4,16,512]{4,3,2,1,0:T(8,128)(2,1)S(1)} collective-permute-done((bf16[2,4,4,16,512]{4,3,2,1,0:T(8,128)(2,1)S(1)}, bf16[2,4,4,16,512]{4,3,2,1,0:T(8,128)(2,1)S(1)}, u32[]{:S(2)}, u32[]{:S(2)}) %collective-permute-start.11) | collective-permute-done | bytes 524320 | tf_op jit(solution)/shard_map/ppermute | solution.py:175
  36.6 2.2 %collective-permute-start.14 = (bf16[10,4,16,512]{3,2,1,0:T(8,128)(2,1)S(1)}, bf16[10,4,16,512]{3,2,1,0:T(8,128)(2,1)S(1)}, u32[]{:S(2)}, u32[]{:S(2)}) collective-permute-start(bf16[10,4,16,512]{3,2,1,0:T(8,128)(2,1)S(1)} %get-tuple-element.100), channel_id=1, source_target_pairs={{0,24},{4,12},{8,16},{12,4},{16,8},{20,28},{24,0},{28,20},{32,56},... | collective-permute-start | bytes 1966088 | tf_op jit(solution)/shard_map/ppermute | solution.py:175
  38.8 4.0 %collective-permute-start.15 = (bf16[10,4,16,512]{3,2,1,0:T(8,128)(2,1)S(1)}, bf16[10,4,16,512]{3,2,1,0:T(8,128)(2,1)S(1)}, u32[]{:S(2)}, u32[]{:S(2)}) collective-permute-start(bf16[10,4,16,512]{3,2,1,0:T(8,128)(2,1)S(1)} %get-tuple-element.101), channel_id=1, source_target_pairs={{0,96},{4,36},{8,104},{12,44},{16,112},{20,52},{24,120},{28,60},{3... | collective-permute-start | bytes 1966088 | tf_op jit(solution)/shard_map/ppermute | solution.py:175
  42.8 1.8 %shard_map.93 = (bf16[4,4,16,512]{3,2,1,0:T(8,128)(2,1)S(1)}, bf16[4,4,16,512]{3,2,1,0:T(8,128)(2,1)S(1)}) custom-call(s32[3]{0:T(128)S(1)} %pad_add_fusion.pos, bf16[28,4,4,2,16,512]{5,4,3,2,1,0:T(8,128)(2,1)} %bitcast.72, bf16[28,4,4,2,16,512]{5,4,3,2,1,0:T(8,128)(2,1)} %bitcast.73, bf16[2,4,4,16,512]{4,3,2,1,0:T(8,128)(2,1)S(1)} %collective-permute-done.4.refs_2_, ...), custom_call_target="tpu_custom_call" | custom-call | flops 1048576 | bytes 2097152 | tf_op jit(solution)/shard_map/pallas_call | solution.py:204
  44.6 1.1 collective-permute-start.12
  45.8 1.8 %shard_map.92 = (f32[4,4,16,512]{3,2,1,0:T(8,128)S(1)}, f32[4,4,16,512]{3,2,1,0:T(8,128)S(1)}) custom-call(s32[3]{0:T(128)S(1)} %pad_add_fusion.pos, bf16[28,4,4,2,16,512]{5,4,3,2,1,0:T(8,128)(2,1)} %bitcast.74, bf16[28,4,4,2,16,512]{5,4,3,2,1,0:T(8,128)(2,1)} %bitcast.75, bf16[2,4,4,16,512]{4,3,2,1,0:T(8,128)(2,1)S(1)} %collective-permute-done.4.refs_2_, ...), custom_call_target="tpu_custom_call" | custom-call | flops 1048576 | bytes 2097152 | tf_op jit(solution)/shard_map/pallas_call | solution.py:204
  47.5 2.5 %shard_map.94 = (f32[10,4,16,512]{3,2,1,0:T(8,128)S(1)}, f32[10,4,16,512]{3,2,1,0:T(8,128)S(1)}) custom-call(s32[3]{0:T(128)S(1)} %pad_add_fusion.pos, bf16[28,4,4,2,16,512]{5,4,3,2,1,0:T(8,128)(2,1)} %bitcast.76, bf16[28,4,4,2,16,512]{5,4,3,2,1,0:T(8,128)(2,1)} %bitcast.77, bf16[2,10,4,16,512]{4,3,2,1,0:T(8,128)(2,1)S(1)} %collective-permute-done.6.refs_2_, ...), custom_call_target="tpu_custom_call" | custom-call | flops 2621440 | bytes 5242880 | tf_op jit(solution)/shard_map/pallas_call | solution.py:204
  50.0 1.4 collective-permute-done.15.refs_3_
  51.4 1.0 shard_map.95
  52.4 1.8 %collective-permute-done.13.refs_3_ = bf16[4,4,16,512]{3,2,1,0:T(8,128)(2,1)S(1)} collective-permute-done((bf16[4,4,16,512]{3,2,1,0:T(8,128)(2,1)S(1)}, bf16[4,4,16,512]{3,2,1,0:T(8,128)(2,1)S(1)}, u32[]{:S(2)}, u32[]{:S(2)}) %collective-permute-start.13) | collective-permute-done | bytes 262176 | tf_op jit(solution)/shard_map/ppermute | solution.py:175
  54.2 1.5 shard_map.96
  55.8 0.7 collective-permute-start.18
  56.4 8.0 %collective-permute-done.16.refs_1_ = bf16[2,14,16,512]{3,2,1,0:T(8,128)(2,1)S(1)} collective-permute-done((bf16[2,14,16,512]{3,2,1,0:T(8,128)(2,1)}, bf16[2,14,16,512]{3,2,1,0:T(8,128)(2,1)S(1)}, u32[]{:S(2)}, u32[]{:S(2)}) %collective-permute-start.16) | collective-permute-done | bytes 458784 | tf_op jit(solution)/shard_map/ppermute | solution.py:175
  64.5 3.3 %collective-permute-start.17 = (bf16[14,16,512]{2,1,0:T(8,128)(2,1)S(1)}, bf16[14,16,512]{2,1,0:T(8,128)(2,1)S(1)}, u32[]{:S(2)}, u32[]{:S(2)}) collective-permute-start(bf16[14,16,512]{2,1,0:T(8,128)(2,1)S(1)} %fusion.1), channel_id=1, source_target_pairs={{0,96},{4,36},{8,104},{12,44},{16,112},{20,52},{24,120},{28,60},{3... | collective-permute-start | bytes 688136 | tf_op jit(solution)/shard_map/ppermute | solution.py:175
  67.9 1.1 collective-permute-start.19
  69.0 0.1 add_minimum_fusion
  69.1 0.1 min.12.wanted
  69.2 2.6 %collective-permute-done.17.refs_2_ = bf16[14,16,512]{2,1,0:T(8,128)(2,1)S(1)} collective-permute-done((bf16[14,16,512]{2,1,0:T(8,128)(2,1)S(1)}, bf16[14,16,512]{2,1,0:T(8,128)(2,1)S(1)}, u32[]{:S(2)}, u32[]{:S(2)}) %collective-permute-start.17) | collective-permute-done | bytes 229408 | tf_op jit(solution)/shard_map/ppermute | solution.py:175
  71.8 3.4 %collective-permute-done.19.refs_5_ = bf16[14,16,512]{2,1,0:T(8,128)(2,1)S(1)} collective-permute-done((bf16[14,16,512]{2,1,0:T(8,128)(2,1)S(1)}, bf16[14,16,512]{2,1,0:T(8,128)(2,1)S(1)}, u32[]{:S(2)}, u32[]{:S(2)}) %collective-permute-start.19) | collective-permute-done | bytes 229408 | tf_op jit(solution)/shard_map/ppermute | solution.py:175
  75.2 2.0 %shard_map.97 = bf16[64,16,512]{2,1,0:T(8,128)(2,1)} custom-call(s32[64]{0:T(128)S(1)} %min.12.wanted, f32[14,16,512]{2,1,0:T(8,128)S(1)} %get-tuple-element.108.refs_0_, bf16[2,14,16,512]{3,2,1,0:T(8,128)(2,1)S(1)} %collective-permute-done.16.refs_1_, bf16[14,16,512]{2,1,0:T(8,128)(2,1)S(1)} %collective-permute-done.17.refs_2_, ...), custom_call_target="tpu_custom_call" | custom-call | flops 2097152 | bytes 4194304 | tf_op jit(solution)/shard_map/pallas_call | solution.py:204
  77.2 4.2 %all-to-all-start = ((bf16[32,2,16,512]{3,2,1,0:T(8,128)(2,1)}), bf16[32,2,16,512]{3,2,1,0:T(8,128)(2,1)S(1)}, u32[]{:S(2)}, u32[]{:S(2)}) async-start(bf16[32,2,16,512]{3,2,1,0:T(8,128)(2,1)} %bitcast.8), calls=%async_computation | async-start | bytes 2097152 | tf_op jit(solution)/shard_map/all_to_all | solution.py:463
  81.4 1.3 dynamic_slice.14
  82.7 15.8 %all-to-all-done.block_ref = bf16[32,2,16,512]{3,2,1,0:T(8,128)(2,1)S(1)} async-done(((bf16[32,2,16,512]{3,2,1,0:T(8,128)(2,1)}), bf16[32,2,16,512]{3,2,1,0:T(8,128)(2,1)S(1)}, u32[]{:S(2)}, u32[]{:S(2)}) %all-to-all-start) | async-done | bytes 1048608 | tf_op jit(solution)/shard_map/all_to_all | solution.py:463
  98.6 5.7 %shard_map.98 = (f32[2,512,512]{2,1,0:T(8,128)}, f32[2,512,512]{2,1,0:T(8,128)}, bf16[32,2,16,512]{3,2,1,0:T(8,128)(2,1)}) custom-call(s32[1]{0:T(128)} %bitcast.count_ref, bf16[32,2,16,512]{3,2,1,0:T(8,128)(2,1)S(1)} %all-to-all-done.block_ref, f32[2,512,512]{2,1,0:T(8,128)S(1)} %bitcast.45, f32[2,512,512]{2,1,0:T(8,128)} %bitcast.80), custom_call_target="tpu_custom_call" | custom-call | flops 9663676416 | bytes 10485760 | tf_op jit(solution)/shard_map/pallas_call | solution.py:123
  104.3 10.2 %all-to-all-start.1 = ((bf16[32,2,16,512]{3,2,1,0:T(8,128)(2,1)}), bf16[32,2,16,512]{3,2,1,0:T(8,128)(2,1)S(1)}, u32[]{:S(2)}, u32[]{:S(2)}) async-start(bf16[32,2,16,512]{3,2,1,0:T(8,128)(2,1)} %get-tuple-element.116), calls=%async_computation.1 | async-start | bytes 2097152 | tf_op jit(solution)/shard_map/all_to_all | solution.py:466
  114.6 0.7 gather_fusion
  115.4 16.4 %all-to-all-done.1 = bf16[32,2,16,512]{3,2,1,0:T(8,128)(2,1)S(1)} async-done(((bf16[32,2,16,512]{3,2,1,0:T(8,128)(2,1)}), bf16[32,2,16,512]{3,2,1,0:T(8,128)(2,1)S(1)}, u32[]{:S(2)}, u32[]{:S(2)}) %all-to-all-start.1) | async-done | bytes 1048608 | tf_op jit(solution)/shard_map/all_to_all | solution.py:466
  131.8 0.6 gather_fusion.1
  132.4 1.6 %collective-permute-start.20 = (bf16[14,16,512]{2,1,0:T(8,128)(2,1)S(1)}, bf16[14,16,512]{2,1,0:T(8,128)(2,1)S(1)}, u32[]{:S(2)}, u32[]{:S(2)}) collective-permute-start(bf16[14,16,512]{2,1,0:T(8,128)(2,1)S(1)} %gather_fusion.1), channel_id=1, source_target_pairs={{0,1},{1,2},{2,3},{3,0},{4,7},{5,4},{6,5},{7,6},{8,9},{9,10},{10,1... | collective-permute-start | bytes 688136 | tf_op jit(solution)/shard_map/ppermute | solution.py:429
  134.0 1.7 %collective-permute-start.24 = (bf16[14,16,512]{2,1,0:T(8,128)(2,1)S(1)}, bf16[14,16,512]{2,1,0:T(8,128)(2,1)S(1)}, u32[]{:S(2)}, u32[]{:S(2)}) collective-permute-start(bf16[14,16,512]{2,1,0:T(8,128)(2,1)S(1)} %gather_fusion.1), channel_id=1, source_target_pairs={{0,3},{1,0},{2,1},{3,2},{4,5},{5,6},{6,7},{7,4},{8,11},{9,8},{10,9... | collective-permute-start | bytes 688136 | tf_op jit(solution)/shard_map/ppermute | solution.py:429
  135.7 0.6 gather_fusion.2
  136.3 0.4 collective-permute-start.21
  136.6 2.9 %collective-permute-start.25 = (bf16[14,16,512]{2,1,0:T(8,128)(2,1)S(1)}, bf16[14,16,512]{2,1,0:T(8,128)(2,1)S(1)}, u32[]{:S(2)}, u32[]{:S(2)}) collective-permute-start(bf16[14,16,512]{2,1,0:T(8,128)(2,1)S(1)} %gather_fusion.2), channel_id=1, source_target_pairs={{0,3},{1,0},{2,1},{3,2},{4,5},{5,6},{6,7},{7,4},{8,11},{9,8},{10,9... | collective-permute-start | bytes 688136 | tf_op jit(solution)/shard_map/ppermute | solution.py:429
  139.6 0.2 broadcast_in_dim.44
  139.9 0.4 collective-permute-done.20
  140.3 1.6 %collective-permute-start.22 = (bf16[14,16,512]{2,1,0:T(8,128)(2,1)S(1)}, bf16[14,16,512]{2,1,0:T(8,128)(2,1)S(1)}, u32[]{:S(2)}, u32[]{:S(2)}) collective-permute-start(bf16[14,16,512]{2,1,0:T(8,128)(2,1)S(1)} %collective-permute-done.20), channel_id=1, source_target_pairs={{0,1},{1,2},{2,3},{3,0},{4,7},{5,4},{6,5},{7,6},{8,9},{9,10},{10,1... | collective-permute-start | bytes 688136 | tf_op jit(solution)/shard_map/ppermute | solution.py:429
  141.9 4.2 %collective-permute-done.21 = bf16[14,16,512]{2,1,0:T(8,128)(2,1)S(1)} collective-permute-done((bf16[14,16,512]{2,1,0:T(8,128)(2,1)S(1)}, bf16[14,16,512]{2,1,0:T(8,128)(2,1)S(1)}, u32[]{:S(2)}, u32[]{:S(2)}) %collective-permute-start.21) | collective-permute-done | bytes 229408 | tf_op jit(solution)/shard_map/ppermute | solution.py:429
  146.1 0.7 collective-permute-start.23
  146.8 2.7 %collective-permute-done.22 = bf16[14,16,512]{2,1,0:T(8,128)(2,1)S(1)} collective-permute-done((bf16[14,16,512]{2,1,0:T(8,128)(2,1)S(1)}, bf16[14,16,512]{2,1,0:T(8,128)(2,1)S(1)}, u32[]{:S(2)}, u32[]{:S(2)}) %collective-permute-start.22) | collective-permute-done | bytes 229408 | tf_op jit(solution)/shard_map/ppermute | solution.py:429
  149.6 3.8 %collective-permute-done.23 = bf16[14,16,512]{2,1,0:T(8,128)(2,1)S(1)} collective-permute-done((bf16[14,16,512]{2,1,0:T(8,128)(2,1)S(1)}, bf16[14,16,512]{2,1,0:T(8,128)(2,1)S(1)}, u32[]{:S(2)}, u32[]{:S(2)}) %collective-permute-start.23) | collective-permute-done | bytes 229408 | tf_op jit(solution)/shard_map/ppermute | solution.py:429
  153.5 1.2 copy-done.3
  (41 shorter events, 0.5 us)
Async XLA Ops:
  0.6 68.4 %copy-start = (s32[4,32]{1,0:T(4,128)S(1)}, s32[4,32]{1,0:T(4,128)}, u32[]{:S(2)}) copy-start(s32[4,32]{1,0:T(4,128)} %param.11) | copy-start | bytes 1540
  3.2 5.5 %collective-permute-start = (bf16[2,10,4,16,512]{4,3,2,1,0:T(8,128)(2,1)S(1)}, bf16[2,10,4,16,512]{4,3,2,1,0:T(8,128)(2,1)S(1)}, u32[]{:S(2)}, u32[]{:S(2)}) collective-permute-start(bf16[2,10,4,16,512]{4,3,2,1,0:T(8,128)(2,1)S(1)} %get-tuple-element.69), channel_id=1, source_target_pairs={{0,4},{4,0},{8,12},{12,8},{16,20},{20,16},{24,28},{28,24},{32,36},... | collective-permute-start | bytes 3932168 | tf_op jit(solution)/shard_map/ppermute | solution.py:179
  3.3 5.4 %collective-permute-start.1 = (bf16[2,10,4,16,512]{4,3,2,1,0:T(8,128)(2,1)S(1)}, bf16[2,10,4,16,512]{4,3,2,1,0:T(8,128)(2,1)S(1)}, u32[]{:S(2)}, u32[]{:S(2)}) collective-permute-start(bf16[2,10,4,16,512]{4,3,2,1,0:T(8,128)(2,1)S(1)} %get-tuple-element.70), channel_id=1, source_target_pairs={{0,4},{4,0},{8,12},{12,8},{16,20},{20,16},{24,28},{28,24},{32,36},... | collective-permute-start | bytes 3932168 | tf_op jit(solution)/shard_map/ppermute | solution.py:179
  8.0 14.5 %collective-permute-start.6 = (bf16[2,10,4,16,512]{4,3,2,1,0:T(8,128)(2,1)S(1)}, bf16[2,10,4,16,512]{4,3,2,1,0:T(8,128)(2,1)S(1)}, u32[]{:S(2)}, u32[]{:S(2)}) collective-permute-start(bf16[2,10,4,16,512]{4,3,2,1,0:T(8,128)(2,1)S(1)} %get-tuple-element.84), channel_id=1, source_target_pairs={{0,4},{4,0},{8,12},{12,8},{16,20},{20,16},{24,28},{28,24},{32,36},... | collective-permute-start | bytes 3932168 | tf_op jit(solution)/shard_map/ppermute | solution.py:179
  8.2 7.1 %collective-permute-start.2 = (bf16[2,4,4,16,512]{4,3,2,1,0:T(8,128)(2,1)S(1)}, bf16[2,4,4,16,512]{4,3,2,1,0:T(8,128)(2,1)S(1)}, u32[]{:S(2)}, u32[]{:S(2)}) collective-permute-start(bf16[2,4,4,16,512]{4,3,2,1,0:T(8,128)(2,1)S(1)} %get-tuple-element.74), channel_id=1, source_target_pairs={{0,4},{4,0},{8,12},{12,8},{16,20},{20,16},{24,28},{28,24},{32,36},... | collective-permute-start | bytes 1572872 | tf_op jit(solution)/shard_map/ppermute | solution.py:179
  8.6 15.7 %collective-permute-start.7 = (bf16[2,10,4,16,512]{4,3,2,1,0:T(8,128)(2,1)S(1)}, bf16[2,10,4,16,512]{4,3,2,1,0:T(8,128)(2,1)S(1)}, u32[]{:S(2)}, u32[]{:S(2)}) collective-permute-start(bf16[2,10,4,16,512]{4,3,2,1,0:T(8,128)(2,1)S(1)} %get-tuple-element.85), channel_id=1, source_target_pairs={{0,4},{4,0},{8,12},{12,8},{16,20},{20,16},{24,28},{28,24},{32,36},... | collective-permute-start | bytes 3932168 | tf_op jit(solution)/shard_map/ppermute | solution.py:179
  11.7 17.7 %collective-permute-start.8 = (bf16[2,10,4,16,512]{4,3,2,1,0:T(8,128)(2,1)S(1)}, bf16[2,10,4,16,512]{4,3,2,1,0:T(8,128)(2,1)S(1)}, u32[]{:S(2)}, u32[]{:S(2)}) collective-permute-start(bf16[2,10,4,16,512]{4,3,2,1,0:T(8,128)(2,1)S(1)} %get-tuple-element.86), channel_id=1, source_target_pairs={{0,8},{4,28},{8,0},{12,20},{16,24},{20,12},{24,16},{28,4},{32,40},... | collective-permute-start | bytes 3932168 | tf_op jit(solution)/shard_map/ppermute | solution.py:175
  13.4 17.6 %collective-permute-start.9 = (bf16[2,10,4,16,512]{4,3,2,1,0:T(8,128)(2,1)S(1)}, bf16[2,10,4,16,512]{4,3,2,1,0:T(8,128)(2,1)S(1)}, u32[]{:S(2)}, u32[]{:S(2)}) collective-permute-start(bf16[2,10,4,16,512]{4,3,2,1,0:T(8,128)(2,1)S(1)} %get-tuple-element.87), channel_id=1, source_target_pairs={{0,32},{4,100},{8,40},{12,108},{16,48},{20,116},{24,56},{28,124},{... | collective-permute-start | bytes 3932168 | tf_op jit(solution)/shard_map/ppermute | solution.py:175
  15.3 5.0 %collective-permute-start.3 = (bf16[2,4,4,16,512]{4,3,2,1,0:T(8,128)(2,1)S(1)}, bf16[2,4,4,16,512]{4,3,2,1,0:T(8,128)(2,1)S(1)}, u32[]{:S(2)}, u32[]{:S(2)}) collective-permute-start(bf16[2,4,4,16,512]{4,3,2,1,0:T(8,128)(2,1)S(1)} %get-tuple-element.75), channel_id=1, source_target_pairs={{0,4},{4,0},{8,12},{12,8},{16,20},{20,16},{24,28},{28,24},{32,36},... | collective-permute-start | bytes 1572872 | tf_op jit(solution)/shard_map/ppermute | solution.py:179
  22.3 12.7 %collective-permute-start.10 = (bf16[2,4,4,16,512]{4,3,2,1,0:T(8,128)(2,1)S(1)}, bf16[2,4,4,16,512]{4,3,2,1,0:T(8,128)(2,1)S(1)}, u32[]{:S(2)}, u32[]{:S(2)}) collective-permute-start(bf16[2,4,4,16,512]{4,3,2,1,0:T(8,128)(2,1)S(1)} %get-tuple-element.90), channel_id=1, source_target_pairs={{0,8},{4,28},{8,0},{12,20},{16,24},{20,12},{24,16},{28,4},{32,40},... | collective-permute-start | bytes 1572872 | tf_op jit(solution)/shard_map/ppermute | solution.py:175
  22.5 14.1 %collective-permute-start.11 = (bf16[2,4,4,16,512]{4,3,2,1,0:T(8,128)(2,1)S(1)}, bf16[2,4,4,16,512]{4,3,2,1,0:T(8,128)(2,1)S(1)}, u32[]{:S(2)}, u32[]{:S(2)}) collective-permute-start(bf16[2,4,4,16,512]{4,3,2,1,0:T(8,128)(2,1)S(1)} %get-tuple-element.91), channel_id=1, source_target_pairs={{0,32},{4,100},{8,40},{12,108},{16,48},{20,116},{24,56},{28,124},{... | collective-permute-start | bytes 1572872 | tf_op jit(solution)/shard_map/ppermute | solution.py:175
  24.4 18.5 %collective-permute-start.4 = (bf16[2,4,4,16,512]{4,3,2,1,0:T(8,128)(2,1)S(1)}, bf16[2,4,4,16,512]{4,3,2,1,0:T(8,128)(2,1)S(1)}, u32[]{:S(2)}, u32[]{:S(2)}) collective-permute-start(bf16[2,4,4,16,512]{4,3,2,1,0:T(8,128)(2,1)S(1)} %get-tuple-element.82), channel_id=1, source_target_pairs={{0,4},{4,0},{8,12},{12,8},{16,20},{20,16},{24,28},{28,24},{32,36},... | collective-permute-start | bytes 1572872 | tf_op jit(solution)/shard_map/ppermute | solution.py:179
  29.3 13.5 %collective-permute-start.5 = (bf16[2,4,4,16,512]{4,3,2,1,0:T(8,128)(2,1)S(1)}, bf16[2,4,4,16,512]{4,3,2,1,0:T(8,128)(2,1)S(1)}, u32[]{:S(2)}, u32[]{:S(2)}) collective-permute-start(bf16[2,4,4,16,512]{4,3,2,1,0:T(8,128)(2,1)S(1)} %get-tuple-element.83), channel_id=1, source_target_pairs={{0,4},{4,0},{8,12},{12,8},{16,20},{20,16},{24,28},{28,24},{32,36},... | collective-permute-start | bytes 1572872 | tf_op jit(solution)/shard_map/ppermute | solution.py:179
  31.0 2.4 %copy-start.1 = (bf16[2,10,4,16,512]{4,3,2,1,0:T(8,128)(2,1)}, bf16[2,10,4,16,512]{4,3,2,1,0:T(8,128)(2,1)S(1)}, u32[]{:S(2)}) copy-start(bf16[2,10,4,16,512]{4,3,2,1,0:T(8,128)(2,1)S(1)} %collective-permute-done.9.refs_5_) | copy-start | bytes 3932164
  36.6 13.4 %collective-permute-start.14 = (bf16[10,4,16,512]{3,2,1,0:T(8,128)(2,1)S(1)}, bf16[10,4,16,512]{3,2,1,0:T(8,128)(2,1)S(1)}, u32[]{:S(2)}, u32[]{:S(2)}) collective-permute-start(bf16[10,4,16,512]{3,2,1,0:T(8,128)(2,1)S(1)} %get-tuple-element.100), channel_id=1, source_target_pairs={{0,24},{4,12},{8,16},{12,4},{16,8},{20,28},{24,0},{28,20},{32,56},... | collective-permute-start | bytes 1966088 | tf_op jit(solution)/shard_map/ppermute | solution.py:175
  38.8 12.6 %collective-permute-start.15 = (bf16[10,4,16,512]{3,2,1,0:T(8,128)(2,1)S(1)}, bf16[10,4,16,512]{3,2,1,0:T(8,128)(2,1)S(1)}, u32[]{:S(2)}, u32[]{:S(2)}) collective-permute-start(bf16[10,4,16,512]{3,2,1,0:T(8,128)(2,1)S(1)} %get-tuple-element.101), channel_id=1, source_target_pairs={{0,96},{4,36},{8,104},{12,44},{16,112},{20,52},{24,120},{28,60},{3... | collective-permute-start | bytes 1966088 | tf_op jit(solution)/shard_map/ppermute | solution.py:175
  44.6 7.8 %collective-permute-start.12 = (bf16[4,4,16,512]{3,2,1,0:T(8,128)(2,1)S(1)}, bf16[4,4,16,512]{3,2,1,0:T(8,128)(2,1)S(1)}, u32[]{:S(2)}, u32[]{:S(2)}) collective-permute-start(bf16[4,4,16,512]{3,2,1,0:T(8,128)(2,1)S(1)} %get-tuple-element.96), channel_id=1, source_target_pairs={{0,24},{4,12},{8,16},{12,4},{16,8},{20,28},{24,0},{28,20},{32,56},... | collective-permute-start | bytes 786440 | tf_op jit(solution)/shard_map/ppermute | solution.py:175
  45.8 8.4 %collective-permute-start.13 = (bf16[4,4,16,512]{3,2,1,0:T(8,128)(2,1)S(1)}, bf16[4,4,16,512]{3,2,1,0:T(8,128)(2,1)S(1)}, u32[]{:S(2)}, u32[]{:S(2)}) collective-permute-start(bf16[4,4,16,512]{3,2,1,0:T(8,128)(2,1)S(1)} %get-tuple-element.97), channel_id=1, source_target_pairs={{0,96},{4,36},{8,104},{12,44},{16,112},{20,52},{24,120},{28,60},{3... | collective-permute-start | bytes 786440 | tf_op jit(solution)/shard_map/ppermute | solution.py:175
  55.8 8.7 %collective-permute-start.16 = (bf16[2,14,16,512]{3,2,1,0:T(8,128)(2,1)}, bf16[2,14,16,512]{3,2,1,0:T(8,128)(2,1)S(1)}, u32[]{:S(2)}, u32[]{:S(2)}) collective-permute-start(bf16[2,14,16,512]{3,2,1,0:T(8,128)(2,1)} %get-tuple-element.109), channel_id=1, source_target_pairs={{0,32},{4,100},{8,40},{12,108},{16,48},{20,116},{24,56},{28,124},{... | collective-permute-start | bytes 1376264 | tf_op jit(solution)/shard_map/ppermute | solution.py:175
  55.8 12.1 %collective-permute-start.18 = (bf16[2,14,16,512]{3,2,1,0:T(8,128)(2,1)S(1)}, bf16[2,14,16,512]{3,2,1,0:T(8,128)(2,1)S(1)}, u32[]{:S(2)}, u32[]{:S(2)}) collective-permute-start(bf16[2,14,16,512]{3,2,1,0:T(8,128)(2,1)S(1)} %get-tuple-element.112), channel_id=1, source_target_pairs={{0,8},{4,28},{8,0},{12,20},{16,24},{20,12},{24,16},{28,4},{32,40},... | collective-permute-start | bytes 1376264 | tf_op jit(solution)/shard_map/ppermute | solution.py:175
  64.5 7.3 %collective-permute-start.17 = (bf16[14,16,512]{2,1,0:T(8,128)(2,1)S(1)}, bf16[14,16,512]{2,1,0:T(8,128)(2,1)S(1)}, u32[]{:S(2)}, u32[]{:S(2)}) collective-permute-start(bf16[14,16,512]{2,1,0:T(8,128)(2,1)S(1)} %fusion.1), channel_id=1, source_target_pairs={{0,96},{4,36},{8,104},{12,44},{16,112},{20,52},{24,120},{28,60},{3... | collective-permute-start | bytes 688136 | tf_op jit(solution)/shard_map/ppermute | solution.py:175
  67.9 7.3 %collective-permute-start.19 = (bf16[14,16,512]{2,1,0:T(8,128)(2,1)S(1)}, bf16[14,16,512]{2,1,0:T(8,128)(2,1)S(1)}, u32[]{:S(2)}, u32[]{:S(2)}) collective-permute-start(bf16[14,16,512]{2,1,0:T(8,128)(2,1)S(1)} %fusion), channel_id=1, source_target_pairs={{0,24},{4,12},{8,16},{12,4},{16,8},{20,28},{24,0},{28,20},{32,56},... | collective-permute-start | bytes 688136 | tf_op jit(solution)/shard_map/ppermute | solution.py:175
  77.2 21.4 %copy-start.2 = (f32[1,2,512,512]{3,2,1,0:T(8,128)S(1)}, f32[1,2,512,512]{3,2,1,0:T(8,128)}, u32[]{:S(2)}) copy-start(f32[1,2,512,512]{3,2,1,0:T(8,128)} %param.7) | copy-start | bytes 6291460
  77.2 21.4 %all-to-all-start = ((bf16[32,2,16,512]{3,2,1,0:T(8,128)(2,1)}), bf16[32,2,16,512]{3,2,1,0:T(8,128)(2,1)S(1)}, u32[]{:S(2)}, u32[]{:S(2)}) async-start(bf16[32,2,16,512]{3,2,1,0:T(8,128)(2,1)} %bitcast.8), calls=%async_computation | async-start | bytes 2097152 | tf_op jit(solution)/shard_map/all_to_all | solution.py:463
  104.3 10.3 %copy-start.4 = (s32[4,28]{1,0:T(4,128)S(1)}, s32[4,28]{1,0:T(4,128)}, u32[]{:S(2)}) copy-start(s32[4,28]{1,0:T(4,128)} %param.9) | copy-start | bytes 1348
  104.3 27.6 %all-to-all-start.1 = ((bf16[32,2,16,512]{3,2,1,0:T(8,128)(2,1)}), bf16[32,2,16,512]{3,2,1,0:T(8,128)(2,1)S(1)}, u32[]{:S(2)}, u32[]{:S(2)}) async-start(bf16[32,2,16,512]{3,2,1,0:T(8,128)(2,1)} %get-tuple-element.116), calls=%async_computation.1 | async-start | bytes 2097152 | tf_op jit(solution)/shard_map/all_to_all | solution.py:466
  132.4 7.8 %collective-permute-start.20 = (bf16[14,16,512]{2,1,0:T(8,128)(2,1)S(1)}, bf16[14,16,512]{2,1,0:T(8,128)(2,1)S(1)}, u32[]{:S(2)}, u32[]{:S(2)}) collective-permute-start(bf16[14,16,512]{2,1,0:T(8,128)(2,1)S(1)} %gather_fusion.1), channel_id=1, source_target_pairs={{0,1},{1,2},{2,3},{3,0},{4,7},{5,4},{6,5},{7,6},{8,9},{9,10},{10,1... | collective-permute-start | bytes 688136 | tf_op jit(solution)/shard_map/ppermute | solution.py:429
  134.0 19.4 %collective-permute-start.24 = (bf16[14,16,512]{2,1,0:T(8,128)(2,1)S(1)}, bf16[14,16,512]{2,1,0:T(8,128)(2,1)S(1)}, u32[]{:S(2)}, u32[]{:S(2)}) collective-permute-start(bf16[14,16,512]{2,1,0:T(8,128)(2,1)S(1)} %gather_fusion.1), channel_id=1, source_target_pairs={{0,3},{1,0},{2,1},{3,2},{4,5},{5,6},{6,7},{7,4},{8,11},{9,8},{10,9... | collective-permute-start | bytes 688136 | tf_op jit(solution)/shard_map/ppermute | solution.py:429
  136.3 9.8 %collective-permute-start.21 = (bf16[14,16,512]{2,1,0:T(8,128)(2,1)S(1)}, bf16[14,16,512]{2,1,0:T(8,128)(2,1)S(1)}, u32[]{:S(2)}, u32[]{:S(2)}) collective-permute-start(bf16[14,16,512]{2,1,0:T(8,128)(2,1)S(1)} %gather_fusion.2), channel_id=1, source_target_pairs={{0,1},{1,2},{2,3},{3,0},{4,7},{5,4},{6,5},{7,6},{8,9},{9,10},{10,1... | collective-permute-start | bytes 688136 | tf_op jit(solution)/shard_map/ppermute | solution.py:429
  136.6 16.8 %collective-permute-start.25 = (bf16[14,16,512]{2,1,0:T(8,128)(2,1)S(1)}, bf16[14,16,512]{2,1,0:T(8,128)(2,1)S(1)}, u32[]{:S(2)}, u32[]{:S(2)}) collective-permute-start(bf16[14,16,512]{2,1,0:T(8,128)(2,1)S(1)} %gather_fusion.2), channel_id=1, source_target_pairs={{0,3},{1,0},{2,1},{3,2},{4,5},{5,6},{6,7},{7,4},{8,11},{9,8},{10,9... | collective-permute-start | bytes 688136 | tf_op jit(solution)/shard_map/ppermute | solution.py:429
  140.3 9.3 %collective-permute-start.22 = (bf16[14,16,512]{2,1,0:T(8,128)(2,1)S(1)}, bf16[14,16,512]{2,1,0:T(8,128)(2,1)S(1)}, u32[]{:S(2)}, u32[]{:S(2)}) collective-permute-start(bf16[14,16,512]{2,1,0:T(8,128)(2,1)S(1)} %collective-permute-done.20), channel_id=1, source_target_pairs={{0,1},{1,2},{2,3},{3,0},{4,7},{5,4},{6,5},{7,6},{8,9},{9,10},{10,1... | collective-permute-start | bytes 688136 | tf_op jit(solution)/shard_map/ppermute | solution.py:429
  146.1 7.2 %collective-permute-start.23 = (bf16[14,16,512]{2,1,0:T(8,128)(2,1)S(1)}, bf16[14,16,512]{2,1,0:T(8,128)(2,1)S(1)}, u32[]{:S(2)}, u32[]{:S(2)}) collective-permute-start(bf16[14,16,512]{2,1,0:T(8,128)(2,1)S(1)} %collective-permute-done.21), channel_id=1, source_target_pairs={{0,1},{1,2},{2,3},{3,0},{4,7},{5,4},{6,5},{7,6},{8,9},{9,10},{10,1... | collective-permute-start | bytes 688136 | tf_op jit(solution)/shard_map/ppermute | solution.py:429
  153.4 1.2 copy-start.3

commit v6 on v5

--- a/solution.py
+++ b/solution.py
@@ -363,9 +363,7 @@
     for half in halves:
         sums = second_sums(left, pos, half, late[half], direct[half])
         if half + 1 < len(SETS):
-            count = len(sums)
-            both = lax.optimization_barrier((*sums, *direct[half + 1]))
-            sums, direct[half + 1] = both[:count], both[count:]
+            *sums, direct[half + 1][0] = lax.optimization_barrier((*sums, direct[half + 1][0]))
         joined.append([exchange(v, 1 - part, 1) for part, v in zip(parts, sums)])
     rest = [rest_sums(left, pos, half, late[half], direct[half]) for half in halves]
     for half in halves:

time: 155 us -> 156 us (level)
  starting transfers between devices: 46.2 us -> 50.2 us
  waiting for transfers between devices: 70.1 us -> 66.3 us
    ppermute x12, starting transfers between devices: 16.4 us -> 20.9 us  [exchange(): return lax.ppermute(value, 'dp', pairs)]
    ppermute x12, waiting for transfers between devices: 25.2 us -> 22.4 us  [exchange(): return lax.ppermute(value, 'dp', pairs)]
  transfers between devices with their start and end apart: 28 -> 28, of which waited for: 16 -> 13; matrix products, arithmetic and copies ran while one was open for 2% -> 2% of each run, Pallas kernels for 13% -> 13%
where the time goes in v6:
time: 156 us; the launch traced here: 155 us
  waiting for transfers between devices  66.3 us (42%)
  starting transfers between devices  50.2 us (32%)
  Pallas kernels  32 us (21%)
  local copies, waits for them, and re-layouts  4.86 us (3%)
    pallas_call x13, Pallas kernels, local_call(): pl.pallas_call(body, grid_spec=pltpu.PrefetchScalarGridSpec(num_scalar_pr...  26.3 us
    ppermute x12, waiting for transfers between devices, exchange(): return lax.ppermute(value, 'dp', pairs)  22.4 us
    ppermute x12, starting transfers between devices, exchange(): return lax.ppermute(value, 'dp', pairs)  20.9 us
    all_to_all x1, waiting for transfers between devices, per_device(): lax.all_to_all(updates, 'dp', split_axis=0, concat_axis=0, tiled=True)  16.4 us
    all_to_all x1, waiting for transfers between devices, per_device(): lax.all_to_all(outgoing, 'dp', split_axis=0, concat_axis=0, tiled=True)  15.8 us
    ppermute x6, waiting for transfers between devices, send_group(): return lax.ppermute(value, ('dp', 'mp'), pairs)  10.1 us
    all_to_all x1, starting transfers between devices, per_device(): lax.all_to_all(updates, 'dp', split_axis=0, concat_axis=0, tiled=True)  9.92 us
    ppermute x6, starting transfers between devices, send_group(): return lax.ppermute(value, ('dp', 'mp'), pairs)  9.86 us
  transfers between devices with their start and end apart: 28, of which 13 were waited for; matrix products, arithmetic and copies ran while one was open for 2% of the time, Pallas kernels for 13%

profile of v6, /device:TPU:0, one launch (start us, length us, event | category | flops | bytes accessed | tf_op | source)
XLA Modules:
  0.0 154.9 jit_solution(960120158417233734)
XLA Ops:
  0.7 0.1 pad_add_fusion.pos
  0.8 2.4 %shard_map.85 = (bf16[2,10,4,16,512]{4,3,2,1,0:T(8,128)(2,1)S(1)}, bf16[2,10,4,16,512]{4,3,2,1,0:T(8,128)(2,1)S(1)}) custom-call(s32[3]{0:T(128)S(1)} %pad_add_fusion.pos, bf16[28,4,4,2,16,512]{5,4,3,2,1,0:T(8,128)(2,1)} %bitcast.46, bf16[28,4,4,2,16,512]{5,4,3,2,1,0:T(8,128)(2,1)} %bitcast.47, bf16[28,4,4,2,16,512]{5,4,3,2,1,0:T(8,128)(2,1)} %bitcast.48, ...), custom_call_target="tpu_custom_call" | custom-call | flops 5242880 | bytes 10485760 | tf_op jit(solution)/shard_map/pallas_call | solution.py:204
  3.2 0.1 collective-permute-start
  3.3 0.5 collective-permute-start.1
  3.8 1.8 %shard_map.86 = (bf16[2,4,4,16,512]{4,3,2,1,0:T(8,128)(2,1)S(1)}, bf16[2,4,4,16,512]{4,3,2,1,0:T(8,128)(2,1)S(1)}) custom-call(s32[3]{0:T(128)S(1)} %pad_add_fusion.pos, bf16[28,4,4,2,16,512]{5,4,3,2,1,0:T(8,128)(2,1)} %bitcast.50, bf16[28,4,4,2,16,512]{5,4,3,2,1,0:T(8,128)(2,1)} %bitcast.51, bf16[28,4,4,2,16,512]{5,4,3,2,1,0:T(8,128)(2,1)} %bitcast.52, ...), custom_call_target="tpu_custom_call" | custom-call | flops 2097152 | bytes 4194304 | tf_op jit(solution)/shard_map/pallas_call | solution.py:204
  5.6 0.2 collective-permute-start.2
  5.8 2.4 %shard_map.87 = (bf16[2,10,4,16,512]{4,3,2,1,0:T(8,128)(2,1)S(1)}, bf16[2,10,4,16,512]{4,3,2,1,0:T(8,128)(2,1)S(1)}) custom-call(s32[3]{0:T(128)S(1)} %pad_add_fusion.pos, bf16[28,4,4,2,16,512]{5,4,3,2,1,0:T(8,128)(2,1)} %bitcast.54, bf16[28,4,4,2,16,512]{5,4,3,2,1,0:T(8,128)(2,1)} %bitcast.55, bf16[28,4,4,2,16,512]{5,4,3,2,1,0:T(8,128)(2,1)} %bitcast.56, ...), custom_call_target="tpu_custom_call" | custom-call | flops 5242880 | bytes 10485760 | tf_op jit(solution)/shard_map/pallas_call | solution.py:204
  8.2 0.5 collective-permute-start.6
  8.7 0.1 collective-permute-start.7
  8.8 2.9 %shard_map.88 = (bf16[2,10,4,16,512]{4,3,2,1,0:T(8,128)(2,1)S(1)}, bf16[2,10,4,16,512]{4,3,2,1,0:T(8,128)(2,1)S(1)}) custom-call(s32[3]{0:T(128)S(1)} %pad_add_fusion.pos, bf16[28,4,4,2,16,512]{5,4,3,2,1,0:T(8,128)(2,1)} %bitcast.61, bf16[28,4,4,2,16,512]{5,4,3,2,1,0:T(8,128)(2,1)} %bitcast.59, bf16[28,4,4,2,16,512]{5,4,3,2,1,0:T(8,128)(2,1)} %bitcast.60, ...), custom_call_target="tpu_custom_call" | custom-call | flops 5242880 | bytes 10485760 | tf_op jit(solution)/shard_map/pallas_call | solution.py:204
  11.7 1.7 %collective-permute-start.8 = (bf16[2,10,4,16,512]{4,3,2,1,0:T(8,128)(2,1)S(1)}, bf16[2,10,4,16,512]{4,3,2,1,0:T(8,128)(2,1)S(1)}, u32[]{:S(2)}, u32[]{:S(2)}) collective-permute-start(bf16[2,10,4,16,512]{4,3,2,1,0:T(8,128)(2,1)S(1)} %get-tuple-element.85), channel_id=1, source_target_pairs={{0,8},{4,28},{8,0},{12,20},{16,24},{20,12},{24,16},{28,4},{32,40},... | collective-permute-start | bytes 3932168 | tf_op jit(solution)/shard_map/ppermute | solution.py:175
  13.5 1.9 %collective-permute-start.9 = (bf16[2,10,4,16,512]{4,3,2,1,0:T(8,128)(2,1)S(1)}, bf16[2,10,4,16,512]{4,3,2,1,0:T(8,128)(2,1)S(1)}, u32[]{:S(2)}, u32[]{:S(2)}) collective-permute-start(bf16[2,10,4,16,512]{4,3,2,1,0:T(8,128)(2,1)S(1)} %get-tuple-element.86), channel_id=1, source_target_pairs={{0,32},{4,100},{8,40},{12,108},{16,48},{20,116},{24,56},{28,124},{... | collective-permute-start | bytes 3932168 | tf_op jit(solution)/shard_map/ppermute | solution.py:175
  15.4 3.4 %collective-permute-start.3 = (bf16[2,4,4,16,512]{4,3,2,1,0:T(8,128)(2,1)S(1)}, bf16[2,4,4,16,512]{4,3,2,1,0:T(8,128)(2,1)S(1)}, u32[]{:S(2)}, u32[]{:S(2)}) collective-permute-start(bf16[2,4,4,16,512]{4,3,2,1,0:T(8,128)(2,1)S(1)} %get-tuple-element.74), channel_id=1, source_target_pairs={{0,4},{4,0},{8,12},{12,8},{16,20},{20,16},{24,28},{28,24},{32,36},... | collective-permute-start | bytes 1572872 | tf_op jit(solution)/shard_map/ppermute | solution.py:179
  18.8 1.5 collective-permute-done.3.refs_5_
  20.3 2.0 %shard_map.89 = (bf16[2,4,4,16,512]{4,3,2,1,0:T(8,128)(2,1)S(1)}, bf16[2,4,4,16,512]{4,3,2,1,0:T(8,128)(2,1)S(1)}) custom-call(s32[3]{0:T(128)S(1)} %pad_add_fusion.pos, bf16[28,4,4,2,16,512]{5,4,3,2,1,0:T(8,128)(2,1)} %bitcast.62, bf16[28,4,4,2,16,512]{5,4,3,2,1,0:T(8,128)(2,1)} %bitcast.63, bf16[28,4,4,2,16,512]{5,4,3,2,1,0:T(8,128)(2,1)} %bitcast.64, ...), custom_call_target="tpu_custom_call" | custom-call | flops 2097152 | bytes 4194304 | tf_op jit(solution)/shard_map/pallas_call | solution.py:204
  22.4 0.2 collective-permute-start.10
  22.6 1.8 %shard_map.90 = (bf16[2,4,4,16,512]{4,3,2,1,0:T(8,128)(2,1)S(1)}, bf16[2,4,4,16,512]{4,3,2,1,0:T(8,128)(2,1)S(1)}) custom-call(s32[3]{0:T(128)S(1)} %pad_add_fusion.pos, bf16[28,4,4,2,16,512]{5,4,3,2,1,0:T(8,128)(2,1)} %bitcast.66, bf16[28,4,4,2,16,512]{5,4,3,2,1,0:T(8,128)(2,1)} %bitcast.67, bf16[28,4,4,2,16,512]{5,4,3,2,1,0:T(8,128)(2,1)} %bitcast.68, ...), custom_call_target="tpu_custom_call" | custom-call | flops 2097152 | bytes 4194304 | tf_op jit(solution)/shard_map/pallas_call | solution.py:204
  24.4 0.4 collective-permute-start.4
  24.8 0.2 collective-permute-start.5
  25.0 4.4 %collective-permute-done.8.refs_4_ = bf16[2,10,4,16,512]{4,3,2,1,0:T(8,128)(2,1)S(1)} collective-permute-done((bf16[2,10,4,16,512]{4,3,2,1,0:T(8,128)(2,1)S(1)}, bf16[2,10,4,16,512]{4,3,2,1,0:T(8,128)(2,1)S(1)}, u32[]{:S(2)}, u32[]{:S(2)}) %collective-permute-start.8) | collective-permute-done | bytes 1310752 | tf_op jit(solution)/shard_map/ppermute | solution.py:175
  29.4 2.0 %collective-permute-start.11 = (bf16[2,4,4,16,512]{4,3,2,1,0:T(8,128)(2,1)S(1)}, bf16[2,4,4,16,512]{4,3,2,1,0:T(8,128)(2,1)S(1)}, u32[]{:S(2)}, u32[]{:S(2)}) collective-permute-start(bf16[2,4,4,16,512]{4,3,2,1,0:T(8,128)(2,1)S(1)} %get-tuple-element.91), channel_id=1, source_target_pairs={{0,32},{4,100},{8,40},{12,108},{16,48},{20,116},{24,56},{28,124},{... | collective-permute-start | bytes 1572872 | tf_op jit(solution)/shard_map/ppermute | solution.py:175
  31.4 2.4 %shard_map.91 = (bf16[10,4,16,512]{3,2,1,0:T(8,128)(2,1)S(1)}, bf16[10,4,16,512]{3,2,1,0:T(8,128)(2,1)S(1)}) custom-call(s32[3]{0:T(128)S(1)} %pad_add_fusion.pos, bf16[28,4,4,2,16,512]{5,4,3,2,1,0:T(8,128)(2,1)} %bitcast.70, bf16[28,4,4,2,16,512]{5,4,3,2,1,0:T(8,128)(2,1)} %bitcast.71, bf16[2,10,4,16,512]{4,3,2,1,0:T(8,128)(2,1)S(1)} %collective-permute-done.6.refs_2_, ...), custom_call_target="tpu_custom_call" | custom-call | flops 2621440 | bytes 5242880 | tf_op jit(solution)/shard_map/pallas_call | solution.py:204
  33.8 1.2 collective-permute-done.10.refs_4_
  35.0 3.1 %collective-permute-start.14 = (bf16[10,4,16,512]{3,2,1,0:T(8,128)(2,1)S(1)}, bf16[10,4,16,512]{3,2,1,0:T(8,128)(2,1)S(1)}, u32[]{:S(2)}, u32[]{:S(2)}) collective-permute-start(bf16[10,4,16,512]{3,2,1,0:T(8,128)(2,1)S(1)} %get-tuple-element.98), channel_id=1, source_target_pairs={{0,24},{4,12},{8,16},{12,4},{16,8},{20,28},{24,0},{28,20},{32,56},... | collective-permute-start | bytes 1966088 | tf_op jit(solution)/shard_map/ppermute | solution.py:175
  38.1 4.0 %collective-permute-start.15 = (bf16[10,4,16,512]{3,2,1,0:T(8,128)(2,1)S(1)}, bf16[10,4,16,512]{3,2,1,0:T(8,128)(2,1)S(1)}, u32[]{:S(2)}, u32[]{:S(2)}) collective-permute-start(bf16[10,4,16,512]{3,2,1,0:T(8,128)(2,1)S(1)} %get-tuple-element.99), channel_id=1, source_target_pairs={{0,96},{4,36},{8,104},{12,44},{16,112},{20,52},{24,120},{28,60},{3... | collective-permute-start | bytes 1966088 | tf_op jit(solution)/shard_map/ppermute | solution.py:175
  42.2 1.8 %shard_map.93 = (bf16[4,4,16,512]{3,2,1,0:T(8,128)(2,1)S(1)}, bf16[4,4,16,512]{3,2,1,0:T(8,128)(2,1)S(1)}) custom-call(s32[3]{0:T(128)S(1)} %pad_add_fusion.pos, bf16[28,4,4,2,16,512]{5,4,3,2,1,0:T(8,128)(2,1)} %bitcast.72, bf16[28,4,4,2,16,512]{5,4,3,2,1,0:T(8,128)(2,1)} %bitcast.73, bf16[2,4,4,16,512]{4,3,2,1,0:T(8,128)(2,1)S(1)} %collective-permute-done.4.refs_2_, ...), custom_call_target="tpu_custom_call" | custom-call | flops 1048576 | bytes 2097152 | tf_op jit(solution)/shard_map/pallas_call | solution.py:204
  44.0 0.3 collective-permute-start.12
  44.3 3.7 %collective-permute-start.13 = (bf16[4,4,16,512]{3,2,1,0:T(8,128)(2,1)S(1)}, bf16[4,4,16,512]{3,2,1,0:T(8,128)(2,1)S(1)}, u32[]{:S(2)}, u32[]{:S(2)}) collective-permute-start(bf16[4,4,16,512]{3,2,1,0:T(8,128)(2,1)S(1)} %get-tuple-element.95), channel_id=1, source_target_pairs={{0,96},{4,36},{8,104},{12,44},{16,112},{20,52},{24,120},{28,60},{3... | collective-permute-start | bytes 786440 | tf_op jit(solution)/shard_map/ppermute | solution.py:175
  48.0 1.8 %shard_map.92 = (f32[4,4,16,512]{3,2,1,0:T(8,128)S(1)}, f32[4,4,16,512]{3,2,1,0:T(8,128)S(1)}) custom-call(s32[3]{0:T(128)S(1)} %pad_add_fusion.pos, bf16[28,4,4,2,16,512]{5,4,3,2,1,0:T(8,128)(2,1)} %bitcast.74, bf16[28,4,4,2,16,512]{5,4,3,2,1,0:T(8,128)(2,1)} %bitcast.75, bf16[2,4,4,16,512]{4,3,2,1,0:T(8,128)(2,1)S(1)} %collective-permute-done.4.refs_2_, ...), custom_call_target="tpu_custom_call" | custom-call | flops 1048576 | bytes 2097152 | tf_op jit(solution)/shard_map/pallas_call | solution.py:204
  49.8 2.5 %shard_map.94 = (f32[10,4,16,512]{3,2,1,0:T(8,128)S(1)}, f32[10,4,16,512]{3,2,1,0:T(8,128)S(1)}) custom-call(s32[3]{0:T(128)S(1)} %pad_add_fusion.pos, bf16[28,4,4,2,16,512]{5,4,3,2,1,0:T(8,128)(2,1)} %bitcast.76, bf16[28,4,4,2,16,512]{5,4,3,2,1,0:T(8,128)(2,1)} %bitcast.77, bf16[2,10,4,16,512]{4,3,2,1,0:T(8,128)(2,1)S(1)} %collective-permute-done.6.refs_2_, ...), custom_call_target="tpu_custom_call" | custom-call | flops 2621440 | bytes 5242880 | tf_op jit(solution)/shard_map/pallas_call | solution.py:204
  52.3 1.0 shard_map.95
  53.3 0.2 collective-permute-done.13.refs_3_
  53.5 1.5 shard_map.96
  55.1 0.1 collective-permute-start.18
  55.2 9.5 %collective-permute-done.16.refs_1_ = bf16[2,14,16,512]{3,2,1,0:T(8,128)(2,1)S(1)} collective-permute-done((bf16[2,14,16,512]{3,2,1,0:T(8,128)(2,1)}, bf16[2,14,16,512]{3,2,1,0:T(8,128)(2,1)S(1)}, u32[]{:S(2)}, u32[]{:S(2)}) %collective-permute-start.16) | collective-permute-done | bytes 458784 | tf_op jit(solution)/shard_map/ppermute | solution.py:175
  64.8 3.6 %collective-permute-start.17 = (bf16[14,16,512]{2,1,0:T(8,128)(2,1)S(1)}, bf16[14,16,512]{2,1,0:T(8,128)(2,1)S(1)}, u32[]{:S(2)}, u32[]{:S(2)}) collective-permute-start(bf16[14,16,512]{2,1,0:T(8,128)(2,1)S(1)} %fusion.1), channel_id=1, source_target_pairs={{0,96},{4,36},{8,104},{12,44},{16,112},{20,52},{24,120},{28,60},{3... | collective-permute-start | bytes 688136 | tf_op jit(solution)/shard_map/ppermute | solution.py:175
  68.5 0.1 collective-permute-start.19
  68.6 0.1 add_minimum_fusion
  68.7 0.1 min.12.wanted
  68.8 3.6 %collective-permute-done.17.refs_2_ = bf16[14,16,512]{2,1,0:T(8,128)(2,1)S(1)} collective-permute-done((bf16[14,16,512]{2,1,0:T(8,128)(2,1)S(1)}, bf16[14,16,512]{2,1,0:T(8,128)(2,1)S(1)}, u32[]{:S(2)}, u32[]{:S(2)}) %collective-permute-start.17) | collective-permute-done | bytes 229408 | tf_op jit(solution)/shard_map/ppermute | solution.py:175
  72.4 3.4 %collective-permute-done.19.refs_5_ = bf16[14,16,512]{2,1,0:T(8,128)(2,1)S(1)} collective-permute-done((bf16[14,16,512]{2,1,0:T(8,128)(2,1)S(1)}, bf16[14,16,512]{2,1,0:T(8,128)(2,1)S(1)}, u32[]{:S(2)}, u32[]{:S(2)}) %collective-permute-start.19) | collective-permute-done | bytes 229408 | tf_op jit(solution)/shard_map/ppermute | solution.py:175
  75.8 2.0 %shard_map.97 = bf16[64,16,512]{2,1,0:T(8,128)(2,1)} custom-call(s32[64]{0:T(128)S(1)} %min.12.wanted, f32[14,16,512]{2,1,0:T(8,128)S(1)} %get-tuple-element.106.refs_0_, bf16[2,14,16,512]{3,2,1,0:T(8,128)(2,1)S(1)} %collective-permute-done.16.refs_1_, bf16[14,16,512]{2,1,0:T(8,128)(2,1)S(1)} %collective-permute-done.17.refs_2_, ...), custom_call_target="tpu_custom_call" | custom-call | flops 2097152 | bytes 4194304 | tf_op jit(solution)/shard_map/pallas_call | solution.py:204
  77.7 4.2 %all-to-all-start = ((bf16[32,2,16,512]{3,2,1,0:T(8,128)(2,1)}), bf16[32,2,16,512]{3,2,1,0:T(8,128)(2,1)S(1)}, u32[]{:S(2)}, u32[]{:S(2)}) async-start(bf16[32,2,16,512]{3,2,1,0:T(8,128)(2,1)} %bitcast.8), calls=%async_computation | async-start | bytes 2097152 | tf_op jit(solution)/shard_map/all_to_all | solution.py:461
  82.0 1.3 dynamic_slice.14
  83.3 15.8 %all-to-all-done.block_ref = bf16[32,2,16,512]{3,2,1,0:T(8,128)(2,1)S(1)} async-done(((bf16[32,2,16,512]{3,2,1,0:T(8,128)(2,1)}), bf16[32,2,16,512]{3,2,1,0:T(8,128)(2,1)S(1)}, u32[]{:S(2)}, u32[]{:S(2)}) %all-to-all-start) | async-done | bytes 1048608 | tf_op jit(solution)/shard_map/all_to_all | solution.py:461
  99.1 5.7 %shard_map.98 = (f32[2,512,512]{2,1,0:T(8,128)}, f32[2,512,512]{2,1,0:T(8,128)}, bf16[32,2,16,512]{3,2,1,0:T(8,128)(2,1)}) custom-call(s32[1]{0:T(128)} %bitcast.count_ref, bf16[32,2,16,512]{3,2,1,0:T(8,128)(2,1)S(1)} %all-to-all-done.block_ref, f32[2,512,512]{2,1,0:T(8,128)S(1)} %bitcast.45, f32[2,512,512]{2,1,0:T(8,128)} %bitcast.80), custom_call_target="tpu_custom_call" | custom-call | flops 9663676416 | bytes 10485760 | tf_op jit(solution)/shard_map/pallas_call | solution.py:123
  104.8 9.9 %all-to-all-start.1 = ((bf16[32,2,16,512]{3,2,1,0:T(8,128)(2,1)}), bf16[32,2,16,512]{3,2,1,0:T(8,128)(2,1)S(1)}, u32[]{:S(2)}, u32[]{:S(2)}) async-start(bf16[32,2,16,512]{3,2,1,0:T(8,128)(2,1)} %get-tuple-element.114), calls=%async_computation.1 | async-start | bytes 2097152 | tf_op jit(solution)/shard_map/all_to_all | solution.py:464
  114.9 0.7 gather_fusion
  115.6 0.1 compare_select_fusion
  115.7 16.4 %all-to-all-done.1 = bf16[32,2,16,512]{3,2,1,0:T(8,128)(2,1)S(1)} async-done(((bf16[32,2,16,512]{3,2,1,0:T(8,128)(2,1)}), bf16[32,2,16,512]{3,2,1,0:T(8,128)(2,1)S(1)}, u32[]{:S(2)}, u32[]{:S(2)}) %all-to-all-start.1) | async-done | bytes 1048608 | tf_op jit(solution)/shard_map/all_to_all | solution.py:464
  132.1 0.6 gather_fusion.1
  132.7 1.8 %collective-permute-start.20 = (bf16[14,16,512]{2,1,0:T(8,128)(2,1)S(1)}, bf16[14,16,512]{2,1,0:T(8,128)(2,1)S(1)}, u32[]{:S(2)}, u32[]{:S(2)}) collective-permute-start(bf16[14,16,512]{2,1,0:T(8,128)(2,1)S(1)} %gather_fusion.1), channel_id=1, source_target_pairs={{0,1},{1,2},{2,3},{3,0},{4,7},{5,4},{6,5},{7,6},{8,9},{9,10},{10,1... | collective-permute-start | bytes 688136 | tf_op jit(solution)/shard_map/ppermute | solution.py:427
  134.5 1.5 collective-permute-start.24
  136.0 0.6 gather_fusion.2
  136.5 0.6 collective-permute-start.21
  137.2 2.7 %collective-permute-start.25 = (bf16[14,16,512]{2,1,0:T(8,128)(2,1)S(1)}, bf16[14,16,512]{2,1,0:T(8,128)(2,1)S(1)}, u32[]{:S(2)}, u32[]{:S(2)}) collective-permute-start(bf16[14,16,512]{2,1,0:T(8,128)(2,1)S(1)} %gather_fusion.2), channel_id=1, source_target_pairs={{0,3},{1,0},{2,1},{3,2},{4,5},{5,6},{6,7},{7,4},{8,11},{9,8},{10,9... | collective-permute-start | bytes 688136 | tf_op jit(solution)/shard_map/ppermute | solution.py:427
  139.9 0.2 broadcast_in_dim.44
  140.1 0.9 collective-permute-done.20
  141.1 1.9 %collective-permute-start.22 = (bf16[14,16,512]{2,1,0:T(8,128)(2,1)S(1)}, bf16[14,16,512]{2,1,0:T(8,128)(2,1)S(1)}, u32[]{:S(2)}, u32[]{:S(2)}) collective-permute-start(bf16[14,16,512]{2,1,0:T(8,128)(2,1)S(1)} %collective-permute-done.20), channel_id=1, source_target_pairs={{0,1},{1,2},{2,3},{3,0},{4,7},{5,4},{6,5},{7,6},{8,9},{9,10},{10,1... | collective-permute-start | bytes 688136 | tf_op jit(solution)/shard_map/ppermute | solution.py:427
  143.0 3.4 %collective-permute-done.21 = bf16[14,16,512]{2,1,0:T(8,128)(2,1)S(1)} collective-permute-done((bf16[14,16,512]{2,1,0:T(8,128)(2,1)S(1)}, bf16[14,16,512]{2,1,0:T(8,128)(2,1)S(1)}, u32[]{:S(2)}, u32[]{:S(2)}) %collective-permute-start.21) | collective-permute-done | bytes 229408 | tf_op jit(solution)/shard_map/ppermute | solution.py:427
  146.4 1.3 collective-permute-start.23
  147.8 2.0 %collective-permute-done.22 = bf16[14,16,512]{2,1,0:T(8,128)(2,1)S(1)} collective-permute-done((bf16[14,16,512]{2,1,0:T(8,128)(2,1)S(1)}, bf16[14,16,512]{2,1,0:T(8,128)(2,1)S(1)}, u32[]{:S(2)}, u32[]{:S(2)}) %collective-permute-start.22) | collective-permute-done | bytes 229408 | tf_op jit(solution)/shard_map/ppermute | solution.py:427
  149.8 3.8 %collective-permute-done.23 = bf16[14,16,512]{2,1,0:T(8,128)(2,1)S(1)} collective-permute-done((bf16[14,16,512]{2,1,0:T(8,128)(2,1)S(1)}, bf16[14,16,512]{2,1,0:T(8,128)(2,1)S(1)}, u32[]{:S(2)}, u32[]{:S(2)}) %collective-permute-start.23) | collective-permute-done | bytes 229408 | tf_op jit(solution)/shard_map/ppermute | solution.py:427
  153.7 1.2 copy-done.3
  (41 shorter events, 0.4 us)
Async XLA Ops:
  0.6 67.9 %copy-start = (s32[4,32]{1,0:T(4,128)S(1)}, s32[4,32]{1,0:T(4,128)}, u32[]{:S(2)}) copy-start(s32[4,32]{1,0:T(4,128)} %param.11) | copy-start | bytes 1540
  3.2 5.6 %collective-permute-start = (bf16[2,10,4,16,512]{4,3,2,1,0:T(8,128)(2,1)S(1)}, bf16[2,10,4,16,512]{4,3,2,1,0:T(8,128)(2,1)S(1)}, u32[]{:S(2)}, u32[]{:S(2)}) collective-permute-start(bf16[2,10,4,16,512]{4,3,2,1,0:T(8,128)(2,1)S(1)} %get-tuple-element.68), channel_id=1, source_target_pairs={{0,4},{4,0},{8,12},{12,8},{16,20},{20,16},{24,28},{28,24},{32,36},... | collective-permute-start | bytes 3932168 | tf_op jit(solution)/shard_map/ppermute | solution.py:179
  3.3 5.5 %collective-permute-start.1 = (bf16[2,10,4,16,512]{4,3,2,1,0:T(8,128)(2,1)S(1)}, bf16[2,10,4,16,512]{4,3,2,1,0:T(8,128)(2,1)S(1)}, u32[]{:S(2)}, u32[]{:S(2)}) collective-permute-start(bf16[2,10,4,16,512]{4,3,2,1,0:T(8,128)(2,1)S(1)} %get-tuple-element.69), channel_id=1, source_target_pairs={{0,4},{4,0},{8,12},{12,8},{16,20},{20,16},{24,28},{28,24},{32,36},... | collective-permute-start | bytes 3932168 | tf_op jit(solution)/shard_map/ppermute | solution.py:179
  5.6 9.8 %collective-permute-start.2 = (bf16[2,4,4,16,512]{4,3,2,1,0:T(8,128)(2,1)S(1)}, bf16[2,4,4,16,512]{4,3,2,1,0:T(8,128)(2,1)S(1)}, u32[]{:S(2)}, u32[]{:S(2)}) collective-permute-start(bf16[2,4,4,16,512]{4,3,2,1,0:T(8,128)(2,1)S(1)} %get-tuple-element.73), channel_id=1, source_target_pairs={{0,4},{4,0},{8,12},{12,8},{16,20},{20,16},{24,28},{28,24},{32,36},... | collective-permute-start | bytes 1572872 | tf_op jit(solution)/shard_map/ppermute | solution.py:179
  8.2 16.2 %collective-permute-start.6 = (bf16[2,10,4,16,512]{4,3,2,1,0:T(8,128)(2,1)S(1)}, bf16[2,10,4,16,512]{4,3,2,1,0:T(8,128)(2,1)S(1)}, u32[]{:S(2)}, u32[]{:S(2)}) collective-permute-start(bf16[2,10,4,16,512]{4,3,2,1,0:T(8,128)(2,1)S(1)} %get-tuple-element.83), channel_id=1, source_target_pairs={{0,4},{4,0},{8,12},{12,8},{16,20},{20,16},{24,28},{28,24},{32,36},... | collective-permute-start | bytes 3932168 | tf_op jit(solution)/shard_map/ppermute | solution.py:179
  8.7 16.1 %collective-permute-start.7 = (bf16[2,10,4,16,512]{4,3,2,1,0:T(8,128)(2,1)S(1)}, bf16[2,10,4,16,512]{4,3,2,1,0:T(8,128)(2,1)S(1)}, u32[]{:S(2)}, u32[]{:S(2)}) collective-permute-start(bf16[2,10,4,16,512]{4,3,2,1,0:T(8,128)(2,1)S(1)} %get-tuple-element.84), channel_id=1, source_target_pairs={{0,4},{4,0},{8,12},{12,8},{16,20},{20,16},{24,28},{28,24},{32,36},... | collective-permute-start | bytes 3932168 | tf_op jit(solution)/shard_map/ppermute | solution.py:179
  11.7 17.7 %collective-permute-start.8 = (bf16[2,10,4,16,512]{4,3,2,1,0:T(8,128)(2,1)S(1)}, bf16[2,10,4,16,512]{4,3,2,1,0:T(8,128)(2,1)S(1)}, u32[]{:S(2)}, u32[]{:S(2)}) collective-permute-start(bf16[2,10,4,16,512]{4,3,2,1,0:T(8,128)(2,1)S(1)} %get-tuple-element.85), channel_id=1, source_target_pairs={{0,8},{4,28},{8,0},{12,20},{16,24},{20,12},{24,16},{28,4},{32,40},... | collective-permute-start | bytes 3932168 | tf_op jit(solution)/shard_map/ppermute | solution.py:175
  13.5 18.0 %collective-permute-start.9 = (bf16[2,10,4,16,512]{4,3,2,1,0:T(8,128)(2,1)S(1)}, bf16[2,10,4,16,512]{4,3,2,1,0:T(8,128)(2,1)S(1)}, u32[]{:S(2)}, u32[]{:S(2)}) collective-permute-start(bf16[2,10,4,16,512]{4,3,2,1,0:T(8,128)(2,1)S(1)} %get-tuple-element.86), channel_id=1, source_target_pairs={{0,32},{4,100},{8,40},{12,108},{16,48},{20,116},{24,56},{28,124},{... | collective-permute-start | bytes 3932168 | tf_op jit(solution)/shard_map/ppermute | solution.py:175
  15.4 5.0 %collective-permute-start.3 = (bf16[2,4,4,16,512]{4,3,2,1,0:T(8,128)(2,1)S(1)}, bf16[2,4,4,16,512]{4,3,2,1,0:T(8,128)(2,1)S(1)}, u32[]{:S(2)}, u32[]{:S(2)}) collective-permute-start(bf16[2,4,4,16,512]{4,3,2,1,0:T(8,128)(2,1)S(1)} %get-tuple-element.74), channel_id=1, source_target_pairs={{0,4},{4,0},{8,12},{12,8},{16,20},{20,16},{24,28},{28,24},{32,36},... | collective-permute-start | bytes 1572872 | tf_op jit(solution)/shard_map/ppermute | solution.py:179
  22.4 12.7 %collective-permute-start.10 = (bf16[2,4,4,16,512]{4,3,2,1,0:T(8,128)(2,1)S(1)}, bf16[2,4,4,16,512]{4,3,2,1,0:T(8,128)(2,1)S(1)}, u32[]{:S(2)}, u32[]{:S(2)}) collective-permute-start(bf16[2,4,4,16,512]{4,3,2,1,0:T(8,128)(2,1)S(1)} %get-tuple-element.89), channel_id=1, source_target_pairs={{0,8},{4,28},{8,0},{12,20},{16,24},{20,12},{24,16},{28,4},{32,40},... | collective-permute-start | bytes 1572872 | tf_op jit(solution)/shard_map/ppermute | solution.py:175
  24.4 17.8 %collective-permute-start.4 = (bf16[2,4,4,16,512]{4,3,2,1,0:T(8,128)(2,1)S(1)}, bf16[2,4,4,16,512]{4,3,2,1,0:T(8,128)(2,1)S(1)}, u32[]{:S(2)}, u32[]{:S(2)}) collective-permute-start(bf16[2,4,4,16,512]{4,3,2,1,0:T(8,128)(2,1)S(1)} %get-tuple-element.81), channel_id=1, source_target_pairs={{0,4},{4,0},{8,12},{12,8},{16,20},{20,16},{24,28},{28,24},{32,36},... | collective-permute-start | bytes 1572872 | tf_op jit(solution)/shard_map/ppermute | solution.py:179
  24.8 17.3 %collective-permute-start.5 = (bf16[2,4,4,16,512]{4,3,2,1,0:T(8,128)(2,1)S(1)}, bf16[2,4,4,16,512]{4,3,2,1,0:T(8,128)(2,1)S(1)}, u32[]{:S(2)}, u32[]{:S(2)}) collective-permute-start(bf16[2,4,4,16,512]{4,3,2,1,0:T(8,128)(2,1)S(1)} %get-tuple-element.82), channel_id=1, source_target_pairs={{0,4},{4,0},{8,12},{12,8},{16,20},{20,16},{24,28},{28,24},{32,36},... | collective-permute-start | bytes 1572872 | tf_op jit(solution)/shard_map/ppermute | solution.py:179
  29.4 12.8 %collective-permute-start.11 = (bf16[2,4,4,16,512]{4,3,2,1,0:T(8,128)(2,1)S(1)}, bf16[2,4,4,16,512]{4,3,2,1,0:T(8,128)(2,1)S(1)}, u32[]{:S(2)}, u32[]{:S(2)}) collective-permute-start(bf16[2,4,4,16,512]{4,3,2,1,0:T(8,128)(2,1)S(1)} %get-tuple-element.91), channel_id=1, source_target_pairs={{0,32},{4,100},{8,40},{12,108},{16,48},{20,116},{24,56},{28,124},{... | collective-permute-start | bytes 1572872 | tf_op jit(solution)/shard_map/ppermute | solution.py:175
  31.4 2.4 %copy-start.1 = (bf16[2,10,4,16,512]{4,3,2,1,0:T(8,128)(2,1)}, bf16[2,10,4,16,512]{4,3,2,1,0:T(8,128)(2,1)S(1)}, u32[]{:S(2)}) copy-start(bf16[2,10,4,16,512]{4,3,2,1,0:T(8,128)(2,1)S(1)} %collective-permute-done.9.refs_5_) | copy-start | bytes 3932164
  35.0 17.2 %collective-permute-start.14 = (bf16[10,4,16,512]{3,2,1,0:T(8,128)(2,1)S(1)}, bf16[10,4,16,512]{3,2,1,0:T(8,128)(2,1)S(1)}, u32[]{:S(2)}, u32[]{:S(2)}) collective-permute-start(bf16[10,4,16,512]{3,2,1,0:T(8,128)(2,1)S(1)} %get-tuple-element.98), channel_id=1, source_target_pairs={{0,24},{4,12},{8,16},{12,4},{16,8},{20,28},{24,0},{28,20},{32,56},... | collective-permute-start | bytes 1966088 | tf_op jit(solution)/shard_map/ppermute | solution.py:175
  38.1 14.1 %collective-permute-start.15 = (bf16[10,4,16,512]{3,2,1,0:T(8,128)(2,1)S(1)}, bf16[10,4,16,512]{3,2,1,0:T(8,128)(2,1)S(1)}, u32[]{:S(2)}, u32[]{:S(2)}) collective-permute-start(bf16[10,4,16,512]{3,2,1,0:T(8,128)(2,1)S(1)} %get-tuple-element.99), channel_id=1, source_target_pairs={{0,96},{4,36},{8,104},{12,44},{16,112},{20,52},{24,120},{28,60},{3... | collective-permute-start | bytes 1966088 | tf_op jit(solution)/shard_map/ppermute | solution.py:175
  44.0 9.3 %collective-permute-start.12 = (bf16[4,4,16,512]{3,2,1,0:T(8,128)(2,1)S(1)}, bf16[4,4,16,512]{3,2,1,0:T(8,128)(2,1)S(1)}, u32[]{:S(2)}, u32[]{:S(2)}) collective-permute-start(bf16[4,4,16,512]{3,2,1,0:T(8,128)(2,1)S(1)} %get-tuple-element.94), channel_id=1, source_target_pairs={{0,24},{4,12},{8,16},{12,4},{16,8},{20,28},{24,0},{28,20},{32,56},... | collective-permute-start | bytes 786440 | tf_op jit(solution)/shard_map/ppermute | solution.py:175
  44.3 9.3 %collective-permute-start.13 = (bf16[4,4,16,512]{3,2,1,0:T(8,128)(2,1)S(1)}, bf16[4,4,16,512]{3,2,1,0:T(8,128)(2,1)S(1)}, u32[]{:S(2)}, u32[]{:S(2)}) collective-permute-start(bf16[4,4,16,512]{3,2,1,0:T(8,128)(2,1)S(1)} %get-tuple-element.95), channel_id=1, source_target_pairs={{0,96},{4,36},{8,104},{12,44},{16,112},{20,52},{24,120},{28,60},{3... | collective-permute-start | bytes 786440 | tf_op jit(solution)/shard_map/ppermute | solution.py:175
  55.1 9.6 %collective-permute-start.16 = (bf16[2,14,16,512]{3,2,1,0:T(8,128)(2,1)}, bf16[2,14,16,512]{3,2,1,0:T(8,128)(2,1)S(1)}, u32[]{:S(2)}, u32[]{:S(2)}) collective-permute-start(bf16[2,14,16,512]{3,2,1,0:T(8,128)(2,1)} %get-tuple-element.107), channel_id=1, source_target_pairs={{0,32},{4,100},{8,40},{12,108},{16,48},{20,116},{24,56},{28,124},{... | collective-permute-start | bytes 1376264 | tf_op jit(solution)/shard_map/ppermute | solution.py:175
  55.1 13.3 %collective-permute-start.18 = (bf16[2,14,16,512]{3,2,1,0:T(8,128)(2,1)S(1)}, bf16[2,14,16,512]{3,2,1,0:T(8,128)(2,1)S(1)}, u32[]{:S(2)}, u32[]{:S(2)}) collective-permute-start(bf16[2,14,16,512]{3,2,1,0:T(8,128)(2,1)S(1)} %get-tuple-element.110), channel_id=1, source_target_pairs={{0,8},{4,28},{8,0},{12,20},{16,24},{20,12},{24,16},{28,4},{32,40},... | collective-permute-start | bytes 1376264 | tf_op jit(solution)/shard_map/ppermute | solution.py:175
  64.8 7.6 %collective-permute-start.17 = (bf16[14,16,512]{2,1,0:T(8,128)(2,1)S(1)}, bf16[14,16,512]{2,1,0:T(8,128)(2,1)S(1)}, u32[]{:S(2)}, u32[]{:S(2)}) collective-permute-start(bf16[14,16,512]{2,1,0:T(8,128)(2,1)S(1)} %fusion.1), channel_id=1, source_target_pairs={{0,96},{4,36},{8,104},{12,44},{16,112},{20,52},{24,120},{28,60},{3... | collective-permute-start | bytes 688136 | tf_op jit(solution)/shard_map/ppermute | solution.py:175
  68.5 7.3 %collective-permute-start.19 = (bf16[14,16,512]{2,1,0:T(8,128)(2,1)S(1)}, bf16[14,16,512]{2,1,0:T(8,128)(2,1)S(1)}, u32[]{:S(2)}, u32[]{:S(2)}) collective-permute-start(bf16[14,16,512]{2,1,0:T(8,128)(2,1)S(1)} %fusion), channel_id=1, source_target_pairs={{0,24},{4,12},{8,16},{12,4},{16,8},{20,28},{24,0},{28,20},{32,56},... | collective-permute-start | bytes 688136 | tf_op jit(solution)/shard_map/ppermute | solution.py:175
  77.7 21.4 %copy-start.2 = (f32[1,2,512,512]{3,2,1,0:T(8,128)S(1)}, f32[1,2,512,512]{3,2,1,0:T(8,128)}, u32[]{:S(2)}) copy-start(f32[1,2,512,512]{3,2,1,0:T(8,128)} %param.7) | copy-start | bytes 6291460
  77.7 21.4 %all-to-all-start = ((bf16[32,2,16,512]{3,2,1,0:T(8,128)(2,1)}), bf16[32,2,16,512]{3,2,1,0:T(8,128)(2,1)S(1)}, u32[]{:S(2)}, u32[]{:S(2)}) async-start(bf16[32,2,16,512]{3,2,1,0:T(8,128)(2,1)} %bitcast.8), calls=%async_computation | async-start | bytes 2097152 | tf_op jit(solution)/shard_map/all_to_all | solution.py:461
  104.8 10.0 %copy-start.4 = (s32[4,28]{1,0:T(4,128)S(1)}, s32[4,28]{1,0:T(4,128)}, u32[]{:S(2)}) copy-start(s32[4,28]{1,0:T(4,128)} %param.9) | copy-start | bytes 1348
  104.8 27.3 %all-to-all-start.1 = ((bf16[32,2,16,512]{3,2,1,0:T(8,128)(2,1)}), bf16[32,2,16,512]{3,2,1,0:T(8,128)(2,1)S(1)}, u32[]{:S(2)}, u32[]{:S(2)}) async-start(bf16[32,2,16,512]{3,2,1,0:T(8,128)(2,1)} %get-tuple-element.114), calls=%async_computation.1 | async-start | bytes 2097152 | tf_op jit(solution)/shard_map/all_to_all | solution.py:464
  132.7 8.4 %collective-permute-start.20 = (bf16[14,16,512]{2,1,0:T(8,128)(2,1)S(1)}, bf16[14,16,512]{2,1,0:T(8,128)(2,1)S(1)}, u32[]{:S(2)}, u32[]{:S(2)}) collective-permute-start(bf16[14,16,512]{2,1,0:T(8,128)(2,1)S(1)} %gather_fusion.1), channel_id=1, source_target_pairs={{0,1},{1,2},{2,3},{3,0},{4,7},{5,4},{6,5},{7,6},{8,9},{9,10},{10,1... | collective-permute-start | bytes 688136 | tf_op jit(solution)/shard_map/ppermute | solution.py:427
  134.5 19.1 %collective-permute-start.24 = (bf16[14,16,512]{2,1,0:T(8,128)(2,1)S(1)}, bf16[14,16,512]{2,1,0:T(8,128)(2,1)S(1)}, u32[]{:S(2)}, u32[]{:S(2)}) collective-permute-start(bf16[14,16,512]{2,1,0:T(8,128)(2,1)S(1)} %gather_fusion.1), channel_id=1, source_target_pairs={{0,3},{1,0},{2,1},{3,2},{4,5},{5,6},{6,7},{7,4},{8,11},{9,8},{10,9... | collective-permute-start | bytes 688136 | tf_op jit(solution)/shard_map/ppermute | solution.py:427
  136.5 9.8 %collective-permute-start.21 = (bf16[14,16,512]{2,1,0:T(8,128)(2,1)S(1)}, bf16[14,16,512]{2,1,0:T(8,128)(2,1)S(1)}, u32[]{:S(2)}, u32[]{:S(2)}) collective-permute-start(bf16[14,16,512]{2,1,0:T(8,128)(2,1)S(1)} %gather_fusion.2), channel_id=1, source_target_pairs={{0,1},{1,2},{2,3},{3,0},{4,7},{5,4},{6,5},{7,6},{8,9},{9,10},{10,1... | collective-permute-start | bytes 688136 | tf_op jit(solution)/shard_map/ppermute | solution.py:427
  137.2 16.5 %collective-permute-start.25 = (bf16[14,16,512]{2,1,0:T(8,128)(2,1)S(1)}, bf16[14,16,512]{2,1,0:T(8,128)(2,1)S(1)}, u32[]{:S(2)}, u32[]{:S(2)}) collective-permute-start(bf16[14,16,512]{2,1,0:T(8,128)(2,1)S(1)} %gather_fusion.2), channel_id=1, source_target_pairs={{0,3},{1,0},{2,1},{3,2},{4,5},{5,6},{6,7},{7,4},{8,11},{9,8},{10,9... | collective-permute-start | bytes 688136 | tf_op jit(solution)/shard_map/ppermute | solution.py:427
  141.1 8.7 %collective-permute-start.22 = (bf16[14,16,512]{2,1,0:T(8,128)(2,1)S(1)}, bf16[14,16,512]{2,1,0:T(8,128)(2,1)S(1)}, u32[]{:S(2)}, u32[]{:S(2)}) collective-permute-start(bf16[14,16,512]{2,1,0:T(8,128)(2,1)S(1)} %collective-permute-done.20), channel_id=1, source_target_pairs={{0,1},{1,2},{2,3},{3,0},{4,7},{5,4},{6,5},{7,6},{8,9},{9,10},{10,1... | collective-permute-start | bytes 688136 | tf_op jit(solution)/shard_map/ppermute | solution.py:427
  146.4 7.2 %collective-permute-start.23 = (bf16[14,16,512]{2,1,0:T(8,128)(2,1)S(1)}, bf16[14,16,512]{2,1,0:T(8,128)(2,1)S(1)}, u32[]{:S(2)}, u32[]{:S(2)}) collective-permute-start(bf16[14,16,512]{2,1,0:T(8,128)(2,1)S(1)} %collective-permute-done.21), channel_id=1, source_target_pairs={{0,1},{1,2},{2,3},{3,0},{4,7},{5,4},{6,5},{7,6},{8,9},{9,10},{10,1... | collective-permute-start | bytes 688136 | tf_op jit(solution)/shard_map/ppermute | solution.py:427
  153.7 1.2 copy-start.3

commit v7 on v5

--- a/solution.py
+++ b/solution.py
@@ -13,6 +13,7 @@
 START = 25.0 / 16.0
 VMEM = 47 * 1024 * 1024
 SETS = (10, 4)
+STEPS = 2
 PLACES = 2
 
 
@@ -179,19 +180,19 @@
     return lax.ppermute(value, "dp", [(flat(z, y, core), flat(z, y, 1 - core)) for z, y, core in places()])
 
 
-def cut_specs(shape, which, half, other=False):
+def cut_specs(shape, which, half, other=False, steps=1):
     _, _, _, _, rows, extent = shape
-    size = SETS[half]
+    size = SETS[half] // steps
     start = 2 * sum(SETS[:half]) // size
 
     def whose(pos):
         return 1 - pos[2] if other else pos[2]
 
     def first(i, pos):
-        return (start, 0, chunk(pos[1], whose(pos), which), whose(pos), 0, 0)
+        return (start + i, 0, chunk(pos[1], whose(pos), which), whose(pos), 0, 0)
 
     def second(i, pos):
-        return (start + 1, chunk(pos[0], whose(pos), which), 0, whose(pos), 0, 0)
+        return (start + steps + i, chunk(pos[0], whose(pos), which), 0, whose(pos), 0, 0)
 
     return [
         pl.BlockSpec((size, RING, 1, 1, rows, extent), first),
@@ -252,10 +253,11 @@
 
 
 def first_sums(view, pos, half, others):
-    whole = pl.BlockSpec(others[0].shape, lambda i, pos: (0, 0, 0, 0, 0))
-    specs = [spec for w in (3, 1) for spec in cut_specs(view.shape, w, half)]
+    full = others[0].shape
+    whole = pl.BlockSpec((full[0], full[1] // STEPS, *full[2:]), lambda i, pos: (0, i, 0, 0, 0))
+    specs = [spec for w in (3, 1) for spec in cut_specs(view.shape, w, half, steps=STEPS)]
     shape = [jax.ShapeDtypeStruct(others[0].shape, jnp.bfloat16)] * 2
-    return local_call(first_kernel, pos, specs + [whole] * 2, [view] * 4 + list(others), [whole] * 2, shape)
+    return local_call(first_kernel, pos, specs + [whole] * 2, [view] * 4 + list(others), [whole] * 2, shape, steps=STEPS)
 
 
 def second_kernel(pos, *refs):

time: 155 us -> 155 us (level)
  Pallas kernels: 32 us -> 35.4 us
  starting transfers between devices: 46.2 us -> 43.2 us
    all_to_all x1, starting transfers between devices: 10.2 us -> 6.13 us  [per_device(): lax.all_to_all(updates, 'dp', split_axis=0, concat_axis=0, tiled=True)]
    pallas_call x1, Pallas kernels: 5.69 us -> 9.16 us  [slot_step(): pl.pallas_call(slot_kernel, grid_spec=pltpu.PrefetchScalarGridSpec(num_sc...]
where the time goes in v7:
time: 155 us; the launch traced here: 154 us
  waiting for transfers between devices  69.2 us (45%)
  starting transfers between devices  43.2 us (28%)
  Pallas kernels  35.4 us (23%)
  local copies, waits for them, and re-layouts  4.85 us (3%)
    pallas_call x13, Pallas kernels, local_call(): pl.pallas_call(body, grid_spec=pltpu.PrefetchScalarGridSpec(num_scalar_pr...  26.2 us
    ppermute x12, waiting for transfers between devices, exchange(): return lax.ppermute(value, 'dp', pairs)  25.2 us
    all_to_all x1, waiting for transfers between devices, per_device(): lax.all_to_all(updates, 'dp', split_axis=0, concat_axis=0, tiled=True)  16.4 us
    ppermute x12, starting transfers between devices, exchange(): return lax.ppermute(value, 'dp', pairs)  16.4 us
    all_to_all x1, waiting for transfers between devices, per_device(): lax.all_to_all(outgoing, 'dp', split_axis=0, concat_axis=0, tiled=True)  15.8 us
    ppermute x6, waiting for transfers between devices, send_group(): return lax.ppermute(value, ('dp', 'mp'), pairs)  10.2 us
    ppermute x6, starting transfers between devices, send_group(): return lax.ppermute(value, ('dp', 'mp'), pairs)  9.97 us
    pallas_call x1, Pallas kernels, slot_step(): pl.pallas_call(slot_kernel, grid_spec=pltpu.PrefetchScalarGridSpec(num_sc...  9.16 us
  transfers between devices with their start and end apart: 28, of which 16 were waited for; matrix products, arithmetic and copies ran while one was open for 2% of the time, Pallas kernels for 13%

profile of v7, /device:TPU:0, one launch (start us, length us, event | category | flops | bytes accessed | tf_op | source)
XLA Modules:
  0.0 154.1 jit_solution(8830310744606318581)
XLA Ops:
  0.7 0.1 pad_add_fusion.pos
  0.8 2.4 %shard_map.85 = (bf16[2,10,4,16,512]{4,3,2,1,0:T(8,128)(2,1)S(1)}, bf16[2,10,4,16,512]{4,3,2,1,0:T(8,128)(2,1)S(1)}) custom-call(s32[3]{0:T(128)S(1)} %pad_add_fusion.pos, bf16[28,4,4,2,16,512]{5,4,3,2,1,0:T(8,128)(2,1)} %bitcast.46, bf16[28,4,4,2,16,512]{5,4,3,2,1,0:T(8,128)(2,1)} %bitcast.47, bf16[28,4,4,2,16,512]{5,4,3,2,1,0:T(8,128)(2,1)} %bitcast.48, ...), custom_call_target="tpu_custom_call" | custom-call | flops 5242880 | bytes 10485760 | tf_op jit(solution)/shard_map/pallas_call | solution.py:205
  3.2 0.1 collective-permute-start
  3.3 0.5 collective-permute-start.1
  3.8 1.8 %shard_map.86 = (bf16[2,4,4,16,512]{4,3,2,1,0:T(8,128)(2,1)S(1)}, bf16[2,4,4,16,512]{4,3,2,1,0:T(8,128)(2,1)S(1)}) custom-call(s32[3]{0:T(128)S(1)} %pad_add_fusion.pos, bf16[28,4,4,2,16,512]{5,4,3,2,1,0:T(8,128)(2,1)} %bitcast.50, bf16[28,4,4,2,16,512]{5,4,3,2,1,0:T(8,128)(2,1)} %bitcast.51, bf16[28,4,4,2,16,512]{5,4,3,2,1,0:T(8,128)(2,1)} %bitcast.52, ...), custom_call_target="tpu_custom_call" | custom-call | flops 2097152 | bytes 4194304 | tf_op jit(solution)/shard_map/pallas_call | solution.py:205
  5.6 2.4 %shard_map.87 = (bf16[2,10,4,16,512]{4,3,2,1,0:T(8,128)(2,1)S(1)}, bf16[2,10,4,16,512]{4,3,2,1,0:T(8,128)(2,1)S(1)}) custom-call(s32[3]{0:T(128)S(1)} %pad_add_fusion.pos, bf16[28,4,4,2,16,512]{5,4,3,2,1,0:T(8,128)(2,1)} %bitcast.54, bf16[28,4,4,2,16,512]{5,4,3,2,1,0:T(8,128)(2,1)} %bitcast.55, bf16[28,4,4,2,16,512]{5,4,3,2,1,0:T(8,128)(2,1)} %bitcast.56, ...), custom_call_target="tpu_custom_call" | custom-call | flops 5242880 | bytes 10485760 | tf_op jit(solution)/shard_map/pallas_call | solution.py:205
  8.0 0.2 collective-permute-start.6
  8.2 0.4 collective-permute-start.2
  8.6 0.1 collective-permute-start.7
  8.7 2.7 %shard_map.88 = (bf16[2,10,4,16,512]{4,3,2,1,0:T(8,128)(2,1)S(1)}, bf16[2,10,4,16,512]{4,3,2,1,0:T(8,128)(2,1)S(1)}) custom-call(s32[3]{0:T(128)S(1)} %pad_add_fusion.pos, bf16[28,4,4,2,16,512]{5,4,3,2,1,0:T(8,128)(2,1)} %bitcast.61, bf16[28,4,4,2,16,512]{5,4,3,2,1,0:T(8,128)(2,1)} %bitcast.59, bf16[28,4,4,2,16,512]{5,4,3,2,1,0:T(8,128)(2,1)} %bitcast.60, ...), custom_call_target="tpu_custom_call" | custom-call | flops 5242880 | bytes 10485760 | tf_op jit(solution)/shard_map/pallas_call | solution.py:205
  11.5 1.7 %collective-permute-start.8 = (bf16[2,10,4,16,512]{4,3,2,1,0:T(8,128)(2,1)S(1)}, bf16[2,10,4,16,512]{4,3,2,1,0:T(8,128)(2,1)S(1)}, u32[]{:S(2)}, u32[]{:S(2)}) collective-permute-start(bf16[2,10,4,16,512]{4,3,2,1,0:T(8,128)(2,1)S(1)} %get-tuple-element.86), channel_id=1, source_target_pairs={{0,8},{4,28},{8,0},{12,20},{16,24},{20,12},{24,16},{28,4},{32,40},... | collective-permute-start | bytes 3932168 | tf_op jit(solution)/shard_map/ppermute | solution.py:176
  13.2 1.9 %collective-permute-start.9 = (bf16[2,10,4,16,512]{4,3,2,1,0:T(8,128)(2,1)S(1)}, bf16[2,10,4,16,512]{4,3,2,1,0:T(8,128)(2,1)S(1)}, u32[]{:S(2)}, u32[]{:S(2)}) collective-permute-start(bf16[2,10,4,16,512]{4,3,2,1,0:T(8,128)(2,1)S(1)} %get-tuple-element.87), channel_id=1, source_target_pairs={{0,32},{4,100},{8,40},{12,108},{16,48},{20,116},{24,56},{28,124},{... | collective-permute-start | bytes 3932168 | tf_op jit(solution)/shard_map/ppermute | solution.py:176
  15.1 3.4 %collective-permute-start.3 = (bf16[2,4,4,16,512]{4,3,2,1,0:T(8,128)(2,1)S(1)}, bf16[2,4,4,16,512]{4,3,2,1,0:T(8,128)(2,1)S(1)}, u32[]{:S(2)}, u32[]{:S(2)}) collective-permute-start(bf16[2,4,4,16,512]{4,3,2,1,0:T(8,128)(2,1)S(1)} %get-tuple-element.75), channel_id=1, source_target_pairs={{0,4},{4,0},{8,12},{12,8},{16,20},{20,16},{24,28},{28,24},{32,36},... | collective-permute-start | bytes 1572872 | tf_op jit(solution)/shard_map/ppermute | solution.py:180
  18.5 1.5 collective-permute-done.3.refs_5_
  20.1 2.1 %shard_map.89 = (bf16[2,4,4,16,512]{4,3,2,1,0:T(8,128)(2,1)S(1)}, bf16[2,4,4,16,512]{4,3,2,1,0:T(8,128)(2,1)S(1)}) custom-call(s32[3]{0:T(128)S(1)} %pad_add_fusion.pos, bf16[28,4,4,2,16,512]{5,4,3,2,1,0:T(8,128)(2,1)} %bitcast.62, bf16[28,4,4,2,16,512]{5,4,3,2,1,0:T(8,128)(2,1)} %bitcast.63, bf16[28,4,4,2,16,512]{5,4,3,2,1,0:T(8,128)(2,1)} %bitcast.64, ...), custom_call_target="tpu_custom_call" | custom-call | flops 2097152 | bytes 4194304 | tf_op jit(solution)/shard_map/pallas_call | solution.py:205
  22.2 0.2 collective-permute-start.10
  22.4 1.8 %shard_map.90 = (bf16[2,4,4,16,512]{4,3,2,1,0:T(8,128)(2,1)S(1)}, bf16[2,4,4,16,512]{4,3,2,1,0:T(8,128)(2,1)S(1)}) custom-call(s32[3]{0:T(128)S(1)} %pad_add_fusion.pos, bf16[28,4,4,2,16,512]{5,4,3,2,1,0:T(8,128)(2,1)} %bitcast.66, bf16[28,4,4,2,16,512]{5,4,3,2,1,0:T(8,128)(2,1)} %bitcast.67, bf16[28,4,4,2,16,512]{5,4,3,2,1,0:T(8,128)(2,1)} %bitcast.68, ...), custom_call_target="tpu_custom_call" | custom-call | flops 2097152 | bytes 4194304 | tf_op jit(solution)/shard_map/pallas_call | solution.py:205
  24.3 1.2 collective-permute-start.4
  25.4 3.7 %collective-permute-done.8.refs_4_ = bf16[2,10,4,16,512]{4,3,2,1,0:T(8,128)(2,1)S(1)} collective-permute-done((bf16[2,10,4,16,512]{4,3,2,1,0:T(8,128)(2,1)S(1)}, bf16[2,10,4,16,512]{4,3,2,1,0:T(8,128)(2,1)S(1)}, u32[]{:S(2)}, u32[]{:S(2)}) %collective-permute-start.8) | collective-permute-done | bytes 1310752 | tf_op jit(solution)/shard_map/ppermute | solution.py:176
  29.2 0.6 collective-permute-start.5
  29.8 1.0 collective-permute-done.9.refs_5_
  30.8 2.4 %shard_map.91 = (bf16[10,4,16,512]{3,2,1,0:T(8,128)(2,1)S(1)}, bf16[10,4,16,512]{3,2,1,0:T(8,128)(2,1)S(1)}) custom-call(s32[3]{0:T(128)S(1)} %pad_add_fusion.pos, bf16[28,4,4,2,16,512]{5,4,3,2,1,0:T(8,128)(2,1)} %bitcast.70, bf16[28,4,4,2,16,512]{5,4,3,2,1,0:T(8,128)(2,1)} %bitcast.71, bf16[2,10,4,16,512]{4,3,2,1,0:T(8,128)(2,1)S(1)} %collective-permute-done.6.refs_2_, ...), custom_call_target="tpu_custom_call" | custom-call | flops 2621440 | bytes 5242880 | tf_op jit(solution)/shard_map/pallas_call | solution.py:205
  33.2 1.6 %collective-permute-done.10.refs_4_ = bf16[2,4,4,16,512]{4,3,2,1,0:T(8,128)(2,1)S(1)} collective-permute-done((bf16[2,4,4,16,512]{4,3,2,1,0:T(8,128)(2,1)S(1)}, bf16[2,4,4,16,512]{4,3,2,1,0:T(8,128)(2,1)S(1)}, u32[]{:S(2)}, u32[]{:S(2)}) %collective-permute-start.10) | collective-permute-done | bytes 524320 | tf_op jit(solution)/shard_map/ppermute | solution.py:176
  34.8 1.7 %collective-permute-done.11.refs_5_ = bf16[2,4,4,16,512]{4,3,2,1,0:T(8,128)(2,1)S(1)} collective-permute-done((bf16[2,4,4,16,512]{4,3,2,1,0:T(8,128)(2,1)S(1)}, bf16[2,4,4,16,512]{4,3,2,1,0:T(8,128)(2,1)S(1)}, u32[]{:S(2)}, u32[]{:S(2)}) %collective-permute-start.11) | collective-permute-done | bytes 524320 | tf_op jit(solution)/shard_map/ppermute | solution.py:176
  36.4 2.2 %collective-permute-start.14 = (bf16[10,4,16,512]{3,2,1,0:T(8,128)(2,1)S(1)}, bf16[10,4,16,512]{3,2,1,0:T(8,128)(2,1)S(1)}, u32[]{:S(2)}, u32[]{:S(2)}) collective-permute-start(bf16[10,4,16,512]{3,2,1,0:T(8,128)(2,1)S(1)} %get-tuple-element.100), channel_id=1, source_target_pairs={{0,24},{4,12},{8,16},{12,4},{16,8},{20,28},{24,0},{28,20},{32,56},... | collective-permute-start | bytes 1966088 | tf_op jit(solution)/shard_map/ppermute | solution.py:176
  38.6 4.0 %collective-permute-start.15 = (bf16[10,4,16,512]{3,2,1,0:T(8,128)(2,1)S(1)}, bf16[10,4,16,512]{3,2,1,0:T(8,128)(2,1)S(1)}, u32[]{:S(2)}, u32[]{:S(2)}) collective-permute-start(bf16[10,4,16,512]{3,2,1,0:T(8,128)(2,1)S(1)} %get-tuple-element.101), channel_id=1, source_target_pairs={{0,96},{4,36},{8,104},{12,44},{16,112},{20,52},{24,120},{28,60},{3... | collective-permute-start | bytes 1966088 | tf_op jit(solution)/shard_map/ppermute | solution.py:176
  42.7 1.8 %shard_map.93 = (bf16[4,4,16,512]{3,2,1,0:T(8,128)(2,1)S(1)}, bf16[4,4,16,512]{3,2,1,0:T(8,128)(2,1)S(1)}) custom-call(s32[3]{0:T(128)S(1)} %pad_add_fusion.pos, bf16[28,4,4,2,16,512]{5,4,3,2,1,0:T(8,128)(2,1)} %bitcast.72, bf16[28,4,4,2,16,512]{5,4,3,2,1,0:T(8,128)(2,1)} %bitcast.73, bf16[2,4,4,16,512]{4,3,2,1,0:T(8,128)(2,1)S(1)} %collective-permute-done.4.refs_2_, ...), custom_call_target="tpu_custom_call" | custom-call | flops 1048576 | bytes 2097152 | tf_op jit(solution)/shard_map/pallas_call | solution.py:205
  44.5 1.1 collective-permute-start.12
  45.6 1.8 %shard_map.92 = (f32[4,4,16,512]{3,2,1,0:T(8,128)S(1)}, f32[4,4,16,512]{3,2,1,0:T(8,128)S(1)}) custom-call(s32[3]{0:T(128)S(1)} %pad_add_fusion.pos, bf16[28,4,4,2,16,512]{5,4,3,2,1,0:T(8,128)(2,1)} %bitcast.74, bf16[28,4,4,2,16,512]{5,4,3,2,1,0:T(8,128)(2,1)} %bitcast.75, bf16[2,4,4,16,512]{4,3,2,1,0:T(8,128)(2,1)S(1)} %collective-permute-done.4.refs_2_, ...), custom_call_target="tpu_custom_call" | custom-call | flops 1048576 | bytes 2097152 | tf_op jit(solution)/shard_map/pallas_call | solution.py:205
  47.4 2.5 %shard_map.94 = (f32[10,4,16,512]{3,2,1,0:T(8,128)S(1)}, f32[10,4,16,512]{3,2,1,0:T(8,128)S(1)}) custom-call(s32[3]{0:T(128)S(1)} %pad_add_fusion.pos, bf16[28,4,4,2,16,512]{5,4,3,2,1,0:T(8,128)(2,1)} %bitcast.76, bf16[28,4,4,2,16,512]{5,4,3,2,1,0:T(8,128)(2,1)} %bitcast.77, bf16[2,10,4,16,512]{4,3,2,1,0:T(8,128)(2,1)S(1)} %collective-permute-done.6.refs_2_, ...), custom_call_target="tpu_custom_call" | custom-call | flops 2621440 | bytes 5242880 | tf_op jit(solution)/shard_map/pallas_call | solution.py:205
  49.8 1.4 collective-permute-done.15.refs_3_
  51.2 1.0 shard_map.95
  52.2 1.8 %collective-permute-done.13.refs_3_ = bf16[4,4,16,512]{3,2,1,0:T(8,128)(2,1)S(1)} collective-permute-done((bf16[4,4,16,512]{3,2,1,0:T(8,128)(2,1)S(1)}, bf16[4,4,16,512]{3,2,1,0:T(8,128)(2,1)S(1)}, u32[]{:S(2)}, u32[]{:S(2)}) %collective-permute-start.13) | collective-permute-done | bytes 262176 | tf_op jit(solution)/shard_map/ppermute | solution.py:176
  54.0 1.5 %shard_map.96 = (bf16[2,14,16,512]{3,2,1,0:T(8,128)(2,1)}, f32[14,16,512]{2,1,0:T(8,128)S(1)}, f32[14,16,512]{2,1,0:T(8,128)S(1)}, bf16[2,14,16,512]{3,2,1,0:T(8...) custom-call(s32[3]{0:T(128)S(1)} %pad_add_fusion.pos, ...), custom_call_target="tpu_custom_call" | custom-call | flops 3670016 | bytes 7340032 | tf_op jit(solution)/shard_map/pallas_call | solution.py:205
  55.6 0.7 collective-permute-start.18
  56.3 8.0 %collective-permute-done.16.refs_1_ = bf16[2,14,16,512]{3,2,1,0:T(8,128)(2,1)S(1)} collective-permute-done((bf16[2,14,16,512]{3,2,1,0:T(8,128)(2,1)}, bf16[2,14,16,512]{3,2,1,0:T(8,128)(2,1)S(1)}, u32[]{:S(2)}, u32[]{:S(2)}) %collective-permute-start.16) | collective-permute-done | bytes 458784 | tf_op jit(solution)/shard_map/ppermute | solution.py:176
  64.3 3.3 %collective-permute-start.17 = (bf16[14,16,512]{2,1,0:T(8,128)(2,1)S(1)}, bf16[14,16,512]{2,1,0:T(8,128)(2,1)S(1)}, u32[]{:S(2)}, u32[]{:S(2)}) collective-permute-start(bf16[14,16,512]{2,1,0:T(8,128)(2,1)S(1)} %fusion.1), channel_id=1, source_target_pairs={{0,96},{4,36},{8,104},{12,44},{16,112},{20,52},{24,120},{28,60},{3... | collective-permute-start | bytes 688136 | tf_op jit(solution)/shard_map/ppermute | solution.py:176
  67.7 1.1 collective-permute-start.19
  68.8 0.1 add_minimum_fusion
  68.9 0.1 min.12.wanted
  69.0 2.6 %collective-permute-done.17.refs_2_ = bf16[14,16,512]{2,1,0:T(8,128)(2,1)S(1)} collective-permute-done((bf16[14,16,512]{2,1,0:T(8,128)(2,1)S(1)}, bf16[14,16,512]{2,1,0:T(8,128)(2,1)S(1)}, u32[]{:S(2)}, u32[]{:S(2)}) %collective-permute-start.17) | collective-permute-done | bytes 229408 | tf_op jit(solution)/shard_map/ppermute | solution.py:176
  71.6 3.4 %collective-permute-done.19.refs_5_ = bf16[14,16,512]{2,1,0:T(8,128)(2,1)S(1)} collective-permute-done((bf16[14,16,512]{2,1,0:T(8,128)(2,1)S(1)}, bf16[14,16,512]{2,1,0:T(8,128)(2,1)S(1)}, u32[]{:S(2)}, u32[]{:S(2)}) %collective-permute-start.19) | collective-permute-done | bytes 229408 | tf_op jit(solution)/shard_map/ppermute | solution.py:176
  75.0 2.0 %shard_map.97 = bf16[64,16,512]{2,1,0:T(8,128)(2,1)} custom-call(s32[64]{0:T(128)S(1)} %min.12.wanted, f32[14,16,512]{2,1,0:T(8,128)S(1)} %get-tuple-element.108.refs_0_, bf16[2,14,16,512]{3,2,1,0:T(8,128)(2,1)S(1)} %collective-permute-done.16.refs_1_, bf16[14,16,512]{2,1,0:T(8,128)(2,1)S(1)} %collective-permute-done.17.refs_2_, ...), custom_call_target="tpu_custom_call" | custom-call | flops 2097152 | bytes 4194304 | tf_op jit(solution)/shard_map/pallas_call | solution.py:205
  77.0 4.2 %all-to-all-start = ((bf16[32,2,16,512]{3,2,1,0:T(8,128)(2,1)}), bf16[32,2,16,512]{3,2,1,0:T(8,128)(2,1)S(1)}, u32[]{:S(2)}, u32[]{:S(2)}) async-start(bf16[32,2,16,512]{3,2,1,0:T(8,128)(2,1)} %bitcast.8), calls=%async_computation | async-start | bytes 2097152 | tf_op jit(solution)/shard_map/all_to_all | solution.py:465
  81.2 1.3 dynamic_slice.14
  82.5 15.8 %all-to-all-done.block_ref = bf16[32,2,16,512]{3,2,1,0:T(8,128)(2,1)S(1)} async-done(((bf16[32,2,16,512]{3,2,1,0:T(8,128)(2,1)}), bf16[32,2,16,512]{3,2,1,0:T(8,128)(2,1)S(1)}, u32[]{:S(2)}, u32[]{:S(2)}) %all-to-all-start) | async-done | bytes 1048608 | tf_op jit(solution)/shard_map/all_to_all | solution.py:465
  98.4 9.2 %shard_map.98 = (f32[2,512,512]{2,1,0:T(8,128)}, f32[2,512,512]{2,1,0:T(8,128)}, bf16[32,2,16,512]{3,2,1,0:T(8,128)(2,1)}) custom-call(s32[1]{0:T(128)} %bitcast.count_ref, bf16[32,2,16,512]{3,2,1,0:T(8,128)(2,1)S(1)} %all-to-all-done.block_ref, f32[2,512,512]{2,1,0:T(8,128)S(1)} %bitcast.45, f32[2,512,512]{2,1,0:T(8,128)} %bitcast.80), custom_call_target="tpu_custom_call" | custom-call | flops 9663676416 | bytes 10485760 | tf_op jit(solution)/shard_map/pallas_call | solution.py:124
  107.6 6.1 %all-to-all-start.1 = ((bf16[32,2,16,512]{3,2,1,0:T(8,128)(2,1)}), bf16[32,2,16,512]{3,2,1,0:T(8,128)(2,1)S(1)}, u32[]{:S(2)}, u32[]{:S(2)}) async-start(bf16[32,2,16,512]{3,2,1,0:T(8,128)(2,1)} %get-tuple-element.116), calls=%async_computation.1 | async-start | bytes 2097152 | tf_op jit(solution)/shard_map/all_to_all | solution.py:468
  113.8 0.7 gather_fusion
  114.5 0.1 compare_select_fusion
  114.6 16.4 %all-to-all-done.1 = bf16[32,2,16,512]{3,2,1,0:T(8,128)(2,1)S(1)} async-done(((bf16[32,2,16,512]{3,2,1,0:T(8,128)(2,1)}), bf16[32,2,16,512]{3,2,1,0:T(8,128)(2,1)S(1)}, u32[]{:S(2)}, u32[]{:S(2)}) %all-to-all-start.1) | async-done | bytes 1048608 | tf_op jit(solution)/shard_map/all_to_all | solution.py:468
  131.0 0.6 gather_fusion.1
  131.6 1.8 %collective-permute-start.20 = (bf16[14,16,512]{2,1,0:T(8,128)(2,1)S(1)}, bf16[14,16,512]{2,1,0:T(8,128)(2,1)S(1)}, u32[]{:S(2)}, u32[]{:S(2)}) collective-permute-start(bf16[14,16,512]{2,1,0:T(8,128)(2,1)S(1)} %gather_fusion.1), channel_id=1, source_target_pairs={{0,1},{1,2},{2,3},{3,0},{4,7},{5,4},{6,5},{7,6},{8,9},{9,10},{10,1... | collective-permute-start | bytes 688136 | tf_op jit(solution)/shard_map/ppermute | solution.py:431
  133.4 1.7 %collective-permute-start.24 = (bf16[14,16,512]{2,1,0:T(8,128)(2,1)S(1)}, bf16[14,16,512]{2,1,0:T(8,128)(2,1)S(1)}, u32[]{:S(2)}, u32[]{:S(2)}) collective-permute-start(bf16[14,16,512]{2,1,0:T(8,128)(2,1)S(1)} %gather_fusion.1), channel_id=1, source_target_pairs={{0,3},{1,0},{2,1},{3,2},{4,5},{5,6},{6,7},{7,4},{8,11},{9,8},{10,9... | collective-permute-start | bytes 688136 | tf_op jit(solution)/shard_map/ppermute | solution.py:431
  135.1 0.6 gather_fusion.2
  135.7 0.9 collective-permute-start.21
  136.5 2.4 %collective-permute-start.25 = (bf16[14,16,512]{2,1,0:T(8,128)(2,1)S(1)}, bf16[14,16,512]{2,1,0:T(8,128)(2,1)S(1)}, u32[]{:S(2)}, u32[]{:S(2)}) collective-permute-start(bf16[14,16,512]{2,1,0:T(8,128)(2,1)S(1)} %gather_fusion.2), channel_id=1, source_target_pairs={{0,3},{1,0},{2,1},{3,2},{4,5},{5,6},{6,7},{7,4},{8,11},{9,8},{10,9... | collective-permute-start | bytes 688136 | tf_op jit(solution)/shard_map/ppermute | solution.py:431
  139.0 0.2 broadcast_in_dim.44
  139.3 2.5 %collective-permute-start.22 = (bf16[14,16,512]{2,1,0:T(8,128)(2,1)S(1)}, bf16[14,16,512]{2,1,0:T(8,128)(2,1)S(1)}, u32[]{:S(2)}, u32[]{:S(2)}) collective-permute-start(bf16[14,16,512]{2,1,0:T(8,128)(2,1)S(1)} %collective-permute-done.20), channel_id=1, source_target_pairs={{0,1},{1,2},{2,3},{3,0},{4,7},{5,4},{6,5},{7,6},{8,9},{9,10},{10,1... | collective-permute-start | bytes 688136 | tf_op jit(solution)/shard_map/ppermute | solution.py:431
  141.9 3.6 %collective-permute-done.21 = bf16[14,16,512]{2,1,0:T(8,128)(2,1)S(1)} collective-permute-done((bf16[14,16,512]{2,1,0:T(8,128)(2,1)S(1)}, bf16[14,16,512]{2,1,0:T(8,128)(2,1)S(1)}, u32[]{:S(2)}, u32[]{:S(2)}) %collective-permute-start.21) | collective-permute-done | bytes 229408 | tf_op jit(solution)/shard_map/ppermute | solution.py:431
  145.5 0.6 collective-permute-start.23
  146.2 2.7 %collective-permute-done.22 = bf16[14,16,512]{2,1,0:T(8,128)(2,1)S(1)} collective-permute-done((bf16[14,16,512]{2,1,0:T(8,128)(2,1)S(1)}, bf16[14,16,512]{2,1,0:T(8,128)(2,1)S(1)}, u32[]{:S(2)}, u32[]{:S(2)}) %collective-permute-start.22) | collective-permute-done | bytes 229408 | tf_op jit(solution)/shard_map/ppermute | solution.py:431
  148.9 3.9 %collective-permute-done.23 = bf16[14,16,512]{2,1,0:T(8,128)(2,1)S(1)} collective-permute-done((bf16[14,16,512]{2,1,0:T(8,128)(2,1)S(1)}, bf16[14,16,512]{2,1,0:T(8,128)(2,1)S(1)}, u32[]{:S(2)}, u32[]{:S(2)}) %collective-permute-start.23) | collective-permute-done | bytes 229408 | tf_op jit(solution)/shard_map/ppermute | solution.py:431
  152.8 1.2 copy-done.3
  (41 shorter events, 0.5 us)
Async XLA Ops:
  0.6 68.2 %copy-start = (s32[4,32]{1,0:T(4,128)S(1)}, s32[4,32]{1,0:T(4,128)}, u32[]{:S(2)}) copy-start(s32[4,32]{1,0:T(4,128)} %param.11) | copy-start | bytes 1540
  3.2 5.5 %collective-permute-start = (bf16[2,10,4,16,512]{4,3,2,1,0:T(8,128)(2,1)S(1)}, bf16[2,10,4,16,512]{4,3,2,1,0:T(8,128)(2,1)S(1)}, u32[]{:S(2)}, u32[]{:S(2)}) collective-permute-start(bf16[2,10,4,16,512]{4,3,2,1,0:T(8,128)(2,1)S(1)} %get-tuple-element.69), channel_id=1, source_target_pairs={{0,4},{4,0},{8,12},{12,8},{16,20},{20,16},{24,28},{28,24},{32,36},... | collective-permute-start | bytes 3932168 | tf_op jit(solution)/shard_map/ppermute | solution.py:180
  3.3 5.4 %collective-permute-start.1 = (bf16[2,10,4,16,512]{4,3,2,1,0:T(8,128)(2,1)S(1)}, bf16[2,10,4,16,512]{4,3,2,1,0:T(8,128)(2,1)S(1)}, u32[]{:S(2)}, u32[]{:S(2)}) collective-permute-start(bf16[2,10,4,16,512]{4,3,2,1,0:T(8,128)(2,1)S(1)} %get-tuple-element.70), channel_id=1, source_target_pairs={{0,4},{4,0},{8,12},{12,8},{16,20},{20,16},{24,28},{28,24},{32,36},... | collective-permute-start | bytes 3932168 | tf_op jit(solution)/shard_map/ppermute | solution.py:180
  8.0 14.4 %collective-permute-start.6 = (bf16[2,10,4,16,512]{4,3,2,1,0:T(8,128)(2,1)S(1)}, bf16[2,10,4,16,512]{4,3,2,1,0:T(8,128)(2,1)S(1)}, u32[]{:S(2)}, u32[]{:S(2)}) collective-permute-start(bf16[2,10,4,16,512]{4,3,2,1,0:T(8,128)(2,1)S(1)} %get-tuple-element.84), channel_id=1, source_target_pairs={{0,4},{4,0},{8,12},{12,8},{16,20},{20,16},{24,28},{28,24},{32,36},... | collective-permute-start | bytes 3932168 | tf_op jit(solution)/shard_map/ppermute | solution.py:180
  8.2 6.9 %collective-permute-start.2 = (bf16[2,4,4,16,512]{4,3,2,1,0:T(8,128)(2,1)S(1)}, bf16[2,4,4,16,512]{4,3,2,1,0:T(8,128)(2,1)S(1)}, u32[]{:S(2)}, u32[]{:S(2)}) collective-permute-start(bf16[2,4,4,16,512]{4,3,2,1,0:T(8,128)(2,1)S(1)} %get-tuple-element.74), channel_id=1, source_target_pairs={{0,4},{4,0},{8,12},{12,8},{16,20},{20,16},{24,28},{28,24},{32,36},... | collective-permute-start | bytes 1572872 | tf_op jit(solution)/shard_map/ppermute | solution.py:180
  8.6 15.6 %collective-permute-start.7 = (bf16[2,10,4,16,512]{4,3,2,1,0:T(8,128)(2,1)S(1)}, bf16[2,10,4,16,512]{4,3,2,1,0:T(8,128)(2,1)S(1)}, u32[]{:S(2)}, u32[]{:S(2)}) collective-permute-start(bf16[2,10,4,16,512]{4,3,2,1,0:T(8,128)(2,1)S(1)} %get-tuple-element.85), channel_id=1, source_target_pairs={{0,4},{4,0},{8,12},{12,8},{16,20},{20,16},{24,28},{28,24},{32,36},... | collective-permute-start | bytes 3932168 | tf_op jit(solution)/shard_map/ppermute | solution.py:180
  11.5 17.7 %collective-permute-start.8 = (bf16[2,10,4,16,512]{4,3,2,1,0:T(8,128)(2,1)S(1)}, bf16[2,10,4,16,512]{4,3,2,1,0:T(8,128)(2,1)S(1)}, u32[]{:S(2)}, u32[]{:S(2)}) collective-permute-start(bf16[2,10,4,16,512]{4,3,2,1,0:T(8,128)(2,1)S(1)} %get-tuple-element.86), channel_id=1, source_target_pairs={{0,8},{4,28},{8,0},{12,20},{16,24},{20,12},{24,16},{28,4},{32,40},... | collective-permute-start | bytes 3932168 | tf_op jit(solution)/shard_map/ppermute | solution.py:176
  13.2 17.6 %collective-permute-start.9 = (bf16[2,10,4,16,512]{4,3,2,1,0:T(8,128)(2,1)S(1)}, bf16[2,10,4,16,512]{4,3,2,1,0:T(8,128)(2,1)S(1)}, u32[]{:S(2)}, u32[]{:S(2)}) collective-permute-start(bf16[2,10,4,16,512]{4,3,2,1,0:T(8,128)(2,1)S(1)} %get-tuple-element.87), channel_id=1, source_target_pairs={{0,32},{4,100},{8,40},{12,108},{16,48},{20,116},{24,56},{28,124},{... | collective-permute-start | bytes 3932168 | tf_op jit(solution)/shard_map/ppermute | solution.py:176
  15.1 5.0 %collective-permute-start.3 = (bf16[2,4,4,16,512]{4,3,2,1,0:T(8,128)(2,1)S(1)}, bf16[2,4,4,16,512]{4,3,2,1,0:T(8,128)(2,1)S(1)}, u32[]{:S(2)}, u32[]{:S(2)}) collective-permute-start(bf16[2,4,4,16,512]{4,3,2,1,0:T(8,128)(2,1)S(1)} %get-tuple-element.75), channel_id=1, source_target_pairs={{0,4},{4,0},{8,12},{12,8},{16,20},{20,16},{24,28},{28,24},{32,36},... | collective-permute-start | bytes 1572872 | tf_op jit(solution)/shard_map/ppermute | solution.py:180
  22.2 12.6 %collective-permute-start.10 = (bf16[2,4,4,16,512]{4,3,2,1,0:T(8,128)(2,1)S(1)}, bf16[2,4,4,16,512]{4,3,2,1,0:T(8,128)(2,1)S(1)}, u32[]{:S(2)}, u32[]{:S(2)}) collective-permute-start(bf16[2,4,4,16,512]{4,3,2,1,0:T(8,128)(2,1)S(1)} %get-tuple-element.90), channel_id=1, source_target_pairs={{0,8},{4,28},{8,0},{12,20},{16,24},{20,12},{24,16},{28,4},{32,40},... | collective-permute-start | bytes 1572872 | tf_op jit(solution)/shard_map/ppermute | solution.py:176
  22.4 14.0 %collective-permute-start.11 = (bf16[2,4,4,16,512]{4,3,2,1,0:T(8,128)(2,1)S(1)}, bf16[2,4,4,16,512]{4,3,2,1,0:T(8,128)(2,1)S(1)}, u32[]{:S(2)}, u32[]{:S(2)}) collective-permute-start(bf16[2,4,4,16,512]{4,3,2,1,0:T(8,128)(2,1)S(1)} %get-tuple-element.91), channel_id=1, source_target_pairs={{0,32},{4,100},{8,40},{12,108},{16,48},{20,116},{24,56},{28,124},{... | collective-permute-start | bytes 1572872 | tf_op jit(solution)/shard_map/ppermute | solution.py:176
  24.3 18.4 %collective-permute-start.4 = (bf16[2,4,4,16,512]{4,3,2,1,0:T(8,128)(2,1)S(1)}, bf16[2,4,4,16,512]{4,3,2,1,0:T(8,128)(2,1)S(1)}, u32[]{:S(2)}, u32[]{:S(2)}) collective-permute-start(bf16[2,4,4,16,512]{4,3,2,1,0:T(8,128)(2,1)S(1)} %get-tuple-element.82), channel_id=1, source_target_pairs={{0,4},{4,0},{8,12},{12,8},{16,20},{20,16},{24,28},{28,24},{32,36},... | collective-permute-start | bytes 1572872 | tf_op jit(solution)/shard_map/ppermute | solution.py:180
  29.2 13.5 %collective-permute-start.5 = (bf16[2,4,4,16,512]{4,3,2,1,0:T(8,128)(2,1)S(1)}, bf16[2,4,4,16,512]{4,3,2,1,0:T(8,128)(2,1)S(1)}, u32[]{:S(2)}, u32[]{:S(2)}) collective-permute-start(bf16[2,4,4,16,512]{4,3,2,1,0:T(8,128)(2,1)S(1)} %get-tuple-element.83), channel_id=1, source_target_pairs={{0,4},{4,0},{8,12},{12,8},{16,20},{20,16},{24,28},{28,24},{32,36},... | collective-permute-start | bytes 1572872 | tf_op jit(solution)/shard_map/ppermute | solution.py:180
  30.8 2.4 %copy-start.1 = (bf16[2,10,4,16,512]{4,3,2,1,0:T(8,128)(2,1)}, bf16[2,10,4,16,512]{4,3,2,1,0:T(8,128)(2,1)S(1)}, u32[]{:S(2)}) copy-start(bf16[2,10,4,16,512]{4,3,2,1,0:T(8,128)(2,1)S(1)} %collective-permute-done.9.refs_5_) | copy-start | bytes 3932164
  36.4 13.4 %collective-permute-start.14 = (bf16[10,4,16,512]{3,2,1,0:T(8,128)(2,1)S(1)}, bf16[10,4,16,512]{3,2,1,0:T(8,128)(2,1)S(1)}, u32[]{:S(2)}, u32[]{:S(2)}) collective-permute-start(bf16[10,4,16,512]{3,2,1,0:T(8,128)(2,1)S(1)} %get-tuple-element.100), channel_id=1, source_target_pairs={{0,24},{4,12},{8,16},{12,4},{16,8},{20,28},{24,0},{28,20},{32,56},... | collective-permute-start | bytes 1966088 | tf_op jit(solution)/shard_map/ppermute | solution.py:176
  38.6 12.6 %collective-permute-start.15 = (bf16[10,4,16,512]{3,2,1,0:T(8,128)(2,1)S(1)}, bf16[10,4,16,512]{3,2,1,0:T(8,128)(2,1)S(1)}, u32[]{:S(2)}, u32[]{:S(2)}) collective-permute-start(bf16[10,4,16,512]{3,2,1,0:T(8,128)(2,1)S(1)} %get-tuple-element.101), channel_id=1, source_target_pairs={{0,96},{4,36},{8,104},{12,44},{16,112},{20,52},{24,120},{28,60},{3... | collective-permute-start | bytes 1966088 | tf_op jit(solution)/shard_map/ppermute | solution.py:176
  44.5 7.8 %collective-permute-start.12 = (bf16[4,4,16,512]{3,2,1,0:T(8,128)(2,1)S(1)}, bf16[4,4,16,512]{3,2,1,0:T(8,128)(2,1)S(1)}, u32[]{:S(2)}, u32[]{:S(2)}) collective-permute-start(bf16[4,4,16,512]{3,2,1,0:T(8,128)(2,1)S(1)} %get-tuple-element.96), channel_id=1, source_target_pairs={{0,24},{4,12},{8,16},{12,4},{16,8},{20,28},{24,0},{28,20},{32,56},... | collective-permute-start | bytes 786440 | tf_op jit(solution)/shard_map/ppermute | solution.py:176
  45.6 8.4 %collective-permute-start.13 = (bf16[4,4,16,512]{3,2,1,0:T(8,128)(2,1)S(1)}, bf16[4,4,16,512]{3,2,1,0:T(8,128)(2,1)S(1)}, u32[]{:S(2)}, u32[]{:S(2)}) collective-permute-start(bf16[4,4,16,512]{3,2,1,0:T(8,128)(2,1)S(1)} %get-tuple-element.97), channel_id=1, source_target_pairs={{0,96},{4,36},{8,104},{12,44},{16,112},{20,52},{24,120},{28,60},{3... | collective-permute-start | bytes 786440 | tf_op jit(solution)/shard_map/ppermute | solution.py:176
  55.6 8.7 %collective-permute-start.16 = (bf16[2,14,16,512]{3,2,1,0:T(8,128)(2,1)}, bf16[2,14,16,512]{3,2,1,0:T(8,128)(2,1)S(1)}, u32[]{:S(2)}, u32[]{:S(2)}) collective-permute-start(bf16[2,14,16,512]{3,2,1,0:T(8,128)(2,1)} %get-tuple-element.109), channel_id=1, source_target_pairs={{0,32},{4,100},{8,40},{12,108},{16,48},{20,116},{24,56},{28,124},{... | collective-permute-start | bytes 1376264 | tf_op jit(solution)/shard_map/ppermute | solution.py:176
  55.6 12.1 %collective-permute-start.18 = (bf16[2,14,16,512]{3,2,1,0:T(8,128)(2,1)S(1)}, bf16[2,14,16,512]{3,2,1,0:T(8,128)(2,1)S(1)}, u32[]{:S(2)}, u32[]{:S(2)}) collective-permute-start(bf16[2,14,16,512]{3,2,1,0:T(8,128)(2,1)S(1)} %get-tuple-element.112), channel_id=1, source_target_pairs={{0,8},{4,28},{8,0},{12,20},{16,24},{20,12},{24,16},{28,4},{32,40},... | collective-permute-start | bytes 1376264 | tf_op jit(solution)/shard_map/ppermute | solution.py:176
  64.3 7.3 %collective-permute-start.17 = (bf16[14,16,512]{2,1,0:T(8,128)(2,1)S(1)}, bf16[14,16,512]{2,1,0:T(8,128)(2,1)S(1)}, u32[]{:S(2)}, u32[]{:S(2)}) collective-permute-start(bf16[14,16,512]{2,1,0:T(8,128)(2,1)S(1)} %fusion.1), channel_id=1, source_target_pairs={{0,96},{4,36},{8,104},{12,44},{16,112},{20,52},{24,120},{28,60},{3... | collective-permute-start | bytes 688136 | tf_op jit(solution)/shard_map/ppermute | solution.py:176
  67.7 7.3 %collective-permute-start.19 = (bf16[14,16,512]{2,1,0:T(8,128)(2,1)S(1)}, bf16[14,16,512]{2,1,0:T(8,128)(2,1)S(1)}, u32[]{:S(2)}, u32[]{:S(2)}) collective-permute-start(bf16[14,16,512]{2,1,0:T(8,128)(2,1)S(1)} %fusion), channel_id=1, source_target_pairs={{0,24},{4,12},{8,16},{12,4},{16,8},{20,28},{24,0},{28,20},{32,56},... | collective-permute-start | bytes 688136 | tf_op jit(solution)/shard_map/ppermute | solution.py:176
  77.0 21.4 %copy-start.2 = (f32[1,2,512,512]{3,2,1,0:T(8,128)S(1)}, f32[1,2,512,512]{3,2,1,0:T(8,128)}, u32[]{:S(2)}) copy-start(f32[1,2,512,512]{3,2,1,0:T(8,128)} %param.7) | copy-start | bytes 6291460
  77.0 21.4 %all-to-all-start = ((bf16[32,2,16,512]{3,2,1,0:T(8,128)(2,1)}), bf16[32,2,16,512]{3,2,1,0:T(8,128)(2,1)S(1)}, u32[]{:S(2)}, u32[]{:S(2)}) async-start(bf16[32,2,16,512]{3,2,1,0:T(8,128)(2,1)} %bitcast.8), calls=%async_computation | async-start | bytes 2097152 | tf_op jit(solution)/shard_map/all_to_all | solution.py:465
  107.5 6.2 %copy-start.4 = (s32[4,28]{1,0:T(4,128)S(1)}, s32[4,28]{1,0:T(4,128)}, u32[]{:S(2)}) copy-start(s32[4,28]{1,0:T(4,128)} %param.9) | copy-start | bytes 1348
  107.6 23.5 %all-to-all-start.1 = ((bf16[32,2,16,512]{3,2,1,0:T(8,128)(2,1)}), bf16[32,2,16,512]{3,2,1,0:T(8,128)(2,1)S(1)}, u32[]{:S(2)}, u32[]{:S(2)}) async-start(bf16[32,2,16,512]{3,2,1,0:T(8,128)(2,1)} %get-tuple-element.116), calls=%async_computation.1 | async-start | bytes 2097152 | tf_op jit(solution)/shard_map/all_to_all | solution.py:468
  131.6 7.7 %collective-permute-start.20 = (bf16[14,16,512]{2,1,0:T(8,128)(2,1)S(1)}, bf16[14,16,512]{2,1,0:T(8,128)(2,1)S(1)}, u32[]{:S(2)}, u32[]{:S(2)}) collective-permute-start(bf16[14,16,512]{2,1,0:T(8,128)(2,1)S(1)} %gather_fusion.1), channel_id=1, source_target_pairs={{0,1},{1,2},{2,3},{3,0},{4,7},{5,4},{6,5},{7,6},{8,9},{9,10},{10,1... | collective-permute-start | bytes 688136 | tf_op jit(solution)/shard_map/ppermute | solution.py:431
  133.4 19.3 %collective-permute-start.24 = (bf16[14,16,512]{2,1,0:T(8,128)(2,1)S(1)}, bf16[14,16,512]{2,1,0:T(8,128)(2,1)S(1)}, u32[]{:S(2)}, u32[]{:S(2)}) collective-permute-start(bf16[14,16,512]{2,1,0:T(8,128)(2,1)S(1)} %gather_fusion.1), channel_id=1, source_target_pairs={{0,3},{1,0},{2,1},{3,2},{4,5},{5,6},{6,7},{7,4},{8,11},{9,8},{10,9... | collective-permute-start | bytes 688136 | tf_op jit(solution)/shard_map/ppermute | solution.py:431
  135.7 9.8 %collective-permute-start.21 = (bf16[14,16,512]{2,1,0:T(8,128)(2,1)S(1)}, bf16[14,16,512]{2,1,0:T(8,128)(2,1)S(1)}, u32[]{:S(2)}, u32[]{:S(2)}) collective-permute-start(bf16[14,16,512]{2,1,0:T(8,128)(2,1)S(1)} %gather_fusion.2), channel_id=1, source_target_pairs={{0,1},{1,2},{2,3},{3,0},{4,7},{5,4},{6,5},{7,6},{8,9},{9,10},{10,1... | collective-permute-start | bytes 688136 | tf_op jit(solution)/shard_map/ppermute | solution.py:431
  136.5 16.3 %collective-permute-start.25 = (bf16[14,16,512]{2,1,0:T(8,128)(2,1)S(1)}, bf16[14,16,512]{2,1,0:T(8,128)(2,1)S(1)}, u32[]{:S(2)}, u32[]{:S(2)}) collective-permute-start(bf16[14,16,512]{2,1,0:T(8,128)(2,1)S(1)} %gather_fusion.2), channel_id=1, source_target_pairs={{0,3},{1,0},{2,1},{3,2},{4,5},{5,6},{6,7},{7,4},{8,11},{9,8},{10,9... | collective-permute-start | bytes 688136 | tf_op jit(solution)/shard_map/ppermute | solution.py:431
  139.3 9.5 %collective-permute-start.22 = (bf16[14,16,512]{2,1,0:T(8,128)(2,1)S(1)}, bf16[14,16,512]{2,1,0:T(8,128)(2,1)S(1)}, u32[]{:S(2)}, u32[]{:S(2)}) collective-permute-start(bf16[14,16,512]{2,1,0:T(8,128)(2,1)S(1)} %collective-permute-done.20), channel_id=1, source_target_pairs={{0,1},{1,2},{2,3},{3,0},{4,7},{5,4},{6,5},{7,6},{8,9},{9,10},{10,1... | collective-permute-start | bytes 688136 | tf_op jit(solution)/shard_map/ppermute | solution.py:431
  145.5 7.2 %collective-permute-start.23 = (bf16[14,16,512]{2,1,0:T(8,128)(2,1)S(1)}, bf16[14,16,512]{2,1,0:T(8,128)(2,1)S(1)}, u32[]{:S(2)}, u32[]{:S(2)}) collective-permute-start(bf16[14,16,512]{2,1,0:T(8,128)(2,1)S(1)} %collective-permute-done.21), channel_id=1, source_target_pairs={{0,1},{1,2},{2,3},{3,0},{4,7},{5,4},{6,5},{7,6},{8,9},{9,10},{10,1... | collective-permute-start | bytes 688136 | tf_op jit(solution)/shard_map/ppermute | solution.py:431
  152.8 1.2 copy-start.3
